TPU v7x, 32 devices: a whole 2x2x4 slice. The times are simulated.
32 devices in a mesh: dp: 4 (over z), ctx: 4 (over x, core), uly: 2 (over y).
Axes of the slice: x: 2, y: 2, z: 4, core: 2. Of those that a mesh axis runs over, the one named last changes fastest.
Arguments:
- layer_input: bfloat16 [8192, 1536], P(('dp', 'ctx', 'uly')), may hold values from -6 to 6
- span_order: int32 [4, 8], P('dp'), may hold values from 0 to 7, as said below
- doc_lengths: int32 [4, 3], P('dp'), may hold values from 1 to 1536, as said below
- pad_mask: int32 [4, 2048], P('dp'), may hold values 0 or 1
- w_qkv: bfloat16 [1536, 2048], P(('dp', 'ctx', 'uly')), may hold values from -0.15625 to 0.15625
- b_qkv: bfloat16 [2048], P(('dp', 'ctx', 'uly')), may hold values from -3 to 3
- w_out: bfloat16 [1536, 1536], P(None, ('dp', 'ctx', 'uly')), may hold values from -2.5 to 2.5
- norm_gain_attn: bfloat16 [1536], P(('dp', 'ctx', 'uly')), may hold values from 0.5 to 1.5
- norm_gain_mlp: bfloat16 [1536], P(('dp', 'ctx', 'uly')), may hold values from 0.5 to 1.5
- w_mlp: bfloat16 [1536, 26880], P(('dp', 'ctx', 'uly')), may hold values from -0.25 to 0.25
- cotangent: bfloat16 [8192, 1536], P(('dp', 'ctx', 'uly')), may hold values from -6 to 6
Outputs:
- block_output: bfloat16 [8192, 1536], P(('dp', 'ctx', 'uly'))
- input_grad: float32 [8192, 1536], P(('dp', 'ctx', 'uly'))
- grad_qkv: float32 [1536, 2048], P(('dp', 'ctx', 'uly'))
- grad_qkv_bias: float32 [2048], P(('dp', 'ctx', 'uly'))
- grad_out: float32 [1536, 1536], P(None, ('dp', 'ctx', 'uly'))
- grad_gain_attn: float32 [1536], P(('dp', 'ctx', 'uly'))
- grad_gain_mlp: float32 [1536], P(('dp', 'ctx', 'uly'))
- grad_mlp: float32 [1536, 26880], P(('dp', 'ctx', 'uly'))
Inputs may be any that keep to these rules, and one draw needn't show every extreme that they name: `span_order`: in each row, entries 2 c and 2 c + 1 are a span i < 4 and 7 - i; each row is a permutation of 0 to 7. `doc_lengths`: each row sums to 2048; the first document has 1024 tokens or more.
All inputs are finite; a program needn't handle non-finite values. No bound on the sum of `pad_mask` on one device may be relied on, other than what follows from the above.
Results may differ from a plain program's by a relative error of at most 0.025.
Values may be sent and summed in bfloat16 or wider, within the bound.
No kernel may reach another device: no remote copies, remote signals or barrier semaphores. Data moves between devices by JAX's collectives and lax.ppermute only.
A program may use at most 704 MiB of HBM per device.

v0:
```python
import jax
import jax.numpy as jnp
from jax import lax
from jax.sharding import PartitionSpec as P

HEADS = 12
KV_HEADS = 2
HEAD = 128
TOK_DEV = 256


NORM_EPS = 1e-06
ROPE_BASE = 1000000.0
NEG_FILL = -1e30
CONTRACT_ROWS = (((0,), (0,)), ((), ()))
CONTRACT_COLS = (((1,), (1,)), ((), ()))


def seq_places(stored, order_row, length_row):
    blocks = order_row.shape[0]
    picked = (stored // TOK_DEV)[:, None] == jnp.arange(blocks, dtype=jnp.int32)[None, :]
    span_of = jnp.sum(jnp.where(picked, order_row[None, :], 0), axis=1)
    places = span_of * TOK_DEV + stored % TOK_DEV
    doc_ends = jnp.cumsum(length_row)
    passed = places[:, None] >= doc_ends[None, :]
    doc_ids = jnp.sum(passed.astype(jnp.int32), axis=1)
    begins = jnp.max(jnp.where(passed, doc_ends[None, :], 0), axis=1)
    return (places, doc_ids, places - begins)


def rms_norm(values):
    return values * lax.rsqrt(jnp.mean(values * values, axis=-1, keepdims=True) + NORM_EPS)


def rotate_pos(vector, inner_pos, direction):
    half_width = vector.shape[-1] // 2
    frequency = ROPE_BASE ** (-(jnp.arange(half_width, dtype=jnp.float32) * 2.0) / vector.shape[-1])
    angles = direction * inner_pos.astype(jnp.float32)[:, None] * frequency[None, :]
    cosine = jnp.cos(angles)[:, None, :]
    sine_part = jnp.sin(angles)[:, None, :]
    first_half = vector[..., :half_width]
    second_half = vector[..., half_width:]
    return jnp.concatenate(
        [
            first_half * cosine - second_half * sine_part,
            second_half * cosine + first_half * sine_part,
        ],
        axis=-1,
    )


def matmul(left, right):
    return jnp.dot(left, right, preferred_element_type=jnp.float32)


def matmul_nt(left, right):
    return lax.dot_general(left, right, CONTRACT_COLS, preferred_element_type=jnp.float32)


def matmul_tn(left, right):
    return lax.dot_general(left, right, CONTRACT_ROWS, preferred_element_type=jnp.float32)


def swiglu(gate_vals, up_vals):
    return jax.nn.silu(gate_vals) * up_vals


def shards(
    layer_input,
    span_order,
    doc_lengths,
    pad_mask,
    w_qkv,
    b_qkv,
    w_out,
    norm_gain_attn,
    norm_gain_mlp,
    w_mlp,
    cotangent,
):
    tok_rows = layer_input.shape[0]
    ctx_count = lax.axis_size("ctx")
    ctx_index = lax.axis_index("ctx")
    uly_index = lax.axis_index("uly")
    order_row = span_order[0]
    length_row = doc_lengths[0]
    mask_row = pad_mask[0]
    hidden_width = w_mlp.shape[1] // 3
    q_width = HEADS * HEAD
    kv_width = KV_HEADS * HEAD
    score_scale = HEAD ** (-0.5)
    inputs = layer_input.astype(jnp.float32)
    own_stored = (ctx_index * lax.axis_size("uly") + uly_index) * tok_rows + jnp.arange(
        tok_rows, dtype=jnp.int32
    )
    _, _, own_inner = seq_places(own_stored, order_row, length_row)
    w_qkv_all, b_qkv_all, w_out_all, gain_attn_all, gain_mlp_all = (
        lax.all_gather(w_qkv, ("dp", "ctx", "uly"), axis=0, tiled=True),
        lax.all_gather(b_qkv, ("dp", "ctx", "uly"), axis=0, tiled=True),
        lax.all_gather(w_out, ("dp", "ctx", "uly"), axis=1, tiled=True),
        lax.all_gather(norm_gain_attn, ("dp", "ctx", "uly"), axis=0, tiled=True),
        lax.all_gather(norm_gain_mlp, ("dp", "ctx", "uly"), axis=0, tiled=True),
    )
    gain_attn = gain_attn_all.astype(jnp.float32)
    gain_mlp = gain_mlp_all.astype(jnp.float32)
    normed_in = (rms_norm(inputs) * gain_attn).astype(jnp.bfloat16)
    projected = matmul(normed_in, w_qkv_all) + b_qkv_all.astype(jnp.float32)
    queries = rotate_pos(
        projected[:, :q_width].reshape(tok_rows, HEADS, HEAD), own_inner, 1.0
    ).astype(jnp.bfloat16)
    keys_rot = rotate_pos(
        projected[:, q_width : q_width + kv_width].reshape(tok_rows, KV_HEADS, HEAD), own_inner, 1.0
    ).astype(jnp.bfloat16)
    value_rows = (
        projected[:, q_width + kv_width :].reshape(tok_rows, KV_HEADS, HEAD).astype(jnp.bfloat16)
    )
    head_queries, head_keys, head_values = (
        lax.all_to_all(queries, "uly", split_axis=1, concat_axis=0, tiled=True),
        lax.all_to_all(keys_rot, "uly", split_axis=1, concat_axis=0, tiled=True),
        lax.all_to_all(value_rows, "uly", split_axis=1, concat_axis=0, tiled=True),
    )
    group_rows = head_queries.shape[0]
    group_heads = head_queries.shape[1]
    flat_rows = group_rows * group_heads
    batch_rows = group_rows * ctx_count
    query_flat = head_queries.reshape(flat_rows, HEAD)
    key_local = head_keys[:, 0, :]
    value_local = head_values[:, 0, :]
    query_stored = ctx_index * group_rows + jnp.arange(group_rows, dtype=jnp.int32)
    query_places, query_docs, _ = seq_places(query_stored, order_row, length_row)
    query_weight = lax.dynamic_slice_in_dim(mask_row, ctx_index * group_rows, group_rows).astype(
        jnp.float32
    )
    rep_places = jnp.repeat(query_places, group_heads)
    rep_docs = jnp.repeat(query_docs, group_heads)
    rep_stored = jnp.repeat(query_stored, group_heads)
    rep_weight = jnp.repeat(query_weight, group_heads)

    def visible(begin_at, row_count):
        key_stored = begin_at + jnp.arange(row_count, dtype=jnp.int32)
        key_places, key_docs, _ = seq_places(key_stored, order_row, length_row)
        key_flags = lax.dynamic_slice_in_dim(mask_row, begin_at, row_count)
        allowed = (key_docs[None, :] == rep_docs[:, None]) & (
            key_places[None, :] <= rep_places[:, None]
        )
        return allowed & ((key_flags[None, :] == 1) | (key_stored[None, :] == rep_stored[:, None]))

    fold_start = (
        jnp.full((flat_rows,), NEG_FILL, jnp.float32),
        jnp.zeros((flat_rows,), jnp.float32),
        jnp.zeros((flat_rows, HEAD), jnp.float32),
    )
    key_piece = lax.all_gather(key_local, "ctx", axis=0, tiled=True)
    value_piece = lax.all_gather(value_local, "ctx", axis=0, tiled=True)
    block_count = key_piece.shape[0] // group_rows

    def forward_one_block(block_no, state_now):
        run_max, run_sum, run_acc = state_now
        offset = block_no * group_rows
        key_blk = lax.dynamic_slice_in_dim(key_piece, offset, group_rows, 0)
        value_blk = lax.dynamic_slice_in_dim(value_piece, offset, group_rows, 0)
        scores = matmul_nt(query_flat, key_blk) * score_scale
        allowed = visible(offset, group_rows)
        scores = jnp.where(allowed, scores, NEG_FILL)
        new_max = jnp.maximum(run_max, jnp.max(scores, axis=1))
        weights = jnp.where(allowed, jnp.exp(scores - new_max[:, None]), 0.0)
        factor = jnp.exp(run_max - new_max)
        new_acc = run_acc * factor[:, None] + matmul(weights.astype(jnp.bfloat16), value_blk)
        return (new_max, run_sum * factor + jnp.sum(weights, axis=1), new_acc)

    run_max, run_sum, run_acc = lax.fori_loop(0, block_count, forward_one_block, fold_start)
    attn_f32 = run_acc / run_sum[:, None]
    log_total = run_max + jnp.log(run_sum)
    attn_sent = (
        (attn_f32 * rep_weight[:, None]).astype(jnp.bfloat16).reshape(group_rows, group_heads, HEAD)
    )
    attn_tok = lax.all_to_all(attn_sent, "uly", split_axis=0, concat_axis=1, tiled=True).reshape(
        tok_rows, q_width
    )
    middle = inputs + matmul(attn_tok, w_out_all)
    normed_mid = (rms_norm(middle) * gain_mlp).astype(jnp.bfloat16)
    out_grad = cotangent.astype(jnp.float32)
    gate_up_local = w_mlp[:, : 2 * hidden_width]
    down_local = w_mlp[:, 2 * hidden_width :]
    gate_up = matmul(
        normed_mid, lax.all_gather(gate_up_local, ("dp", "ctx", "uly"), axis=0, tiled=True)
    )
    hidden_act = swiglu(gate_up[:, :hidden_width], gate_up[:, hidden_width:]).astype(jnp.bfloat16)
    mlp_out = matmul_nt(
        hidden_act, lax.all_gather(down_local, ("dp", "ctx", "uly"), axis=0, tiled=True)
    )
    pieces = lax.all_gather(w_mlp, ("dp", "ctx", "uly"), axis=0, tiled=True)
    row_count = pieces.shape[0]
    mid_cols = normed_mid
    grad_cols = cotangent
    again_gate_up = matmul(mid_cols, pieces[:, : 2 * hidden_width])
    hidden_grad = matmul(grad_cols, pieces[:, 2 * hidden_width :])
    gate_again = again_gate_up[:, :hidden_width]
    up_again = again_gate_up[:, hidden_width:]
    hidden_again = swiglu(gate_again, up_again).astype(jnp.bfloat16)
    _, act_pull = jax.vjp(swiglu, gate_again, up_again)
    gate_grad, up_grad = act_pull(hidden_grad)
    gate_up_grad = jnp.concatenate([gate_grad, up_grad], axis=1).astype(jnp.bfloat16)
    mid_grad = matmul_nt(
        gate_up_grad, lax.all_gather(gate_up_local, ("dp", "ctx", "uly"), axis=0, tiled=True)
    )
    mid_cols = normed_mid
    grad_cols = cotangent
    grad_mlp = lax.psum_scatter(
        jnp.concatenate(
            [matmul_tn(mid_cols, gate_up_grad), matmul_tn(grad_cols, hidden_again)], axis=1
        ),
        ("dp", "ctx", "uly"),
        scatter_dimension=0,
        tiled=True,
    )
    block_output = (middle + mlp_out).astype(jnp.bfloat16)
    _, mid_pull = jax.vjp(
        lambda mid_vals, gain_vals: rms_norm(mid_vals) * gain_vals, middle, gain_mlp
    )
    middle_part, gain_mlp_grad = mid_pull(mid_grad)
    middle_grad = out_grad + middle_part
    middle_low = middle_grad.astype(jnp.bfloat16)
    attn_tok_grad = (
        matmul_nt(middle_low, w_out_all).astype(jnp.bfloat16).reshape(tok_rows, HEADS, HEAD)
    )
    out_weight_grad = matmul_tn(attn_tok, middle_low)
    head_grad = lax.all_to_all(attn_tok_grad, "uly", split_axis=1, concat_axis=0, tiled=True)
    out_grad_flat = head_grad.reshape(flat_rows, HEAD).astype(jnp.float32) * rep_weight[:, None]
    out_grad_low = out_grad_flat.astype(jnp.bfloat16)
    row_dots = jnp.sum(out_grad_flat * attn_f32, axis=1)
    back_start = (
        jnp.zeros((flat_rows, HEAD), jnp.float32),
        jnp.zeros((batch_rows, HEAD), jnp.float32),
        jnp.zeros((batch_rows, HEAD), jnp.float32),
    )
    backward_key_piece = lax.all_gather(key_local, "ctx", axis=0, tiled=True)
    backward_value_piece = lax.all_gather(value_local, "ctx", axis=0, tiled=True)
    block_count = backward_key_piece.shape[0] // group_rows

    def backward_one_block(block_no, state_now):
        query_grad, key_grad, value_grad = state_now
        offset = block_no * group_rows
        key_blk = lax.dynamic_slice_in_dim(backward_key_piece, offset, group_rows, 0)
        value_blk = lax.dynamic_slice_in_dim(backward_value_piece, offset, group_rows, 0)
        scores = matmul_nt(query_flat, key_blk) * score_scale
        allowed = visible(offset, group_rows)
        prob_blk = jnp.where(allowed, jnp.exp(scores - log_total[:, None]), 0.0)
        prob_grad = matmul_nt(out_grad_low, value_blk)
        score_grad = (prob_blk * (prob_grad - row_dots[:, None])).astype(jnp.bfloat16)
        query_grad = query_grad + matmul(score_grad, key_blk) * score_scale
        key_blk_grad = matmul_tn(score_grad, query_flat) * score_scale
        value_blk_grad = matmul_tn(prob_blk.astype(jnp.bfloat16), out_grad_low)
        key_grad = lax.dynamic_update_slice_in_dim(
            key_grad,
            lax.dynamic_slice_in_dim(key_grad, offset, group_rows, 0) + key_blk_grad,
            offset,
            0,
        )
        value_grad = lax.dynamic_update_slice_in_dim(
            value_grad,
            lax.dynamic_slice_in_dim(value_grad, offset, group_rows, 0) + value_blk_grad,
            offset,
            0,
        )
        return (query_grad, key_grad, value_grad)

    query_grad, key_all_grad, value_all_grad = lax.fori_loop(
        0, block_count, backward_one_block, back_start
    )
    key_own_grad, value_own_grad = (
        lax.psum_scatter(
            key_all_grad.astype(jnp.bfloat16), "ctx", scatter_dimension=0, tiled=True
        ).astype(jnp.float32),
        lax.psum_scatter(
            value_all_grad.astype(jnp.bfloat16), "ctx", scatter_dimension=0, tiled=True
        ).astype(jnp.float32),
    )
    query_send = query_grad.astype(jnp.bfloat16).reshape(group_rows, group_heads, HEAD)
    key_send = key_own_grad.astype(jnp.bfloat16).reshape(group_rows, 1, HEAD)
    value_send = value_own_grad.astype(jnp.bfloat16).reshape(group_rows, 1, HEAD)
    query_back, key_back, value_back = (
        lax.all_to_all(query_send, "uly", split_axis=0, concat_axis=1, tiled=True),
        lax.all_to_all(key_send, "uly", split_axis=0, concat_axis=1, tiled=True),
        lax.all_to_all(value_send, "uly", split_axis=0, concat_axis=1, tiled=True),
    )
    query_pre = rotate_pos(query_back.astype(jnp.float32), own_inner, -1.0).reshape(
        tok_rows, q_width
    )
    key_pre = rotate_pos(key_back.astype(jnp.float32), own_inner, -1.0).reshape(tok_rows, kv_width)
    value_pre = value_back.astype(jnp.float32).reshape(tok_rows, kv_width)
    projected_grad = jnp.concatenate([query_pre, key_pre, value_pre], axis=1).astype(jnp.bfloat16)
    qkv_weight_grad = matmul_tn(normed_in, projected_grad)
    qkv_bias_grad = jnp.sum(projected_grad.astype(jnp.float32), axis=0)
    normed_in_grad = matmul_nt(projected_grad, w_qkv_all)
    _, first_pull = jax.vjp(
        lambda in_vals, gain_vals: rms_norm(in_vals) * gain_vals, inputs, gain_attn
    )
    input_part, gain_attn_grad = first_pull(normed_in_grad)
    input_grad = middle_grad + input_part
    grad_qkv, grad_qkv_bias, grad_out, grad_gain_attn, grad_gain_mlp = (
        lax.psum_scatter(qkv_weight_grad, ("dp", "ctx", "uly"), scatter_dimension=0, tiled=True),
        lax.psum_scatter(qkv_bias_grad, ("dp", "ctx", "uly"), scatter_dimension=0, tiled=True),
        lax.psum_scatter(out_weight_grad, ("dp", "ctx", "uly"), scatter_dimension=1, tiled=True),
        lax.psum_scatter(gain_attn_grad, ("dp", "ctx", "uly"), scatter_dimension=0, tiled=True),
        lax.psum_scatter(gain_mlp_grad, ("dp", "ctx", "uly"), scatter_dimension=0, tiled=True),
    )
    return (
        block_output,
        input_grad,
        grad_qkv,
        grad_qkv_bias,
        grad_out,
        grad_gain_attn,
        grad_gain_mlp,
        grad_mlp,
    )


def solution(mesh):
    placed = (
        P(("dp", "ctx", "uly"), None),
        P("dp", None),
        P("dp", None),
        P("dp", None),
        P(("dp", "ctx", "uly"), None),
        P(("dp", "ctx", "uly")),
        P(None, ("dp", "ctx", "uly")),
        P(("dp", "ctx", "uly")),
        P(("dp", "ctx", "uly")),
        P(("dp", "ctx", "uly"), None),
        P(("dp", "ctx", "uly"), None),
    )
    return jax.shard_map(
        shards,
        mesh=mesh,
        in_specs=placed,
        out_specs=(
            P(("dp", "ctx", "uly"), None),
            P(("dp", "ctx", "uly"), None),
            P(("dp", "ctx", "uly"), None),
            P(("dp", "ctx", "uly")),
            P(None, ("dp", "ctx", "uly")),
            P(("dp", "ctx", "uly")),
            P(("dp", "ctx", "uly")),
            P(("dp", "ctx", "uly"), None),
        ),
        check_vma=False,
    )
```

profile of v0, /device:TPU:0, one launch (start us, length us, event | category | flops | bytes accessed | tf_op | source)
XLA Modules:
  0.0 2895.6 jit_solution(14591317870900240060)
XLA Ops:
  12.0 42.5 %all-reduce.7 = (bf16[2048]{0:T(1024)(128)(2,1)S(1)}, bf16[1536]{0:T(1024)(128)(2,1)S(1)}, bf16[1536]{0:T(1024)(128)(2,1)S(1)}) all-reduce(bf16[2048]{0:T(1024)(128)(2,1)S(1)} %dynamic-update-slice.1, bf16[1536]{0:T(1024)(128)(2,1)S(1)} %dynamic-update-slice, ...), channel_id=1, replica_groups=mesh['dp'=4,'ctx'=4,'uly'=2] {'dp','ctx','uly'}, use_global_device_ids=true, to_apply=%add.1 | all-reduce | flops 5120 | bytes 20480
  58.3 25.1 all-gather.6.cloned.1.call-done
  83.4 4.6 convolution_add_fusion.1
  90.7 4.0 all-to-all-start.2
  113.2 8.1 all_gather.36
  121.4 8.3 all_gather.37
  132.5 54.9 %while.40 = (s32[]{:T(128)}, f32[3072]{0:T(1024)S(1)}, f32[3072]{0:T(1024)S(1)}, f32[3072,128]{1,0:T(8,128)S(1)}, s32[1,8]{1,0:T(1,128)S(1)}, /*index=5*/s32[1,3...) while((s32[]{:T(128)}, f32[3072]{0:T(1024)S(1)}, ...), condition=%wide.region_12.13_spmd.clone, body=%wide.region_7.12_spmd.clone.sunk | while | flops 855291904 | bytes 23531808 | solution.py:171
  133.7 3.6 fusion.153
  137.4 3.8 fusion.154
  141.2 5.0 convolution_add_fusion.3
  147.4 3.6 fusion.153
  151.1 3.8 fusion.154
  155.0 5.0 convolution_add_fusion.3
  161.2 3.7 fusion.153
  164.9 3.8 fusion.154
  168.7 5.0 convolution_add_fusion.3
  174.9 3.6 fusion.153
  178.6 3.8 fusion.154
  182.4 5.0 convolution_add_fusion.3
  196.9 14.5 all-to-all-done.3
  213.1 4.1 multiply_reduce_fusion.3
  218.5 363.0 %all-gather.14.cloned.1.call-done = bf16[1536,26880]{1,0:T(8,128)(2,1)} async-done(((bf16[48,26880]{1,0:T(8,128)(2,1)}), bf16[1536,26880]{1,0:T(8,128)(2,1)}) %all-gather.14.cloned.1.call-update) | async-done | bytes 82575376 | tf_op jit(solution)/shard_map/all_gather | solution.py:192
  581.6 27.9 fusion.55
  609.5 22.0 fusion.61
  631.5 249.6 %all-gather.10.cloned.1.call-done = bf16[1536,17920]{1,0:T(8,128)(2,1)} async-done(((bf16[48,17920]{1,0:T(8,128)(2,1)}), bf16[1536,17920]{1,0:T(8,128)(2,1)}) %all-gather.10.cloned.1.call-update) | async-done | bytes 55050256 | tf_op jit(solution)/shard_map/all_gather | solution.py:186
  881.1 25.6 multiply_reduce_fusion
  909.6 3.7 convolution_convert_fusion
  914.5 3.7 all-to-all-start.4
  918.3 11.4 all-to-all-done.4
  942.0 54.6 %while.41 = (s32[]{:T(128)}, f32[3072,128]{1,0:T(8,128)S(1)}, f32[2048,128]{1,0:T(8,128)}, f32[2048,128]{1,0:T(8,128)}, s32[1,8]{1,0:T(1,128)S(1)}, /*index=5*/s...) while((s32[]{:T(128)}, f32[3072,128]{1,0:T(8,128)S(1)}, ...), condition=%wide.region_19.20_spmd.clone, body=%wide.region_16.19_spmd.clone.sunk | while | flops 2035121152 | bytes 44637560 | solution.py:268
  943.2 4.1 bitcast_select_fusion.3
  956.9 4.1 bitcast_select_fusion.3
  970.5 4.1 bitcast_select_fusion.3
  984.2 4.1 bitcast_select_fusion.3
  1003.2 6.2 fusion.83
  1012.5 3.8 all-to-all-start.5
  1016.3 26.6 convolution_bitcast_fusion
  1053.7 4.0 all-to-all-start.6
  1065.2 6.5 fusion.86
  1072.8 41.1 %fusion.64 = f32[1536,17920]{1,0:T(8,128)} fusion(bf16[256,1536]{1,0:T(8,128)(2,1)S(1)} %copy-done.17, bf16[256,8960]{1,0:T(8,128)(2,1)} %get-tuple-element.900, bf16[256,8960]{1,0:T(8,128)(2,1)} %get-tuple-element.899), kind=kOutput, calls=%fused_computation.95 | convolution fusion | flops 14111211520 | bytes 120061952 | tf_op jit(solution)/shard_map/dot_general | solution.py:61
  1113.9 107.7 %pad_maximum_fusion = f32[1536,26880]{1,0:T(8,128)} fusion(f32[1536,8960]{1,0:T(8,128)} %convolution_bitcast_fusion, f32[1536,17920]{1,0:T(8,128)} %fusion.64), kind=kLoop, calls=%fused_computation.78 | loop fusion | flops 41287680 | bytes 330301440 | tf_op jit(solution)/shard_map/concatenate | solution.py:210
  1221.6 31.5 %fusion.104 = f32[256,17920]{1,0:T(8,128)} fusion(bf16[256,1536]{1,0:T(8,128)(2,1)S(1)} %copy-done.17, bf16[1536,17920]{1,0:T(8,128)(2,1)} %all-gather.10.cloned.1.call-done), kind=kOutput, calls=%fused_computation.194 | convolution fusion | flops 14092861440 | bytes 74186752 | tf_op jit(solution)/shard_map/dot_general | solution.py:53
  1253.2 18.9 fusion.71
  1272.5 6.0 fusion.77
  1278.6 40.7 %all-reduce.6 = (f32[2048]{0:T(1024)S(1)}, f32[1536]{0:T(1024)S(1)}, f32[1536]{0:T(1024)S(1)}) all-reduce(f32[2048]{0:T(1024)S(1)} %convert_reduce_fusion.2, f32[1536]{0:T(1024)S(1)} %get-tuple-element.823, f32[1536]{0:T(1024)S(1)} %copy-done.36), channel_id=5, replica_groups=mesh['dp'=4,'ctx'=4,'uly'=2] {'dp','ctx','uly'}, use_global_device_ids=true, to_apply=%region_25.26.clone | all-reduce | flops 5120 | bytes 40960
  1324.1 28.6 reduce-scatter.12.cloned.1.call-done
  1352.7 162.0 %reduce-scatter.10.cloned.1.call-done = f32[48,2048]{1,0:T(8,128)} async-done(((f32[1536,2048]{1,0:T(8,128)}), f32[48,2048]{1,0:T(8,128)}) %reduce-scatter.10.cloned.1.call-update) | async-done | bytes 393232 | tf_op jit(solution)/shard_map/reduce_scatter | solution.py:302
  1514.7 1373.7 %reduce-scatter.14.cloned.1.call-done = f32[48,26880]{1,0:T(8,128)} async-done(((f32[1536,26880]{1,0:T(8,128)}), f32[48,26880]{1,0:T(8,128)}) %reduce-scatter.14.cloned.1.call-update) | async-done | bytes 5160976 | tf_op jit(solution)/shard_map/reduce_scatter | solution.py:209
  (337 shorter events, 137.5 us)
Async XLA Ops:
  7.2 76.2 %all-gather.6.cloned.1.call-start = ((), (), s32[]{:S(2)}) async-start(), calls=%async_computation.13 | async-start | bytes 6488064 | tf_op jit(solution)/shard_map/all_gather | solution.py:98
  7.9 205.2 %all-gather.8.cloned.1.call-start = ((), (), s32[]{:S(2)}) async-start(), calls=%async_computation.14 | async-start | bytes 4866048 | tf_op jit(solution)/shard_map/all_gather | solution.py:100
  8.7 572.9 %all-gather.14.cloned.1.call-start = ((), (), s32[]{:S(2)}) async-start(), calls=%async_computation.17 | async-start | bytes 85155840 | tf_op jit(solution)/shard_map/all_gather | solution.py:192
  9.4 45.2 %copy-start.29 = (s32[1,8]{1,0:T(1,128)S(1)}, s32[1,8]{1,0:T(1,128)}, u32[]{:S(2)}) copy-start(s32[1,8]{1,0:T(1,128)} %param.16) | copy-start | bytes 100
  9.4 48.1 %copy-start.30 = (s32[1,2048]{1,0:T(1,128)S(1)}, s32[1,2048]{1,0:T(1,128)}, u32[]{:S(2)}) copy-start(s32[1,2048]{1,0:T(1,128)} %param.18) | copy-start | bytes 24580
  9.5 48.6 %copy-start.6 = (bf16[256,1536]{1,0:T(8,128)(2,1)S(1)}, bf16[256,1536]{1,0:T(8,128)(2,1)}, u32[]{:S(2)}) copy-start(bf16[256,1536]{1,0:T(8,128)(2,1)} %param.15) | copy-start | bytes 2359300
  9.5 871.6 %all-gather.10.cloned.1.call-start = ((), (), s32[]{:S(2)}) async-start(), calls=%async_computation.15 | async-start | bytes 56770560 | tf_op jit(solution)/shard_map/all_gather | solution.py:186
  54.6 33.4 %copy-start.26 = (f32[1536]{0:T(1024)}, f32[1536]{0:T(1024)S(1)}, u32[]{:S(2)}) copy-start(f32[1536]{0:T(1024)S(1)} %convert_element_type.187) | copy-start | bytes 18436
  58.3 29.7 %copy-start.34 = (f32[256]{0:T(256)}, f32[256]{0:T(256)S(1)}, u32[]{:S(2)}) copy-start(f32[256]{0:T(256)S(1)} %fusion.80) | copy-start | bytes 3076
  58.3 29.7 %copy-start.31 = (f32[256]{0:T(256)}, f32[256]{0:T(256)S(1)}, u32[]{:S(2)}) copy-start(f32[256]{0:T(256)S(1)} %fusion.96) | copy-start | bytes 3076
  90.7 11.1 all-to-all-start.2
  101.8 7.9 all-to-all-start
  109.7 20.0 all-to-all-start.1
  191.1 22.1 copy-start.7
  193.3 18.1 all-to-all-start.3
  217.2 689.4 %copy-start.13 = (f32[256,1536]{1,0:T(8,128)}, f32[256,1536]{1,0:T(8,128)S(1)}, u32[]{:S(2)}) copy-start(f32[256,1536]{1,0:T(8,128)S(1)} %get-tuple-element.920) | copy-start | bytes 4718596
  218.5 391.0 %copy-start.15 = (bf16[256,1536]{1,0:T(8,128)(2,1)S(1)}, bf16[256,1536]{1,0:T(8,128)(2,1)}, u32[]{:S(2)}) copy-start(bf16[256,1536]{1,0:T(8,128)(2,1)} %param.25) | copy-start | bytes 2359300
  914.5 15.2 all-to-all-start.4
  918.2 124.8 %reduce-scatter.8.cloned.1.call-start = ((), (), s32[]{:S(2)}) async-start(), calls=%async_computation.19 | async-start | bytes 655360 | tf_op jit(solution)/shard_map/reduce_scatter | solution.py:275
  948.3 7.3 copy-start.4
  962.0 7.3 copy-start.4
  975.6 7.3 copy-start.4
  989.3 7.3 copy-start.4
  996.6 6.6 copy-start.1
  998.8 51.0 %reduce-scatter.6.cloned.1.call-start = ((), (), s32[]{:S(2)}) async-start(), calls=%async_computation.18 | async-start | bytes 655360 | tf_op jit(solution)/shard_map/reduce_scatter | solution.py:272
  1001.0 252.2 %all-gather.12.cloned.1.call-start = ((), (), s32[]{:S(2)}) async-start(), calls=%async_computation.16 | async-start | bytes 28385280 | tf_op jit(solution)/shard_map/all_gather | solution.py:190
  1003.2 349.5 %reduce-scatter.12.cloned.1.call-start = ((), (), s32[]{:S(2)}) async-start(), calls=%async_computation.21 | async-start | bytes 9732096 | tf_op jit(solution)/shard_map/reduce_scatter | solution.py:304
  1012.5 30.4 %all-to-all-start.5 = ((bf16[512,6,128]{2,1,0:T(8,128)(2,1)}), bf16[512,6,128]{2,1,0:T(8,128)(2,1)S(1)}, u32[]{:S(2)}, u32[]{:S(2)}) async-start(bf16[512,6,128]{2,1,0:T(8,128)(2,1)} %reshape.484), calls=%async_computation.5 | async-start | bytes 2097152 | tf_op jit(solution)/shard_map/all_to_all | solution.py:283
  1042.9 6.3 copy-start.22
  1045.8 7.8 all-to-all-start.7
  1053.7 10.0 all-to-all-start.6
  1057.7 457.0 %reduce-scatter.10.cloned.1.call-start = ((), (), s32[]{:S(2)}) async-start(), calls=%async_computation.20 | async-start | bytes 12976128 | tf_op jit(solution)/shard_map/reduce_scatter | solution.py:302
  1059.1 6.1 copy-start.8
  1059.1 6.1 copy-start.27
  1059.1 6.1 copy-start.32
  1060.6 11.1 copy-start.10
  1060.8 10.8 copy-start.18
  1065.1 6.5 copy-start.20
  1071.7 1816.7 %reduce-scatter.14.cloned.1.call-start = ((), (), s32[]{:S(2)}) async-start(), calls=%async_computation.22 | async-start | bytes 170311680 | tf_op jit(solution)/shard_map/reduce_scatter | solution.py:209
  1221.6 31.6 %copy-start.14 = (f32[256,1536]{1,0:T(8,128)S(1)}, f32[256,1536]{1,0:T(8,128)}, u32[]{:S(2)}) copy-start(f32[256,1536]{1,0:T(8,128)} %copy-done.13) | copy-start | bytes 4718596
  1253.1 19.0 copy-start.11
  1253.1 19.0 copy-start.19
  1253.1 19.0 copy-start.21
  1253.1 19.4 copy-start.9
  1253.1 19.4 copy-start.28
  1253.1 19.4 copy-start.33
  1272.5 48.5 %copy-start.35 = (f32[256]{0:T(256)S(1)}, f32[256]{0:T(256)}, u32[]{:S(2)}) copy-start(f32[256]{0:T(256)} %copy-done.34) | copy-start | bytes 3076
  1272.5 48.5 %copy-start.2 = (f32[256,1536]{1,0:T(8,128)S(1)}, f32[256,1536]{1,0:T(8,128)}, u32[]{:S(2)}) copy-start(f32[256,1536]{1,0:T(8,128)} %copy-done) | copy-start | bytes 4718596
  (17 other events, 44.7 us)
Sparse Core Ops, SparseCore 0:
  10.9 72.4 all-gather.5
  86.3 63.0 all-gather.7
  152.3 429.2 all-gather.13
  584.3 296.6 all-gather.9
  999.0 19.7 reduce-scatter.7
  1021.2 21.6 reduce-scatter.5
  1045.8 165.9 all-gather.11
  1218.3 134.3 reduce-scatter.11
  1360.3 154.3 reduce-scatter.9
  1521.5 1366.7 reduce-scatter.13
where the time goes:
time: 2900 us
  waiting for transfers between devices  2240 us (77%)
  matrix products  309 us (11%)
  other arithmetic  157 us (5%)
  blocking collectives  99.7 us (3%)
  local copies, waits for them, and re-layouts  47.2 us (2%)
  starting transfers between devices  30.1 us (1%)
    reduce_scatter x1, waiting for transfers between devices, shards(): lax.psum_scatter(jnp.concatenate([matmul_tn(mid_cols, gate_up_grad), matm...  1370 us
    all_gather x1, waiting for transfers between devices, shards(): pieces = lax.all_gather(w_mlp, ('dp', 'ctx', 'uly'), axis=0, tiled=True)  363 us
    all_gather x1, waiting for transfers between devices, shards(): lax.all_gather(gate_up_local, ('dp', 'ctx', 'uly'), axis=0, tiled=True)  250 us
    reduce_scatter x1, waiting for transfers between devices, shards(): lax.psum_scatter(qkv_weight_grad, ('dp', 'ctx', 'uly'), scatter_dimension...  162 us
    dot_general x13, matrix products, matmul(): return jnp.dot(left, right, preferred_element_type=jnp.float32)  120 us
    concatenate x1, other arithmetic, shards(): jnp.concatenate([matmul_tn(mid_cols, gate_up_grad), matmul_tn(grad_cols,...  108 us
    dot_general x12, matrix products, matmul_tn(): lax.dot_general(left, right, CONTRACT_ROWS, preferred_element_type=jnp.fl...  94.9 us
    dot_general x16, matrix products, matmul_nt(): lax.dot_general(left, right, CONTRACT_COLS, preferred_element_type=jnp.fl...  93.5 us
  transfers between devices with their start and end apart: 18, of which 11 were waited for; matrix products, arithmetic and copies ran while one was open for 14% of the time, Pallas kernels for 0%

commit v1 on v0

v1 whole, which is shorter than its diff:
```python
import functools

import jax
import jax.numpy as jnp
from jax import lax
from jax.experimental import pallas as pl
from jax.experimental.pallas import tpu as pltpu
from jax.sharding import PartitionSpec as P

HEADS = 12
KV_HEADS = 2
HEAD = 128
TOK_DEV = 256
LANES = 128
GROUP = HEADS // KV_HEADS

NORM_EPS = 1e-06
ROPE_BASE = 1000000.0
NEG_FILL = -1e30
LOG2E = 1.4426950408889634
SCALE = HEAD ** (-0.5)
FAR = 1 << 30
PLANE = ("ctx", "uly")
EVERY = ("dp", "ctx", "uly")
VMEM_LIMIT = 56 * 1024 * 1024
F32 = jnp.float32
BF16 = jnp.bfloat16


def dot(left, right, left_dim, right_dim):
    return lax.dot_general(
        left, right, (((left_dim,), (right_dim,)), ((), ())), preferred_element_type=F32
    )


def block_bias(kinfo_ref, qinfo_ref, rows):
    info = kinfo_ref[rows, :]
    usable, place = info[:, 0:1], info[:, 1:2]
    q_place, q_begin = qinfo_ref[0:1, :], qinfo_ref[1:2, :]
    allowed = ((usable <= q_place) & (usable >= q_begin)) | (place == q_place)
    return jnp.where(allowed, 0.0, NEG_FILL)


def attn_fwd_kernel(
    need_ref, kinfo_ref, qinfo_ref, q_ref, kv_ref, o_ref, lse_ref, m_ref, l_ref, acc_ref, bias_ref
):
    blocks = kv_ref.shape[0] // TOK_DEV
    m_ref[...] = jnp.full(m_ref.shape, NEG_FILL, F32)
    l_ref[...] = jnp.zeros(l_ref.shape, F32)
    acc_ref[...] = jnp.zeros(acc_ref.shape, F32)

    def one_block(block, carry):
        @pl.when(need_ref[block] > 0)
        def _():
            rows = pl.ds(pl.multiple_of(block * TOK_DEV, TOK_DEV), TOK_DEV)
            bias_ref[...] = block_bias(kinfo_ref, qinfo_ref, rows)
            for group in range(KV_HEADS):
                key = kv_ref[rows, group * HEAD : (group + 1) * HEAD]
                value = kv_ref[rows, (KV_HEADS + group) * HEAD : (KV_HEADS + group + 1) * HEAD]
                value_t = value.T
                for head in range(group * GROUP, (group + 1) * GROUP):
                    span = slice(head * HEAD, (head + 1) * HEAD)
                    scores = dot(key, q_ref[span, :], 1, 0) * (SCALE * LOG2E) + bias_ref[...]
                    old = m_ref[head : head + 1, :]
                    new = jnp.maximum(old, jnp.max(scores, axis=0, keepdims=True))
                    weights = jnp.exp2(scores - new)
                    factor = jnp.exp2(old - new)
                    m_ref[head : head + 1, :] = new
                    l_ref[head : head + 1, :] = l_ref[head : head + 1, :] * factor + jnp.sum(
                        weights, axis=0, keepdims=True
                    )
                    acc_ref[span, :] = acc_ref[span, :] * factor + dot(
                        value_t, weights.astype(BF16), 1, 0
                    )

        return carry

    lax.fori_loop(0, blocks, one_block, 0)
    real = qinfo_ref[2:3, :].astype(F32)
    lse_ref[...] = jnp.zeros(lse_ref.shape, F32)
    for head in range(HEADS):
        span = slice(head * HEAD, (head + 1) * HEAD)
        total = l_ref[head : head + 1, :]
        o_ref[span, :] = (acc_ref[span, :] * (real / total)).astype(BF16)
        lse_ref[head : head + 1, :] = m_ref[head : head + 1, :] + jnp.log(total) * LOG2E


def attn_bwd_kernel(
    need_ref,
    kinfo_ref,
    qinfo_ref,
    cos_ref,
    sin_ref,
    q_ref,
    kv_ref,
    o_ref,
    do_ref,
    lse_ref,
    dq_ref,
    dkv_ref,
    dots_ref,
    acc_ref,
    bias_ref,
    low_ref,
):
    blocks = kv_ref.shape[0] // TOK_DEV
    real = qinfo_ref[2:3, :].astype(F32)
    for head in range(HEADS):
        span = slice(head * HEAD, (head + 1) * HEAD)
        grad = do_ref[span, :].astype(F32) * real
        low_ref[span, :] = grad.astype(BF16)
        dots_ref[head : head + 1, :] = jnp.sum(
            grad * o_ref[span, :].astype(F32), axis=0, keepdims=True
        )
    acc_ref[...] = jnp.zeros(acc_ref.shape, F32)

    def one_block(block, carry):
        rows = pl.ds(pl.multiple_of(block * TOK_DEV, TOK_DEV), TOK_DEV)

        @pl.when(need_ref[block] == 0)
        def _():
            dkv_ref[rows, :] = jnp.zeros((TOK_DEV, 2 * KV_HEADS * HEAD), BF16)

        @pl.when(need_ref[block] > 0)
        def _():
            bias_ref[...] = block_bias(kinfo_ref, qinfo_ref, rows)
            for group in range(KV_HEADS):
                key_cols = slice(group * HEAD, (group + 1) * HEAD)
                value_cols = slice((KV_HEADS + group) * HEAD, (KV_HEADS + group + 1) * HEAD)
                key = kv_ref[rows, key_cols]
                value = kv_ref[rows, value_cols]
                key_t = key.T
                key_grad = jnp.zeros((TOK_DEV, HEAD), F32)
                value_grad = jnp.zeros((TOK_DEV, HEAD), F32)
                for head in range(group * GROUP, (group + 1) * GROUP):
                    span = slice(head * HEAD, (head + 1) * HEAD)
                    query, grad = q_ref[span, :], low_ref[span, :]
                    scores = dot(key, query, 1, 0) * (SCALE * LOG2E) + bias_ref[...]
                    probs = jnp.exp2(scores - lse_ref[head : head + 1, :])
                    prob_grad = dot(value, grad, 1, 0)
                    score_grad = (probs * (prob_grad - dots_ref[head : head + 1, :])).astype(BF16)
                    acc_ref[span, :] += dot(key_t, score_grad, 1, 0)
                    key_grad += dot(score_grad, query, 1, 1)
                    value_grad += dot(probs.astype(BF16), grad, 1, 1)
                dkv_ref[rows, key_cols] = (key_grad * SCALE).astype(BF16)
                dkv_ref[rows, value_cols] = value_grad.astype(BF16)

        return carry

    lax.fori_loop(0, blocks, one_block, 0)
    cosine, sine = cos_ref[...], sin_ref[...]
    half = HEAD // 2
    for head in range(HEADS):
        start = head * HEAD
        whole = (acc_ref[start : start + HEAD, :] * SCALE).astype(BF16).astype(F32)
        first, second = whole[:half], whole[half:]
        turned = jnp.concatenate(
            [first * cosine + second * sine, second * cosine - first * sine], axis=0
        )
        dq_ref[:, start : start + HEAD] = turned.T.astype(BF16)


def vmem_specs(count):
    return [pl.BlockSpec(memory_space=pltpu.VMEM)] * count


def attention_forward(need, kinfo, qinfo, query_t, kv_all):
    rows = query_t.shape[1]
    return pl.pallas_call(
        attn_fwd_kernel,
        out_shape=(
            jax.ShapeDtypeStruct((HEADS * HEAD, rows), BF16),
            jax.ShapeDtypeStruct((16, rows), F32),
        ),
        in_specs=[pl.BlockSpec(memory_space=pltpu.SMEM)] + vmem_specs(4),
        out_specs=tuple(vmem_specs(2)),
        scratch_shapes=[
            pltpu.VMEM((16, rows), F32),
            pltpu.VMEM((16, rows), F32),
            pltpu.VMEM((HEADS * HEAD, rows), F32),
            pltpu.VMEM((TOK_DEV, rows), F32),
        ],
        compiler_params=pltpu.CompilerParams(vmem_limit_bytes=VMEM_LIMIT),
        cost_estimate=pl.CostEstimate(
            flops=4 * HEADS * rows * kv_all.shape[0] * HEAD,
            bytes_accessed=8 * 1024 * 1024,
            transcendentals=HEADS * rows * kv_all.shape[0],
        ),
    )(need, kinfo, qinfo, query_t, kv_all)


def attention_backward(need, kinfo, qinfo, cos_t, sin_t, query_t, kv_all, out_t, grad_t, lse):
    rows = query_t.shape[1]
    return pl.pallas_call(
        attn_bwd_kernel,
        out_shape=(
            jax.ShapeDtypeStruct((rows, HEADS * HEAD), BF16),
            jax.ShapeDtypeStruct(kv_all.shape, BF16),
        ),
        in_specs=[pl.BlockSpec(memory_space=pltpu.SMEM)] + vmem_specs(9),
        out_specs=tuple(vmem_specs(2)),
        scratch_shapes=[
            pltpu.VMEM((16, rows), F32),
            pltpu.VMEM((HEADS * HEAD, rows), F32),
            pltpu.VMEM((TOK_DEV, rows), F32),
            pltpu.VMEM((HEADS * HEAD, rows), BF16),
        ],
        compiler_params=pltpu.CompilerParams(vmem_limit_bytes=VMEM_LIMIT),
        cost_estimate=pl.CostEstimate(
            flops=10 * HEADS * rows * kv_all.shape[0] * HEAD,
            bytes_accessed=12 * 1024 * 1024,
            transcendentals=HEADS * rows * kv_all.shape[0],
        ),
    )(need, kinfo, qinfo, cos_t, sin_t, query_t, kv_all, out_t, grad_t, lse)


def ffn_kernel(parts, mid_ref, cot_ref, *refs):
    gate_w, up_w, down_w = refs[:parts], refs[parts : 2 * parts], refs[2 * parts : 3 * parts]
    hidden_ref, gate_grad_ref, up_grad_ref, mid_grad_ref, out_ref = refs[3 * parts :]
    depth = gate_w[0].shape[0]

    def through(rows_ref, weights):
        total = None
        for part in range(parts):
            term = dot(rows_ref[:, part * depth : (part + 1) * depth], weights[part][...], 1, 0)
            total = term if total is None else total + term
        return total

    gate = through(mid_ref, gate_w)
    up = through(mid_ref, up_w)
    hidden_grad = through(cot_ref, down_w)
    share = 1.0 / (1.0 + jnp.exp(-gate))
    acted = gate * share
    hidden = (acted * up).astype(BF16)
    up_grad = (hidden_grad * acted).astype(BF16)
    gate_grad = (hidden_grad * up * (share * (1.0 + gate * (1.0 - share)))).astype(BF16)
    hidden_ref[...] = hidden
    gate_grad_ref[...] = gate_grad
    up_grad_ref[...] = up_grad
    for part in range(parts):
        cols = slice(part * depth, (part + 1) * depth)
        mid_grad_ref[:, cols] = (
            dot(gate_grad, gate_w[part][...], 1, 1) + dot(up_grad, up_w[part][...], 1, 1)
        ).astype(BF16)
        out_ref[:, cols] = dot(hidden, down_w[part][...], 1, 1).astype(BF16)


def feed_forward(mid_rows, cot_rows, gate_w, up_w, down_w):
    parts = len(gate_w)
    tokens, width = mid_rows.shape
    depth, cols = gate_w[0].shape
    tile = TOK_DEV
    row_spec = pl.BlockSpec((tile, width), lambda i: (i, 0))
    act_spec = pl.BlockSpec((tile, cols), lambda i: (i, 0))
    w_spec = pl.BlockSpec((depth, cols), lambda i: (0, 0), pipeline_mode=pl.Buffered(1))
    return pl.pallas_call(
        functools.partial(ffn_kernel, parts),
        grid=(tokens // tile,),
        out_shape=(jax.ShapeDtypeStruct((tokens, cols), BF16),) * 3
        + (jax.ShapeDtypeStruct((tokens, width), BF16),) * 2,
        in_specs=[row_spec] * 2 + [w_spec] * (3 * parts),
        out_specs=(act_spec,) * 3 + (row_spec,) * 2,
        compiler_params=pltpu.CompilerParams(vmem_limit_bytes=VMEM_LIMIT),
        cost_estimate=pl.CostEstimate(
            flops=12 * tokens * width * cols,
            bytes_accessed=2 * (3 * width * cols + 3 * tokens * cols + 4 * tokens * width),
            transcendentals=tokens * cols,
        ),
    )(mid_rows, cot_rows, *gate_w, *up_w, *down_w)


def shift(array, axis, step):
    count = lax.axis_size(axis)
    return lax.ppermute(array, axis, [(i, (i + step) % count) for i in range(count)])


def ring_gather(block, axis):
    pieces = [block]
    for _ in range(lax.axis_size(axis) - 1):
        pieces.append(shift(pieces[-1], axis, -1))
    return pieces


def ring_reduce(block_of, axis):
    count = lax.axis_size(axis)
    running = block_of(count - 1)
    for r in range(count - 2, -1, -1):
        moved = shift(running, axis, 1)
        running = (moved.astype(F32) + block_of(r).astype(F32)).astype(BF16)
    return running


def plane_bits():
    ctx, uly = lax.axis_size("ctx"), lax.axis_size("uly")
    count = ctx * uly
    assert count & (count - 1) == 0 and ctx % 2 == 0
    core = uly
    near = [1 << i for i in range(uly.bit_length() - 1)]
    far = [core << i for i in range(1, (ctx // 2).bit_length())]
    return count, core, near, far


def swap(array, bit):
    count = lax.axis_size("ctx") * lax.axis_size("uly")
    return lax.ppermute(array, PLANE, [(i, i ^ bit) for i in range(count)])


def plane_gather(rows):
    count, core, near, far = plane_bits()
    half = rows.shape[0] // 2
    got = []
    for piece, order in ((rows[:half], far + near), (rows[half:], near + far)):
        held = {0: piece}
        for bit in order:
            for i in sorted(held):
                held[i ^ bit] = swap(held[i], bit)
        for i in sorted(held):
            held[i ^ core] = swap(held[i], core)
        got.append(held)
    return [(got[0][i], got[1][i]) for i in range(count)]


def plane_reduce(block_of):
    count, core, near, far = plane_bits()
    halves = []
    for which, order in ((0, near + far), (1, far + near)):
        held = {i: block_of(i)[which] for i in range(count)}
        for bit in [core] + order:
            kept = {}
            for i in sorted(held):
                if not i & bit:
                    moved = swap(held[i | bit], bit)
                    kept[i] = (held[i].astype(F32) + moved.astype(F32)).astype(BF16)
            held = kept
        halves.append(held[0])
    return jnp.concatenate(halves, axis=0)


def place_info(spans, row_in_span, length_row):
    places = spans * TOK_DEV + row_in_span
    begins = jnp.zeros_like(places)
    end = jnp.int32(0)
    for doc in range(length_row.shape[0]):
        end = end + length_row[doc]
        begins = jnp.where(places >= end, jnp.maximum(begins, end), begins)
    return places, begins


def inverse_rms(values):
    return lax.rsqrt(jnp.mean(values * values, axis=-1, keepdims=True) + NORM_EPS)


def norm_backward(values, inverse, scaled):
    return inverse * scaled - values * (
        inverse**3 * jnp.mean(scaled * values, axis=-1, keepdims=True)
    )


def turn(heads, cosine, sine):
    half = HEAD // 2
    first, second = heads[..., :half], heads[..., half:]
    return jnp.concatenate(
        [first * cosine - second * sine, second * cosine + first * sine], axis=-1
    )


def shards(
    layer_input,
    span_order,
    doc_lengths,
    pad_mask,
    w_qkv,
    b_qkv,
    w_out,
    norm_gain_attn,
    norm_gain_mlp,
    w_mlp,
    cotangent,
):
    tok_rows, width = layer_input.shape
    n_dp = lax.axis_size("dp")
    n_plane = lax.axis_size("ctx") * lax.axis_size("uly")
    n_all = n_dp * n_plane
    me = lax.axis_index("ctx") * lax.axis_size("uly") + lax.axis_index("uly")
    my_dp = lax.axis_index("dp")
    order_row, length_row, mask_row = span_order[0], doc_lengths[0], pad_mask[0]
    ffn_width = w_mlp.shape[1] // 3
    local_rows = w_mlp.shape[0]
    zone = local_rows * n_plane
    q_width, kv_width = HEADS * HEAD, KV_HEADS * HEAD
    qkv_width = q_width + 2 * kv_width
    bias_rows = b_qkv.shape[0]
    slice_cols = -(-(ffn_width // LANES) // n_plane) * LANES
    pad_cols = slice_cols * n_plane - ffn_width

    def to_slice(which):
        mine = w_mlp[:, which * ffn_width : (which + 1) * ffn_width]
        mine = jnp.pad(mine, ((0, 0), (0, pad_cols))).reshape(local_rows, n_plane, slice_cols)
        mine = mine.transpose(1, 0, 2).reshape(zone, slice_cols)
        mine = lax.all_to_all(mine, PLANE, split_axis=0, concat_axis=0, tiled=True)
        return ring_gather(mine, "dp")

    side = jnp.concatenate(
        [
            norm_gain_attn[:, None],
            norm_gain_mlp[:, None],
            jnp.zeros((local_rows, 62), BF16),
            jnp.pad(b_qkv[None, :], ((0, local_rows - 1), (0, 64 - bias_rows))),
        ],
        axis=1,
    )
    w_qkv_all = lax.all_gather(
        jnp.concatenate([w_qkv, side], axis=1), EVERY, axis=0, tiled=True
    )
    w_out_all = lax.all_gather(w_out.T, EVERY, axis=0, tiled=True)
    side_all = w_qkv_all[:, qkv_width:].astype(F32)
    gain_attn = side_all[:, 0]
    gain_mlp = side_all[:, 1]
    bias_all = side_all.reshape(n_all, local_rows, LANES)[:, 0, 64 : 64 + bias_rows].reshape(-1)

    gate_w, up_w, down_w = to_slice(0), to_slice(1), to_slice(2)

    row_in_span = jnp.arange(tok_rows, dtype=jnp.int32)
    stored_block = me ^ jnp.arange(n_plane, dtype=jnp.int32)
    spans = order_row[stored_block]
    own_place, own_begin = place_info(spans[0], row_in_span, length_row)
    flags = mask_row.reshape(n_plane, tok_rows)[stored_block]
    key_place = spans[:, None] * TOK_DEV + row_in_span[None, :]
    kinfo = jnp.stack(
        [jnp.where(flags == 1, key_place, FAR).reshape(-1), key_place.reshape(-1)], axis=1
    )
    qinfo = jnp.concatenate(
        [
            own_place[None],
            own_begin[None],
            flags[0][None],
            jnp.zeros((5, tok_rows), jnp.int32),
        ],
        axis=0,
    )
    need = ((spans <= spans[0]) & ((spans + 1) * TOK_DEV > own_begin[0])).astype(jnp.int32)

    inner = (own_place - own_begin).astype(F32)
    half = HEAD // 2
    frequency = ROPE_BASE ** (-(jnp.arange(half, dtype=F32) * 2.0) / HEAD)
    angles_t = frequency[:, None] * inner[None, :]
    cos_t, sin_t = jnp.cos(angles_t), jnp.sin(angles_t)
    cos_r, sin_r = cos_t.T[:, None, :], sin_t.T[:, None, :]

    inputs = layer_input.astype(F32)
    in_inverse = inverse_rms(inputs)
    normed_in = (inputs * in_inverse * gain_attn).astype(BF16)

    kv_proj = dot(normed_in, w_qkv_all[:, q_width:qkv_width], 1, 0) + bias_all[q_width:]
    key_own = turn(kv_proj[:, :kv_width].reshape(tok_rows, KV_HEADS, HEAD), cos_r, sin_r)
    kv_own = jnp.concatenate([key_own.reshape(tok_rows, kv_width), kv_proj[:, kv_width:]], axis=1)
    kv_pieces = plane_gather(kv_own.astype(BF16))
    kv_all = jnp.concatenate([half_rows for pair in kv_pieces for half_rows in pair], axis=0)

    q_proj = dot(w_qkv_all[:, :q_width], normed_in, 0, 1) + bias_all[:q_width, None]
    q_heads = q_proj.reshape(HEADS, 2, half, tok_rows)
    q_first, q_second = q_heads[:, 0], q_heads[:, 1]
    query_t = (
        jnp.stack(
            [q_first * cos_t - q_second * sin_t, q_second * cos_t + q_first * sin_t], axis=1
        )
        .reshape(q_width, tok_rows)
        .astype(BF16)
    )
    attended_t, lse = attention_forward(need, kinfo, qinfo, query_t, kv_all)

    middle = inputs + dot(attended_t, w_out_all, 0, 1)
    mid_inverse = inverse_rms(middle)
    normed_mid = (middle * mid_inverse * gain_mlp).astype(BF16)

    def turn_zone(array, zones):
        return lax.dynamic_slice_in_dim(
            jnp.concatenate([array, array], axis=1), zones * zone, width, 1
        )

    def gather_tokens(array):
        pieces = plane_gather(turn_zone(array, my_dp))
        return jnp.concatenate([rows for pair in pieces for rows in pair], axis=0)

    cot_rows = gather_tokens(cotangent)
    mid_rows = gather_tokens(normed_mid)
    hidden, gate_grad, up_grad, mid_grad_part, out_part = feed_forward(
        mid_rows, cot_rows, gate_w, up_w, down_w
    )

    def token_blocks(array):
        cut = tok_rows // 2
        return lambda i: (
            array[i * tok_rows : i * tok_rows + cut],
            array[i * tok_rows + cut : (i + 1) * tok_rows],
        )

    mid_grad = turn_zone(plane_reduce(token_blocks(mid_grad_part)), n_dp - my_dp).astype(F32)

    def slice_gradient(rows, columns):
        mine = ring_reduce(
            lambda r: dot(rows[:, r * zone : (r + 1) * zone], columns, 0, 0).astype(BF16), "dp"
        )
        mine = lax.all_to_all(mine, PLANE, split_axis=0, concat_axis=0, tiled=True)
        mine = mine.reshape(n_plane, local_rows, slice_cols).transpose(1, 0, 2)
        return mine.reshape(local_rows, n_plane * slice_cols)[:, :ffn_width].astype(F32)

    grad_down = slice_gradient(cot_rows, hidden)
    grad_gate = slice_gradient(mid_rows, gate_grad)
    grad_up = slice_gradient(mid_rows, up_grad)
    grad_mlp = jnp.concatenate([grad_gate, grad_up, grad_down], axis=1)

    out_grad = cotangent.astype(F32)
    gain_mlp_grad = jnp.sum(mid_grad * (middle * mid_inverse), axis=0)
    middle_grad = out_grad + norm_backward(middle, mid_inverse, mid_grad * gain_mlp)
    middle_low = middle_grad.astype(BF16)
    attended_grad_t = dot(w_out_all, middle_low, 0, 1).astype(BF16)
    out_weight_grad = dot(middle_low, attended_t, 0, 1).astype(BF16)
    grad_out = lax.psum_scatter(out_weight_grad, EVERY, scatter_dimension=0, tiled=True)
    query_grad, kv_grad = attention_backward(
        need, kinfo, qinfo, cos_t, sin_t, query_t, kv_all, attended_t, attended_grad_t, lse
    )
    kv_back = plane_reduce(token_blocks(kv_grad)).astype(F32)
    key_back = turn(kv_back[:, :kv_width].reshape(tok_rows, KV_HEADS, HEAD), cos_r, -sin_r)
    projected_grad = jnp.concatenate(
        [query_grad, key_back.reshape(tok_rows, kv_width).astype(BF16), kv_back[:, kv_width:].astype(BF16)],
        axis=1,
    )
    in_grad = dot(projected_grad, w_qkv_all[:, :qkv_width], 1, 1)
    gain_attn_grad = jnp.sum(in_grad * (inputs * in_inverse), axis=0)
    input_grad = middle_grad + norm_backward(inputs, in_inverse, in_grad * gain_attn)
    qkv_bias_grad = jnp.sum(projected_grad.astype(F32), axis=0)
    side_grad = jnp.zeros((n_all, local_rows, LANES), F32)
    side_grad = side_grad.at[:, :, 0].set(gain_attn_grad.reshape(n_all, local_rows))
    side_grad = side_grad.at[:, :, 1].set(gain_mlp_grad.reshape(n_all, local_rows))
    side_grad = side_grad.at[:, 0, 64 : 64 + bias_rows].set(qkv_bias_grad.reshape(n_all, bias_rows))
    side_grad = side_grad.reshape(n_all * local_rows, LANES).astype(BF16)
    qkv_weight_grad = dot(normed_in, projected_grad, 0, 0).astype(BF16)
    qkv_sum = lax.psum_scatter(
        jnp.concatenate([qkv_weight_grad, side_grad], axis=1),
        EVERY,
        scatter_dimension=0,
        tiled=True,
    ).astype(F32)

    mlp_out = turn_zone(plane_reduce(token_blocks(out_part)), n_dp - my_dp)
    block_output = (middle + mlp_out.astype(F32)).astype(BF16)
    return (
        block_output,
        input_grad,
        qkv_sum[:, :qkv_width],
        qkv_sum[0, qkv_width + 64 : qkv_width + 64 + bias_rows],
        grad_out.astype(F32).T,
        qkv_sum[:, qkv_width],
        qkv_sum[:, qkv_width + 1],
        grad_mlp,
    )


def solution(mesh):
    rows = P(EVERY, None)
    flat = P(EVERY)
    columns = P(None, EVERY)
    batch = P("dp", None)
    return jax.shard_map(
        shards,
        mesh=mesh,
        in_specs=(rows, batch, batch, batch, rows, flat, columns, flat, flat, rows, rows),
        out_specs=(rows, rows, rows, flat, columns, flat, flat, rows),
        check_vma=False,
    )
```

time: 2900 us -> 858 us (0.30)
  waiting for transfers between devices: 2240 us -> 393 us
  matrix products: 309 us -> 88.2 us
  other arithmetic: 157 us -> 49.1 us
  Pallas kernels: 0 us -> 101 us
  blocking collectives: 99.7 us -> 0 us
  starting transfers between devices: 30.1 us -> 128 us
    reduce_scatter x5 -> x2, waiting for transfers between devices: 1560 us -> 94.5 us  [the longest x1 94.5 us: shards(): lax.psum_scatter(jnp.concatenate([qkv_weight_grad, side_grad], axis=1), E...]
    all_gather x5 -> x2, waiting for transfers between devices: 638 us -> 21.6 us  [the longest x1 19.7 us: shards(): w_out_all = lax.all_gather(w_out.T, EVERY, axis=0, tiled=True)]
    ppermute x0 -> x102, waiting for transfers between devices: none -> 249 us  [the longest x18 153 us: shift(): lax.ppermute(array, axis, [(i, (i + step) % count) for i in range(count)])]
    dot_general x41 -> x19, matrix products: 309 us -> 88.2 us  [dot(): lax.dot_general(left, right, (((left_dim,), (right_dim,)), ((), ())), pre...]
    concatenate x5 -> x6, other arithmetic: 112 us -> 8.32 us  [the longest x1 3.55 us: shards(): jnp.concatenate([qkv_weight_grad, side_grad], axis=1)]
    ppermute x0 -> x102, starting transfers between devices: none -> 101 us  [the longest x84 53.8 us: swap(): return lax.ppermute(array, PLANE, [(i, i ^ bit) for i in range(count)])]
    pallas_call x0 -> x3, Pallas kernels: none -> 101 us  [the longest x1 71.3 us: feed_forward(): pl.pallas_call(functools.partial(ffn_kernel, parts), grid=(tokens // tile...]
    unnamed x2 -> x0, blocking collectives: 83.3 us -> none
  transfers between devices with their start and end apart: 18 -> 112, of which waited for: 11 -> 36; matrix products, arithmetic and copies ran while one was open for 14% -> 23% of each run, Pallas kernels for 0% -> 4%
where the time goes in v1:
time: 858 us; the launch traced here: 849 us
  waiting for transfers between devices  393 us (46%)
  starting transfers between devices  128 us (15%)
  Pallas kernels  101 us (12%)
  matrix products  88.2 us (10%)
  local copies, waits for them, and re-layouts  71.7 us (8%)
  other arithmetic  49.1 us (6%)
  between operations  17.9 us (2%)
    ppermute x18, waiting for transfers between devices, shift(): lax.ppermute(array, axis, [(i, (i + step) % count) for i in range(count)])  153 us
    ppermute x84, waiting for transfers between devices, swap(): return lax.ppermute(array, PLANE, [(i, i ^ bit) for i in range(count)])  95.7 us
    reduce_scatter x1, waiting for transfers between devices, shards(): lax.psum_scatter(jnp.concatenate([qkv_weight_grad, side_grad], axis=1), E...  94.5 us
    dot_general x19, matrix products, dot(): lax.dot_general(left, right, (((left_dim,), (right_dim,)), ((), ())), pre...  88.2 us
    pallas_call x1, Pallas kernels, feed_forward(): pl.pallas_call(functools.partial(ffn_kernel, parts), grid=(tokens // tile...  71.3 us
    ppermute x84, starting transfers between devices, swap(): return lax.ppermute(array, PLANE, [(i, i ^ bit) for i in range(count)])  53.8 us
    ppermute x18, starting transfers between devices, shift(): lax.ppermute(array, axis, [(i, (i + step) % count) for i in range(count)])  47.7 us
    unnamed x124, local copies, waits for them, and re-layouts  32.9 us
  transfers between devices with their start and end apart: 112, of which 36 were waited for; matrix products, arithmetic and copies ran while one was open for 23% of the time, Pallas kernels for 4%

profile of v1, /device:TPU:0, one launch (start us, length us, event | category | flops | bytes accessed | tf_op | source)
XLA Modules:
  0.0 849.4 jit_solution(12065159641592525803)
XLA Ops:
  21.0 4.4 all-to-all-start.1
  68.3 18.8 %all-to-all-done.2 = bf16[8,48,1152]{2,1,0:T(8,128)(2,1)} async-done(((bf16[8,48,1152]{2,1,0:T(8,128)(2,1)}), bf16[8,48,1152]{2,1,0:T(8,128)(2,1)}, u32[]{:S(2)}, u32[]{:S(2)}) %all-to-all-start.2) | async-done | bytes 884768 | tf_op jit(solution)/shard_map/all_to_all | solution.py:400
  87.1 4.2 all-to-all-start
  119.8 24.4 %collective-permute-start.42 = (bf16[384,1152]{1,0:T(8,128)(2,1)}, bf16[384,1152]{1,0:T(8,128)(2,1)}, u32[]{:S(2)}, u32[]{:S(2)}) collective-permute-start(bf16[384,1152]{1,0:T(8,128)(2,1)} %bitcast.15.refs_0_), channel_id=1, source_target_pairs={{0,24},{8,0},{16,8},{24,16},{1,25},{9,1},{17,9},{25,17},{2,26},{10... | collective-permute-start | bytes 2654216 | tf_op jit(solution)/shard_map/ppermute | solution.py:274
  152.1 5.6 collective-permute-done.9
  162.1 13.7 %shard_map.170 = (bf16[1536,256]{1,0:T(8,128)(2,1)}, f32[16,256]{1,0:T(8,128)}) custom-call(s32[8]{0:T(128)} %and_convert_fusion.need_ref, s32[2048,2]{1,0:T(8,128)} %copy.70.kinfo_ref, s32[8,256]{1,0:T(8,128)} %add_add_fusion.qinfo_ref, bf16[1536,256]{1,0:T(8,128)(2,1)} %bitcast.115, bf16[2048,512]{1,0:T(8,128)(2,1)} %constant_dynamic-update-slice_fusion.kv_ref), custom_call_target="tpu_custom_call" | custom-call | flops 3221225472 | bytes 8388608 | tf_op jit(solution)/shard_map/pallas_call | solution.py:169
  175.8 19.7 %all-gather.5.cloned.1.call-done = bf16[1536,1536]{1,0:T(8,128)(2,1)} async-done(((bf16[48,1536]{1,0:T(8,128)(2,1)}), bf16[1536,1536]{1,0:T(8,128)(2,1)}) %all-gather.5.cloned.1.call-update) | async-done | bytes 4718608 | tf_op jit(solution)/shard_map/all_gather | solution.py:415
  212.3 7.7 collective-permute-done.15
  220.7 4.6 collective-permute-done.46.refs_6_
  225.9 18.4 %collective-permute-done.49.refs_10_ = bf16[384,1152]{1,0:T(8,128)(2,1)S(1)} collective-permute-done((bf16[384,1152]{1,0:T(8,128)(2,1)}, bf16[384,1152]{1,0:T(8,128)(2,1)S(1)}, u32[]{:S(2)}, u32[]{:S(2)}) %collective-permute-start.49) | collective-permute-done | bytes 884768 | tf_op jit(solution)/shard_map/ppermute | solution.py:274
  248.2 15.0 %collective-permute-done.43.refs_2_ = bf16[384,1152]{1,0:T(8,128)(2,1)S(1)} collective-permute-done((bf16[384,1152]{1,0:T(8,128)(2,1)}, bf16[384,1152]{1,0:T(8,128)(2,1)S(1)}, u32[]{:S(2)}, u32[]{:S(2)}) %collective-permute-start.43) | collective-permute-done | bytes 884768 | tf_op jit(solution)/shard_map/ppermute | solution.py:274
  269.4 7.2 collective-permute-done.21
  277.3 7.3 collective-permute-done.23
  290.8 10.3 %collective-permute-done.50.refs_11_ = bf16[384,1152]{1,0:T(8,128)(2,1)S(1)} collective-permute-done((bf16[384,1152]{1,0:T(8,128)(2,1)S(1)}, bf16[384,1152]{1,0:T(8,128)(2,1)S(1)}, u32[]{:S(2)}, u32[]{:S(2)}) %collective-permute-start.50) | collective-permute-done | bytes 884768 | tf_op jit(solution)/shard_map/ppermute | solution.py:274
  302.0 17.4 %collective-permute-done.44.refs_3_ = bf16[384,1152]{1,0:T(8,128)(2,1)} collective-permute-done((bf16[384,1152]{1,0:T(8,128)(2,1)S(1)}, bf16[384,1152]{1,0:T(8,128)(2,1)}, u32[]{:S(2)}, u32[]{:S(2)}) %collective-permute-start.44) | collective-permute-done | bytes 884768 | tf_op jit(solution)/shard_map/ppermute | solution.py:274
  319.4 71.3 %shard_map.171 = (bf16[2048,1152]{1,0:T(8,128)(2,1)}, bf16[2048,1152]{1,0:T(8,128)(2,1)}, bf16[2048,1152]{1,0:T(8,128)(2,1)}, bf16[2048,1536]{1,0:T(8,128)(2,1)}, bf16[2048,1536]{1,0:T(8,128)(2,1)}) custom-call(bf16[2048,1536]{1,0:T(8,128)(2,1)} %copy-done.11, bf16[2048,1536]{1,0:T(8,128)(2,1)} %constant_dynamic-update-slice_fusion.29.cot_ref, ...), custom_call_target="tpu_custom_call" | custom-call | flops 43486543872 | bytes 49938432 | tf_op jit(solution)/shard_map/pallas_call | solution.py:256
  396.8 4.9 convolution_convert_fusion.13
  403.6 10.5 %collective-permute-done.70 = bf16[128,1536]{1,0:T(8,128)(2,1)S(1)} collective-permute-done((bf16[128,1536]{1,0:T(8,128)(2,1)S(1)}, bf16[128,1536]{1,0:T(8,128)(2,1)S(1)}, u32[]{:S(2)}, u32[]{:S(2)}) %collective-permute-start.70) | collective-permute-done | bytes 393248 | tf_op jit(solution)/shard_map/ppermute | solution.py:305
  416.3 8.4 collective-permute-done.63
  427.6 9.2 %collective-permute-done.71 = bf16[128,1536]{1,0:T(8,128)(2,1)S(1)} collective-permute-done((bf16[128,1536]{1,0:T(8,128)(2,1)S(1)}, bf16[128,1536]{1,0:T(8,128)(2,1)S(1)}, u32[]{:S(2)}, u32[]{:S(2)}) %collective-permute-start.71) | collective-permute-done | bytes 393248 | tf_op jit(solution)/shard_map/ppermute | solution.py:305
  445.6 8.9 %collective-permute-done.77 = bf16[128,1536]{1,0:T(8,128)(2,1)S(1)} collective-permute-done((bf16[128,1536]{1,0:T(8,128)(2,1)S(1)}, bf16[128,1536]{1,0:T(8,128)(2,1)S(1)}, u32[]{:S(2)}, u32[]{:S(2)}) %collective-permute-start.77) | collective-permute-done | bytes 393248 | tf_op jit(solution)/shard_map/ppermute | solution.py:305
  456.6 7.1 collective-permute-done.56
  466.6 9.2 %collective-permute-done.78 = bf16[128,1536]{1,0:T(8,128)(2,1)S(1)} collective-permute-done((bf16[128,1536]{1,0:T(8,128)(2,1)S(1)}, bf16[128,1536]{1,0:T(8,128)(2,1)S(1)}, u32[]{:S(2)}, u32[]{:S(2)}) %collective-permute-start.78) | collective-permute-done | bytes 393248 | tf_op jit(solution)/shard_map/ppermute | solution.py:305
  487.4 16.4 %shard_map.172 = (bf16[256,1536]{1,0:T(8,128)(2,1)}, bf16[2048,512]{1,0:T(8,128)(2,1)}) custom-call(s32[8]{0:T(128)} %and_convert_fusion.need_ref, s32[2048,2]{1,0:T(8,128)} %copy.70.kinfo_ref, s32[8,256]{1,0:T(8,128)} %add_add_fusion.qinfo_ref, f32[64,256]{1,0:T(8,128)} %copy-done.9, f32[64,256]{1,0:T(8,128)} %get-tuple-element.136.sin_ref, ...), custom_call_target="tpu_custom_call" | custom-call | flops 8053063680 | bytes 12582912 | tf_op jit(solution)/shard_map/pallas_call | solution.py:194
  511.3 11.6 %collective-permute-start.84 = (bf16[128,512]{1,0:T(8,128)(2,1)S(1)}, bf16[128,512]{1,0:T(8,128)(2,1)S(1)}, u32[]{:S(2)}, u32[]{:S(2)}) collective-permute-start(bf16[128,512]{1,0:T(8,128)(2,1)S(1)} %get-tuple-element.117), channel_id=1, source_target_pairs={{0,1},{1,0},{2,3},{3,2},{4,5},{5,4},{6,7},{7,6},{8,9},{9,8},{10,11... | collective-permute-start | bytes 393224 | tf_op jit(solution)/shard_map/ppermute | solution.py:305
  523.0 5.4 convolution_convert_fusion.9
  530.5 6.3 convolution_convert_fusion.5
  540.9 4.4 fusion.6
  548.4 12.7 %collective-permute-done.96 = bf16[384,1152]{1,0:T(8,128)(2,1)S(1)} collective-permute-done((bf16[384,1152]{1,0:T(8,128)(2,1)S(1)}, bf16[384,1152]{1,0:T(8,128)(2,1)S(1)}, u32[]{:S(2)}, u32[]{:S(2)}) %collective-permute-start.96) | collective-permute-done | bytes 884768 | tf_op jit(solution)/shard_map/ppermute | solution.py:274
  572.0 6.3 fusion.42
  586.8 6.2 scatter.14
  599.7 18.5 %collective-permute-done.94 = bf16[384,1152]{1,0:T(8,128)(2,1)} collective-permute-done((bf16[384,1152]{1,0:T(8,128)(2,1)}, bf16[384,1152]{1,0:T(8,128)(2,1)}, u32[]{:S(2)}, u32[]{:S(2)}) %collective-permute-start.94) | collective-permute-done | bytes 884768 | tf_op jit(solution)/shard_map/ppermute | solution.py:274
  618.2 5.4 fusion.9
  623.8 6.4 fusion.24
  630.3 10.0 %collective-permute-done.97 = bf16[384,1152]{1,0:T(8,128)(2,1)} collective-permute-done((bf16[384,1152]{1,0:T(8,128)(2,1)}, bf16[384,1152]{1,0:T(8,128)(2,1)}, u32[]{:S(2)}, u32[]{:S(2)}) %collective-permute-start.97) | collective-permute-done | bytes 884768 | tf_op jit(solution)/shard_map/ppermute | solution.py:274
  640.4 4.4 fusion.18
  644.7 14.4 %collective-permute-done.95 = bf16[384,1152]{1,0:T(8,128)(2,1)S(1)} collective-permute-done((bf16[384,1152]{1,0:T(8,128)(2,1)S(1)}, bf16[384,1152]{1,0:T(8,128)(2,1)S(1)}, u32[]{:S(2)}, u32[]{:S(2)}) %collective-permute-start.95) | collective-permute-done | bytes 884768 | tf_op jit(solution)/shard_map/ppermute | solution.py:274
  662.4 4.5 all-to-all-start.3
  666.9 11.4 %collective-permute-done.100 = bf16[384,1152]{1,0:T(8,128)(2,1)} collective-permute-done((bf16[384,1152]{1,0:T(8,128)(2,1)}, bf16[384,1152]{1,0:T(8,128)(2,1)}, u32[]{:S(2)}, u32[]{:S(2)}) %collective-permute-start.100) | collective-permute-done | bytes 884768 | tf_op jit(solution)/shard_map/ppermute | solution.py:274
  678.2 6.2 fusion.27
  684.5 12.6 %collective-permute-done.98 = bf16[384,1152]{1,0:T(8,128)(2,1)S(1)} collective-permute-done((bf16[384,1152]{1,0:T(8,128)(2,1)}, bf16[384,1152]{1,0:T(8,128)(2,1)S(1)}, u32[]{:S(2)}, u32[]{:S(2)}) %collective-permute-start.98) | collective-permute-done | bytes 884768 | tf_op jit(solution)/shard_map/ppermute | solution.py:274
  697.1 6.0 fusion.21
  703.1 4.5 all-to-all-start.4
  707.7 7.6 collective-permute-done.101
  715.2 6.2 fusion.30
  721.5 4.2 all-to-all-start.5
  729.4 9.2 %all-to-all-done.5 = bf16[8,48,1152]{2,1,0:T(8,128)(2,1)} async-done(((bf16[8,48,1152]{2,1,0:T(8,128)(2,1)}), bf16[8,48,1152]{2,1,0:T(8,128)(2,1)}, u32[]{:S(2)}, u32[]{:S(2)}) %all-to-all-start.5) | async-done | bytes 884768 | tf_op jit(solution)/shard_map/all_to_all | solution.py:504
  744.3 94.5 %reduce-scatter.3.cloned.1.call-done = bf16[48,2176]{1,0:T(8,128)(2,1)} async-done(((bf16[1536,2176]{1,0:T(8,128)(2,1)}), bf16[48,2176]{1,0:T(8,128)(2,1)}) %reduce-scatter.3.cloned.1.call-update) | async-done | bytes 208912 | tf_op jit(solution)/shard_map/reduce_scatter | solution.py:539
  (447 shorter events, 228.0 us)
Async XLA Ops:
  7.2 94.7 %all-gather.3.cloned.1.call-start = ((), (), s32[]{:S(2)}) async-start(), calls=%async_computation.8 | async-start | bytes 6893568 | tf_op jit(solution)/shard_map/all_gather | solution.py:412
  14.6 29.6 %collective-permute-start.28 = (bf16[128,1536]{1,0:T(8,128)(2,1)}, bf16[128,1536]{1,0:T(8,128)(2,1)}, u32[]{:S(2)}, u32[]{:S(2)}) collective-permute-start(bf16[128,1536]{1,0:T(8,128)(2,1)} %get-tuple-element.123), channel_id=1, source_target_pairs={{0,1},{1,0},{2,3},{3,2},{4,5},{5,4},{6,7},{7,6},{8,9},{9,8},{10,11... | collective-permute-start | bytes 1179656 | tf_op jit(solution)/shard_map/ppermute | solution.py:305
  17.5 32.1 %collective-permute-start.30 = (bf16[128,1536]{1,0:T(8,128)(2,1)}, bf16[128,1536]{1,0:T(8,128)(2,1)}, u32[]{:S(2)}, u32[]{:S(2)}) collective-permute-start(bf16[128,1536]{1,0:T(8,128)(2,1)} %get-tuple-element.123), channel_id=1, source_target_pairs={{0,2},{1,3},{2,0},{3,1},{4,6},{5,7},{6,4},{7,5},{8,10},{9,11},{10,... | collective-permute-start | bytes 1179656 | tf_op jit(solution)/shard_map/ppermute | solution.py:305
  17.5 30.3 %collective-permute-start.29 = (bf16[128,1536]{1,0:T(8,128)(2,1)}, bf16[128,1536]{1,0:T(8,128)(2,1)}, u32[]{:S(2)}, u32[]{:S(2)}) collective-permute-start(bf16[128,1536]{1,0:T(8,128)(2,1)} %get-tuple-element.122), channel_id=1, source_target_pairs={{0,1},{1,0},{2,3},{3,2},{4,5},{5,4},{6,7},{7,6},{8,9},{9,8},{10,11... | collective-permute-start | bytes 1179656 | tf_op jit(solution)/shard_map/ppermute | solution.py:305
  17.6 34.3 %collective-permute-start.31 = (bf16[128,1536]{1,0:T(8,128)(2,1)}, bf16[128,1536]{1,0:T(8,128)(2,1)}, u32[]{:S(2)}, u32[]{:S(2)}) collective-permute-start(bf16[128,1536]{1,0:T(8,128)(2,1)} %get-tuple-element.122), channel_id=1, source_target_pairs={{0,2},{1,3},{2,0},{3,1},{4,6},{5,7},{6,4},{7,5},{8,10},{9,11},{10,... | collective-permute-start | bytes 1179656 | tf_op jit(solution)/shard_map/ppermute | solution.py:305
  18.1 34.0 %collective-permute-start.34 = (bf16[128,1536]{1,0:T(8,128)(2,1)}, bf16[128,1536]{1,0:T(8,128)(2,1)}, u32[]{:S(2)}, u32[]{:S(2)}) collective-permute-start(bf16[128,1536]{1,0:T(8,128)(2,1)} %get-tuple-element.123), channel_id=1, source_target_pairs={{0,4},{1,5},{2,6},{3,7},{4,0},{5,1},{6,2},{7,3},{8,12},{9,13},{10,... | collective-permute-start | bytes 1179656 | tf_op jit(solution)/shard_map/ppermute | solution.py:305
  21.0 34.7 %all-to-all-start.1 = ((bf16[8,48,1152]{2,1,0:T(8,128)(2,1)}), bf16[8,48,1152]{2,1,0:T(8,128)(2,1)}, u32[]{:S(2)}, u32[]{:S(2)}) async-start(bf16[8,48,1152]{2,1,0:T(8,128)(2,1)} %bitcast.90), calls=%async_computation.1 | async-start | bytes 1769472 | tf_op jit(solution)/shard_map/all_to_all | solution.py:400
  25.4 170.1 %all-gather.5.cloned.1.call-start = ((), (), s32[]{:S(2)}) async-start(), calls=%async_computation.9 | async-start | bytes 4866048 | tf_op jit(solution)/shard_map/all_gather | solution.py:415
  51.9 43.7 %collective-permute-start.37 = (bf16[128,1536]{1,0:T(8,128)(2,1)}, bf16[128,1536]{1,0:T(8,128)(2,1)S(1)}, u32[]{:S(2)}, u32[]{:S(2)}) collective-permute-start(bf16[128,1536]{1,0:T(8,128)(2,1)} %collective-permute-done.29), channel_id=1, source_target_pairs={{0,4},{1,5},{2,6},{3,7},{4,0},{5,1},{6,2},{7,3},{8,12},{9,13},{10,... | collective-permute-start | bytes 1179656 | tf_op jit(solution)/shard_map/ppermute | solution.py:305
  52.0 39.4 %collective-permute-start.36 = (bf16[128,1536]{1,0:T(8,128)(2,1)}, bf16[128,1536]{1,0:T(8,128)(2,1)S(1)}, u32[]{:S(2)}, u32[]{:S(2)}) collective-permute-start(bf16[128,1536]{1,0:T(8,128)(2,1)} %collective-permute-done.34), channel_id=1, source_target_pairs={{0,1},{1,0},{2,3},{3,2},{4,5},{5,4},{6,7},{7,6},{8,9},{9,8},{10,11... | collective-permute-start | bytes 1179656 | tf_op jit(solution)/shard_map/ppermute | solution.py:305
  55.7 31.4 %all-to-all-start.2 = ((bf16[8,48,1152]{2,1,0:T(8,128)(2,1)}), bf16[8,48,1152]{2,1,0:T(8,128)(2,1)}, u32[]{:S(2)}, u32[]{:S(2)}) async-start(bf16[8,48,1152]{2,1,0:T(8,128)(2,1)} %bitcast.88), calls=%async_computation.2 | async-start | bytes 1769472 | tf_op jit(solution)/shard_map/all_to_all | solution.py:400
  59.9 36.5 %collective-permute-start.38 = (bf16[128,1536]{1,0:T(8,128)(2,1)}, bf16[128,1536]{1,0:T(8,128)(2,1)}, u32[]{:S(2)}, u32[]{:S(2)}) collective-permute-start(bf16[128,1536]{1,0:T(8,128)(2,1)} %collective-permute-done.34), channel_id=1, source_target_pairs={{0,2},{1,3},{2,0},{3,1},{4,6},{5,7},{6,4},{7,5},{8,10},{9,11},{10,... | collective-permute-start | bytes 1179656 | tf_op jit(solution)/shard_map/ppermute | solution.py:305
  60.3 37.8 %collective-permute-start.39 = (bf16[128,1536]{1,0:T(8,128)(2,1)S(1)}, bf16[128,1536]{1,0:T(8,128)(2,1)}, u32[]{:S(2)}, u32[]{:S(2)}) collective-permute-start(bf16[128,1536]{1,0:T(8,128)(2,1)S(1)} %collective-permute-done.35), channel_id=1, source_target_pairs={{0,2},{1,3},{2,0},{3,1},{4,6},{5,7},{6,4},{7,5},{8,10},{9,11},{10,... | collective-permute-start | bytes 1179656 | tf_op jit(solution)/shard_map/ppermute | solution.py:305
  61.3 141.3 %collective-permute-start.45 = (bf16[384,1152]{1,0:T(8,128)(2,1)}, bf16[384,1152]{1,0:T(8,128)(2,1)}, u32[]{:S(2)}, u32[]{:S(2)}) collective-permute-start(bf16[384,1152]{1,0:T(8,128)(2,1)} %bitcast.17.refs_4_), channel_id=1, source_target_pairs={{0,24},{8,0},{16,8},{24,16},{1,25},{9,1},{17,9},{25,17},{2,26},{10... | collective-permute-start | bytes 2654216 | tf_op jit(solution)/shard_map/ppermute | solution.py:274
  87.1 32.7 %all-to-all-start = ((bf16[8,48,1152]{2,1,0:T(8,128)(2,1)}), bf16[8,48,1152]{2,1,0:T(8,128)(2,1)}, u32[]{:S(2)}, u32[]{:S(2)}) async-start(bf16[8,48,1152]{2,1,0:T(8,128)(2,1)} %bitcast.92), calls=%async_computation | async-start | bytes 1769472 | tf_op jit(solution)/shard_map/all_to_all | solution.py:400
  91.4 651.2 %reduce-scatter.5.cloned.1.call-start = ((), (), s32[]{:S(2)}) async-start(), calls=%async_computation.11 | async-start | bytes 4866048 | tf_op jit(solution)/shard_map/reduce_scatter | solution.py:519
  91.4 114.6 %collective-permute-start.48 = (bf16[384,1152]{1,0:T(8,128)(2,1)}, bf16[384,1152]{1,0:T(8,128)(2,1)}, u32[]{:S(2)}, u32[]{:S(2)}) collective-permute-start(bf16[384,1152]{1,0:T(8,128)(2,1)} %bitcast.19.refs_8_), channel_id=1, source_target_pairs={{0,24},{8,0},{16,8},{24,16},{1,25},{9,1},{17,9},{25,17},{2,26},{10... | collective-permute-start | bytes 2654216 | tf_op jit(solution)/shard_map/ppermute | solution.py:274
  116.7 28.2 %collective-permute-start.6 = (bf16[128,512]{1,0:T(8,128)(2,1)}, bf16[128,512]{1,0:T(8,128)(2,1)S(1)}, u32[]{:S(2)}, u32[]{:S(2)}) collective-permute-start(bf16[128,512]{1,0:T(8,128)(2,1)} %get-tuple-element.131), channel_id=1, source_target_pairs={{0,4},{1,5},{2,6},{3,7},{4,0},{5,1},{6,2},{7,3},{8,12},{9,13},{10,... | collective-permute-start | bytes 393224 | tf_op jit(solution)/shard_map/ppermute | solution.py:305
  118.6 26.9 %collective-permute-start.5 = (bf16[128,512]{1,0:T(8,128)(2,1)S(1)}, bf16[128,512]{1,0:T(8,128)(2,1)S(1)}, u32[]{:S(2)}, u32[]{:S(2)}) collective-permute-start(bf16[128,512]{1,0:T(8,128)(2,1)S(1)} %collective-permute-done.1), channel_id=1, source_target_pairs={{0,2},{1,3},{2,0},{3,1},{4,6},{5,7},{6,4},{7,5},{8,10},{9,11},{10,... | collective-permute-start | bytes 393224 | tf_op jit(solution)/shard_map/ppermute | solution.py:305
  119.8 87.7 %collective-permute-start.42 = (bf16[384,1152]{1,0:T(8,128)(2,1)}, bf16[384,1152]{1,0:T(8,128)(2,1)}, u32[]{:S(2)}, u32[]{:S(2)}) collective-permute-start(bf16[384,1152]{1,0:T(8,128)(2,1)} %bitcast.15.refs_0_), channel_id=1, source_target_pairs={{0,24},{8,0},{16,8},{24,16},{1,25},{9,1},{17,9},{25,17},{2,26},{10... | collective-permute-start | bytes 2654216 | tf_op jit(solution)/shard_map/ppermute | solution.py:274
  160.2 40.0 %collective-permute-start.40 = (bf16[128,1536]{1,0:T(8,128)(2,1)S(1)}, bf16[128,1536]{1,0:T(8,128)(2,1)S(1)}, u32[]{:S(2)}, u32[]{:S(2)}) collective-permute-start(bf16[128,1536]{1,0:T(8,128)(2,1)S(1)} %collective-permute-done.36), channel_id=1, source_target_pairs={{0,2},{1,3},{2,0},{3,1},{4,6},{5,7},{6,4},{7,5},{8,10},{9,11},{10,... | collective-permute-start | bytes 1179656 | tf_op jit(solution)/shard_map/ppermute | solution.py:305
  161.4 43.3 %collective-permute-start.41 = (bf16[128,1536]{1,0:T(8,128)(2,1)S(1)}, bf16[128,1536]{1,0:T(8,128)(2,1)S(1)}, u32[]{:S(2)}, u32[]{:S(2)}) collective-permute-start(bf16[128,1536]{1,0:T(8,128)(2,1)S(1)} %collective-permute-done.37), channel_id=1, source_target_pairs={{0,2},{1,3},{2,0},{3,1},{4,6},{5,7},{6,4},{7,5},{8,10},{9,11},{10,... | collective-permute-start | bytes 1179656 | tf_op jit(solution)/shard_map/ppermute | solution.py:305
  202.6 22.7 %collective-permute-start.46 = (bf16[384,1152]{1,0:T(8,128)(2,1)}, bf16[384,1152]{1,0:T(8,128)(2,1)S(1)}, u32[]{:S(2)}, u32[]{:S(2)}) collective-permute-start(bf16[384,1152]{1,0:T(8,128)(2,1)} %collective-permute-done.45.refs_5_), channel_id=1, source_target_pairs={{0,24},{8,0},{16,8},{24,16},{1,25},{9,1},{17,9},{25,17},{2,26},{10... | collective-permute-start | bytes 2654216 | tf_op jit(solution)/shard_map/ppermute | solution.py:274
  206.1 38.2 %collective-permute-start.49 = (bf16[384,1152]{1,0:T(8,128)(2,1)}, bf16[384,1152]{1,0:T(8,128)(2,1)S(1)}, u32[]{:S(2)}, u32[]{:S(2)}) collective-permute-start(bf16[384,1152]{1,0:T(8,128)(2,1)} %collective-permute-done.48.refs_9_), channel_id=1, source_target_pairs={{0,24},{8,0},{16,8},{24,16},{1,25},{9,1},{17,9},{25,17},{2,26},{10... | collective-permute-start | bytes 2654216 | tf_op jit(solution)/shard_map/ppermute | solution.py:274
  207.5 55.6 %collective-permute-start.43 = (bf16[384,1152]{1,0:T(8,128)(2,1)}, bf16[384,1152]{1,0:T(8,128)(2,1)S(1)}, u32[]{:S(2)}, u32[]{:S(2)}) collective-permute-start(bf16[384,1152]{1,0:T(8,128)(2,1)} %collective-permute-done.42.refs_1_), channel_id=1, source_target_pairs={{0,24},{8,0},{16,8},{24,16},{1,25},{9,1},{17,9},{25,17},{2,26},{10... | collective-permute-start | bytes 2654216 | tf_op jit(solution)/shard_map/ppermute | solution.py:274
  220.1 47.1 %collective-permute-start.18 = (bf16[128,1536]{1,0:T(8,128)(2,1)S(1)}, bf16[128,1536]{1,0:T(8,128)(2,1)S(1)}, u32[]{:S(2)}, u32[]{:S(2)}) collective-permute-start(bf16[128,1536]{1,0:T(8,128)(2,1)S(1)} %collective-permute-done.14), channel_id=1, source_target_pairs={{0,2},{1,3},{2,0},{3,1},{4,6},{5,7},{6,4},{7,5},{8,10},{9,11},{10,... | collective-permute-start | bytes 1179656 | tf_op jit(solution)/shard_map/ppermute | solution.py:305
  225.3 42.0 %collective-permute-start.20 = (bf16[128,1536]{1,0:T(8,128)(2,1)S(1)}, bf16[128,1536]{1,0:T(8,128)(2,1)S(1)}, u32[]{:S(2)}, u32[]{:S(2)}) collective-permute-start(bf16[128,1536]{1,0:T(8,128)(2,1)S(1)} %get-tuple-element.125), channel_id=1, source_target_pairs={{0,4},{1,5},{2,6},{3,7},{4,0},{5,1},{6,2},{7,3},{8,12},{9,13},{10,... | collective-permute-start | bytes 1179656 | tf_op jit(solution)/shard_map/ppermute | solution.py:305
  225.8 42.0 %collective-permute-start.19 = (bf16[128,1536]{1,0:T(8,128)(2,1)S(1)}, bf16[128,1536]{1,0:T(8,128)(2,1)S(1)}, u32[]{:S(2)}, u32[]{:S(2)}) collective-permute-start(bf16[128,1536]{1,0:T(8,128)(2,1)S(1)} %collective-permute-done.15), channel_id=1, source_target_pairs={{0,2},{1,3},{2,0},{3,1},{4,6},{5,7},{6,4},{7,5},{8,10},{9,11},{10,... | collective-permute-start | bytes 1179656 | tf_op jit(solution)/shard_map/ppermute | solution.py:305
  244.2 46.6 %collective-permute-start.47 = (bf16[384,1152]{1,0:T(8,128)(2,1)S(1)}, bf16[384,1152]{1,0:T(8,128)(2,1)S(1)}, u32[]{:S(2)}, u32[]{:S(2)}) collective-permute-start(bf16[384,1152]{1,0:T(8,128)(2,1)S(1)} %collective-permute-done.46.refs_6_), channel_id=1, source_target_pairs={{0,24},{8,0},{16,8},{24,16},{1,25},{9,1},{17,9},{25,17},{2,26},{10... | collective-permute-start | bytes 2654216 | tf_op jit(solution)/shard_map/ppermute | solution.py:274
  263.2 37.9 %collective-permute-start.50 = (bf16[384,1152]{1,0:T(8,128)(2,1)S(1)}, bf16[384,1152]{1,0:T(8,128)(2,1)S(1)}, u32[]{:S(2)}, u32[]{:S(2)}) collective-permute-start(bf16[384,1152]{1,0:T(8,128)(2,1)S(1)} %collective-permute-done.49.refs_10_), channel_id=1, source_target_pairs={{0,24},{8,0},{16,8},{24,16},{1,25},{9,1},{17,9},{25,17},{2,26},{10... | collective-permute-start | bytes 2654216 | tf_op jit(solution)/shard_map/ppermute | solution.py:274
  267.1 52.2 %collective-permute-start.44 = (bf16[384,1152]{1,0:T(8,128)(2,1)S(1)}, bf16[384,1152]{1,0:T(8,128)(2,1)}, u32[]{:S(2)}, u32[]{:S(2)}) collective-permute-start(bf16[384,1152]{1,0:T(8,128)(2,1)S(1)} %collective-permute-done.43.refs_2_), channel_id=1, source_target_pairs={{0,24},{8,0},{16,8},{24,16},{1,25},{9,1},{17,9},{25,17},{2,26},{10... | collective-permute-start | bytes 2654216 | tf_op jit(solution)/shard_map/ppermute | solution.py:274
  393.5 21.3 %collective-permute-start.61 = (bf16[128,1536]{1,0:T(8,128)(2,1)S(1)}, bf16[128,1536]{1,0:T(8,128)(2,1)S(1)}, u32[]{:S(2)}, u32[]{:S(2)}) collective-permute-start(bf16[128,1536]{1,0:T(8,128)(2,1)S(1)} %get-tuple-element.95), channel_id=1, source_target_pairs={{0,2},{1,3},{2,0},{3,1},{4,6},{5,7},{6,4},{7,5},{8,10},{9,11},{10,... | collective-permute-start | bytes 1179656 | tf_op jit(solution)/shard_map/ppermute | solution.py:305
  401.7 23.7 %collective-permute-start.65 = (bf16[128,1536]{1,0:T(8,128)(2,1)S(1)}, bf16[128,1536]{1,0:T(8,128)(2,1)S(1)}, u32[]{:S(2)}, u32[]{:S(2)}) collective-permute-start(bf16[128,1536]{1,0:T(8,128)(2,1)S(1)} %get-tuple-element.80), channel_id=1, source_target_pairs={{0,2},{1,3},{2,0},{3,1},{4,6},{5,7},{6,4},{7,5},{8,10},{9,11},{10,... | collective-permute-start | bytes 1179656 | tf_op jit(solution)/shard_map/ppermute | solution.py:305
  402.4 23.1 %collective-permute-start.73 = (bf16[128,1536]{1,0:T(8,128)(2,1)S(1)}, bf16[128,1536]{1,0:T(8,128)(2,1)S(1)}, u32[]{:S(2)}, u32[]{:S(2)}) collective-permute-start(bf16[128,1536]{1,0:T(8,128)(2,1)S(1)} %get-tuple-element.83), channel_id=1, source_target_pairs={{0,2},{1,3},{2,0},{3,1},{4,6},{5,7},{6,4},{7,5},{8,10},{9,11},{10,... | collective-permute-start | bytes 1179656 | tf_op jit(solution)/shard_map/ppermute | solution.py:305
  403.4 22.6 %collective-permute-start.76 = (bf16[128,1536]{1,0:T(8,128)(2,1)S(1)}, bf16[128,1536]{1,0:T(8,128)(2,1)S(1)}, u32[]{:S(2)}, u32[]{:S(2)}) collective-permute-start(bf16[128,1536]{1,0:T(8,128)(2,1)S(1)} %get-tuple-element.81), channel_id=1, source_target_pairs={{0,2},{1,3},{2,0},{3,1},{4,6},{5,7},{6,4},{7,5},{8,10},{9,11},{10,... | collective-permute-start | bytes 1179656 | tf_op jit(solution)/shard_map/ppermute | solution.py:305
  437.7 103.2 %collective-permute-start.93 = (bf16[384,1152]{1,0:T(8,128)(2,1)}, bf16[384,1152]{1,0:T(8,128)(2,1)}, u32[]{:S(2)}, u32[]{:S(2)}) collective-permute-start(bf16[384,1152]{1,0:T(8,128)(2,1)} %convolution_convert_fusion.13), channel_id=1, source_target_pairs={{0,8},{8,16},{16,24},{24,0},{1,9},{9,17},{17,25},{25,1},{2,10},{10... | collective-permute-start | bytes 2654216 | tf_op jit(solution)/shard_map/ppermute | solution.py:274
  439.7 39.8 %collective-permute-start.51 = (bf16[128,1536]{1,0:T(8,128)(2,1)S(1)}, bf16[128,1536]{1,0:T(8,128)(2,1)S(1)}, u32[]{:S(2)}, u32[]{:S(2)}) collective-permute-start(bf16[128,1536]{1,0:T(8,128)(2,1)S(1)} %get-tuple-element.100), channel_id=1, source_target_pairs={{0,2},{1,3},{2,0},{3,1},{4,6},{5,7},{6,4},{7,5},{8,10},{9,11},{10,... | collective-permute-start | bytes 1179656 | tf_op jit(solution)/shard_map/ppermute | solution.py:305
  510.0 328.7 %reduce-scatter.3.cloned.1.call-start = ((), (), s32[]{:S(2)}) async-start(), calls=%async_computation.10 | async-start | bytes 6893568 | tf_op jit(solution)/shard_map/reduce_scatter | solution.py:539
  536.8 24.3 %collective-permute-start.96 = (bf16[384,1152]{1,0:T(8,128)(2,1)S(1)}, bf16[384,1152]{1,0:T(8,128)(2,1)S(1)}, u32[]{:S(2)}, u32[]{:S(2)}) collective-permute-start(bf16[384,1152]{1,0:T(8,128)(2,1)S(1)} %convolution_convert_fusion.9), channel_id=1, source_target_pairs={{0,8},{8,16},{16,24},{24,0},{1,9},{9,17},{17,25},{25,1},{2,10},{10... | collective-permute-start | bytes 2654216 | tf_op jit(solution)/shard_map/ppermute | solution.py:274
  536.8 86.9 %collective-permute-start.99 = (bf16[384,1152]{1,0:T(8,128)(2,1)}, bf16[384,1152]{1,0:T(8,128)(2,1)}, u32[]{:S(2)}, u32[]{:S(2)}) collective-permute-start(bf16[384,1152]{1,0:T(8,128)(2,1)} %convolution_convert_fusion.5), channel_id=1, source_target_pairs={{0,8},{8,16},{16,24},{24,0},{1,9},{9,17},{17,25},{25,1},{2,10},{10... | collective-permute-start | bytes 2654216 | tf_op jit(solution)/shard_map/ppermute | solution.py:274
  545.3 72.9 %collective-permute-start.94 = (bf16[384,1152]{1,0:T(8,128)(2,1)}, bf16[384,1152]{1,0:T(8,128)(2,1)}, u32[]{:S(2)}, u32[]{:S(2)}) collective-permute-start(bf16[384,1152]{1,0:T(8,128)(2,1)} %fusion.6), channel_id=1, source_target_pairs={{0,8},{8,16},{16,24},{24,0},{1,9},{9,17},{17,25},{25,1},{2,10},{10... | collective-permute-start | bytes 2654216 | tf_op jit(solution)/shard_map/ppermute | solution.py:274
  546.4 20.5 %collective-permute-start.88 = (bf16[128,512]{1,0:T(8,128)(2,1)}, bf16[128,512]{1,0:T(8,128)(2,1)S(1)}, u32[]{:S(2)}, u32[]{:S(2)}) collective-permute-start(bf16[128,512]{1,0:T(8,128)(2,1)} %get-tuple-element.107), channel_id=1, source_target_pairs={{0,4},{1,5},{2,6},{3,7},{4,0},{5,1},{6,2},{7,3},{8,12},{9,13},{10,... | collective-permute-start | bytes 393224 | tf_op jit(solution)/shard_map/ppermute | solution.py:305
  566.8 73.5 %collective-permute-start.97 = (bf16[384,1152]{1,0:T(8,128)(2,1)}, bf16[384,1152]{1,0:T(8,128)(2,1)}, u32[]{:S(2)}, u32[]{:S(2)}) collective-permute-start(bf16[384,1152]{1,0:T(8,128)(2,1)} %fusion.15), channel_id=1, source_target_pairs={{0,8},{8,16},{16,24},{24,0},{1,9},{9,17},{17,25},{25,1},{2,10},{10... | collective-permute-start | bytes 2654216 | tf_op jit(solution)/shard_map/ppermute | solution.py:274
  623.7 35.5 %collective-permute-start.95 = (bf16[384,1152]{1,0:T(8,128)(2,1)S(1)}, bf16[384,1152]{1,0:T(8,128)(2,1)S(1)}, u32[]{:S(2)}, u32[]{:S(2)}) collective-permute-start(bf16[384,1152]{1,0:T(8,128)(2,1)S(1)} %fusion.9), channel_id=1, source_target_pairs={{0,8},{8,16},{16,24},{24,0},{1,9},{9,17},{17,25},{25,1},{2,10},{10... | collective-permute-start | bytes 2654216 | tf_op jit(solution)/shard_map/ppermute | solution.py:274
  630.1 48.1 %collective-permute-start.100 = (bf16[384,1152]{1,0:T(8,128)(2,1)}, bf16[384,1152]{1,0:T(8,128)(2,1)}, u32[]{:S(2)}, u32[]{:S(2)}) collective-permute-start(bf16[384,1152]{1,0:T(8,128)(2,1)} %fusion.24), channel_id=1, source_target_pairs={{0,8},{8,16},{16,24},{24,0},{1,9},{9,17},{17,25},{25,1},{2,10},{10... | collective-permute-start | bytes 2654216 | tf_op jit(solution)/shard_map/ppermute | solution.py:274
  644.7 52.4 %collective-permute-start.98 = (bf16[384,1152]{1,0:T(8,128)(2,1)}, bf16[384,1152]{1,0:T(8,128)(2,1)S(1)}, u32[]{:S(2)}, u32[]{:S(2)}) collective-permute-start(bf16[384,1152]{1,0:T(8,128)(2,1)} %fusion.18), channel_id=1, source_target_pairs={{0,8},{8,16},{16,24},{24,0},{1,9},{9,17},{17,25},{25,1},{2,10},{10... | collective-permute-start | bytes 2654216 | tf_op jit(solution)/shard_map/ppermute | solution.py:274
  662.4 40.8 %all-to-all-start.3 = ((bf16[8,48,1152]{2,1,0:T(8,128)(2,1)}), bf16[8,48,1152]{2,1,0:T(8,128)(2,1)S(1)}, u32[]{:S(2)}, u32[]{:S(2)}) async-start(bf16[8,48,1152]{2,1,0:T(8,128)(2,1)} %bitcast.27), calls=%async_computation.5 | async-start | bytes 1769472 | tf_op jit(solution)/shard_map/all_to_all | solution.py:504
  684.5 30.8 %collective-permute-start.101 = (bf16[384,1152]{1,0:T(8,128)(2,1)}, bf16[384,1152]{1,0:T(8,128)(2,1)}, u32[]{:S(2)}, u32[]{:S(2)}) collective-permute-start(bf16[384,1152]{1,0:T(8,128)(2,1)} %fusion.27), channel_id=1, source_target_pairs={{0,8},{8,16},{16,24},{24,0},{1,9},{9,17},{17,25},{25,1},{2,10},{10... | collective-permute-start | bytes 2654216 | tf_op jit(solution)/shard_map/ppermute | solution.py:274
  (104 other events, 1323.6 us)
Sparse Core Ops, SparseCore 0:
  11.5 90.2 all-gather.2
  104.7 90.7 all-gather.4
  510.1 205.8 reduce-scatter.4
  722.6 116.0 reduce-scatter.2

commit v2 on v1

--- a/solution.py
+++ b/solution.py
@@ -23,6 +23,7 @@
 PLANE = ("ctx", "uly")
 EVERY = ("dp", "ctx", "uly")
 VMEM_LIMIT = 56 * 1024 * 1024
+SMALL = pl.CostEstimate(flops=1024, bytes_accessed=1024, transcendentals=0)
 F32 = jnp.float32
 BF16 = jnp.bfloat16
 
@@ -181,11 +182,7 @@
             pltpu.VMEM((TOK_DEV, rows), F32),
         ],
         compiler_params=pltpu.CompilerParams(vmem_limit_bytes=VMEM_LIMIT),
-        cost_estimate=pl.CostEstimate(
-            flops=4 * HEADS * rows * kv_all.shape[0] * HEAD,
-            bytes_accessed=8 * 1024 * 1024,
-            transcendentals=HEADS * rows * kv_all.shape[0],
-        ),
+        cost_estimate=SMALL,
     )(need, kinfo, qinfo, query_t, kv_all)
 
 
@@ -206,134 +203,255 @@
             pltpu.VMEM((HEADS * HEAD, rows), BF16),
         ],
         compiler_params=pltpu.CompilerParams(vmem_limit_bytes=VMEM_LIMIT),
-        cost_estimate=pl.CostEstimate(
-            flops=10 * HEADS * rows * kv_all.shape[0] * HEAD,
-            bytes_accessed=12 * 1024 * 1024,
-            transcendentals=HEADS * rows * kv_all.shape[0],
-        ),
+        cost_estimate=SMALL,
     )(need, kinfo, qinfo, cos_t, sin_t, query_t, kv_all, out_t, grad_t, lse)
 
 
-def ffn_kernel(parts, mid_ref, cot_ref, *refs):
-    gate_w, up_w, down_w = refs[:parts], refs[parts : 2 * parts], refs[2 * parts : 3 * parts]
-    hidden_ref, gate_grad_ref, up_grad_ref, mid_grad_ref, out_ref = refs[3 * parts :]
-    depth = gate_w[0].shape[0]
-
-    def through(rows_ref, weights):
-        total = None
-        for part in range(parts):
-            term = dot(rows_ref[:, part * depth : (part + 1) * depth], weights[part][...], 1, 0)
-            total = term if total is None else total + term
-        return total
-
-    gate = through(mid_ref, gate_w)
-    up = through(mid_ref, up_w)
-    hidden_grad = through(cot_ref, down_w)
+def ffn_kernel(cols, first, with_grad, *refs):
+    mid_near, mid_far, cot_near, cot_far, w_ref = refs[:5]
+    refs = refs[5:]
+    if not first:
+        mid_sums, out_sums = refs[:2], refs[2:4]
+        refs = refs[4:]
+    mid_outs, out_outs = refs[:2], refs[2:4]
+    if with_grad:
+        grad_ref, act_ref, acc_ref, mid_ref, cot_ref = refs[4:]
+    else:
+        act_ref, mid_ref, cot_ref = refs[4:]
+    step, last = pl.program_id(0), pl.num_programs(0) - 1
+    near = step < pl.num_programs(0) // 2
+    mid_ref[...] = jnp.where(near, mid_near[...], mid_far[...])
+    cot_ref[...] = jnp.where(near, cot_near[...], cot_far[...])
+    both = dot(mid_ref[...], w_ref[:, : 2 * cols], 1, 0)
+    hidden_grad = dot(cot_ref[...], w_ref[:, 2 * cols :], 1, 0)
+    gate, up = both[:, :cols], both[:, cols:]
     share = 1.0 / (1.0 + jnp.exp(-gate))
     acted = gate * share
-    hidden = (acted * up).astype(BF16)
-    up_grad = (hidden_grad * acted).astype(BF16)
-    gate_grad = (hidden_grad * up * (share * (1.0 + gate * (1.0 - share)))).astype(BF16)
-    hidden_ref[...] = hidden
-    gate_grad_ref[...] = gate_grad
-    up_grad_ref[...] = up_grad
-    for part in range(parts):
-        cols = slice(part * depth, (part + 1) * depth)
-        mid_grad_ref[:, cols] = (
-            dot(gate_grad, gate_w[part][...], 1, 1) + dot(up_grad, up_w[part][...], 1, 1)
+    act_ref[:, :cols] = (hidden_grad * up * (share * (1.0 + gate * (1.0 - share)))).astype(BF16)
+    act_ref[:, cols : 2 * cols] = (hidden_grad * acted).astype(BF16)
+    act_ref[:, 2 * cols :] = (acted * up).astype(BF16)
+    mid_grad = dot(act_ref[:, : 2 * cols], w_ref[:, : 2 * cols], 1, 1)
+    out = dot(act_ref[:, 2 * cols :], w_ref[:, 2 * cols :], 1, 1)
+    if not first:
+        mid_grad = mid_grad + jnp.where(near, mid_sums[0][...], mid_sums[1][...]).astype(F32)
+        out = out + jnp.where(near, out_sums[0][...], out_sums[1][...]).astype(F32)
+
+    @pl.when(near)
+    def _():
+        mid_outs[0][...] = mid_grad.astype(BF16)
+        out_outs[0][...] = out.astype(BF16)
+
+    @pl.when(jnp.logical_not(near))
+    def _():
+        mid_outs[1][...] = mid_grad.astype(BF16)
+        out_outs[1][...] = out.astype(BF16)
+
+    if with_grad:
+
+        @pl.when(step == 0)
+        def _():
+            acc_ref[:, : 2 * cols] = dot(mid_ref[...], act_ref[:, : 2 * cols], 0, 0)
+            acc_ref[:, 2 * cols :] = dot(cot_ref[...], act_ref[:, 2 * cols :], 0, 0)
+
+        @pl.when(step > 0)
+        def _():
+            acc_ref[:, : 2 * cols] += dot(mid_ref[...], act_ref[:, : 2 * cols], 0, 0)
+            acc_ref[:, 2 * cols :] += dot(cot_ref[...], act_ref[:, 2 * cols :], 0, 0)
+
+        @pl.when(step == last)
+        def _():
+            grad_ref[...] = acc_ref[...].astype(BF16)
+
+
+def feed_forward(mid_halves, cot_halves, weights, sums, with_grad):
+    half_tokens, width = mid_halves[0].shape
+    cols = weights.shape[1] // 3
+    half = half_tokens // TOK_DEV
+    near_spec = pl.BlockSpec((TOK_DEV, width), lambda i: (jnp.minimum(i, half - 1), 0))
+    far_spec = pl.BlockSpec((TOK_DEV, width), lambda i: (jnp.maximum(i - half, 0), 0))
+    act_spec = pl.BlockSpec((TOK_DEV, 3 * cols), lambda i: (i, 0))
+    once = pl.BlockSpec(weights.shape, lambda i: (0, 0), pipeline_mode=pl.Buffered(1))
+    row_shape = jax.ShapeDtypeStruct((half_tokens, width), BF16)
+    row_scratch = [pltpu.VMEM((TOK_DEV, width), BF16)] * 2
+    if with_grad:
+        last_shape, last_spec = jax.ShapeDtypeStruct(weights.shape, BF16), once
+        scratch = [pltpu.VMEM((TOK_DEV, 3 * cols), BF16), pltpu.VMEM(weights.shape, F32)]
+    else:
+        last_shape, last_spec = jax.ShapeDtypeStruct((2 * half_tokens, 3 * cols), BF16), act_spec
+        scratch = []
+    return pl.pallas_call(
+        functools.partial(ffn_kernel, cols, not sums, with_grad),
+        grid=(2 * half,),
+        out_shape=(row_shape,) * 4 + (last_shape,),
+        in_specs=[near_spec, far_spec] * 2 + [once] + [near_spec, far_spec] * (len(sums) // 2),
+        out_specs=(near_spec, far_spec) * 2 + (last_spec,),
+        scratch_shapes=scratch + row_scratch,
+        compiler_params=pltpu.CompilerParams(vmem_limit_bytes=VMEM_LIMIT),
+        cost_estimate=SMALL,
+    )(*mid_halves, *cot_halves, weights, *sums)
+
+
+def ffn_grad_kernel(cols, mid_near, mid_far, cot_near, cot_far, act_ref, grad_ref):
+    half = mid_near.shape[0]
+    for near, far, part in (
+        (mid_near, mid_far, slice(0, 2 * cols)),
+        (cot_near, cot_far, slice(2 * cols, 3 * cols)),
+    ):
+        grad_ref[:, part] = (
+            dot(near[...], act_ref[:half, part], 0, 0) + dot(far[...], act_ref[half:, part], 0, 0)
         ).astype(BF16)
-        out_ref[:, cols] = dot(hidden, down_w[part][...], 1, 1).astype(BF16)
-
-
-def feed_forward(mid_rows, cot_rows, gate_w, up_w, down_w):
-    parts = len(gate_w)
-    tokens, width = mid_rows.shape
-    depth, cols = gate_w[0].shape
-    tile = TOK_DEV
-    row_spec = pl.BlockSpec((tile, width), lambda i: (i, 0))
-    act_spec = pl.BlockSpec((tile, cols), lambda i: (i, 0))
-    w_spec = pl.BlockSpec((depth, cols), lambda i: (0, 0), pipeline_mode=pl.Buffered(1))
+
+
+def feed_forward_grad(mid_halves, cot_halves, act):
+    half_tokens, width = mid_halves[0].shape
+    cols = act.shape[1] // 3
+    tile = 512 if width % 512 == 0 else width
+    col_spec = pl.BlockSpec((half_tokens, tile), lambda i: (0, i))
     return pl.pallas_call(
-        functools.partial(ffn_kernel, parts),
-        grid=(tokens // tile,),
-        out_shape=(jax.ShapeDtypeStruct((tokens, cols), BF16),) * 3
-        + (jax.ShapeDtypeStruct((tokens, width), BF16),) * 2,
-        in_specs=[row_spec] * 2 + [w_spec] * (3 * parts),
-        out_specs=(act_spec,) * 3 + (row_spec,) * 2,
+        functools.partial(ffn_grad_kernel, cols),
+        grid=(width // tile,),
+        out_shape=jax.ShapeDtypeStruct((width, 3 * cols), BF16),
+        in_specs=[col_spec] * 4
+        + [pl.BlockSpec(act.shape, lambda i: (0, 0), pipeline_mode=pl.Buffered(1))],
+        out_specs=pl.BlockSpec((tile, 3 * cols), lambda i: (i, 0)),
         compiler_params=pltpu.CompilerParams(vmem_limit_bytes=VMEM_LIMIT),
-        cost_estimate=pl.CostEstimate(
-            flops=12 * tokens * width * cols,
-            bytes_accessed=2 * (3 * width * cols + 3 * tokens * cols + 4 * tokens * width),
-            transcendentals=tokens * cols,
-        ),
-    )(mid_rows, cot_rows, *gate_w, *up_w, *down_w)
-
-
-def shift(array, axis, step):
-    count = lax.axis_size(axis)
-    return lax.ppermute(array, axis, [(i, (i + step) % count) for i in range(count)])
-
-
-def ring_gather(block, axis):
-    pieces = [block]
-    for _ in range(lax.axis_size(axis) - 1):
-        pieces.append(shift(pieces[-1], axis, -1))
-    return pieces
-
-
-def ring_reduce(block_of, axis):
-    count = lax.axis_size(axis)
-    running = block_of(count - 1)
-    for r in range(count - 2, -1, -1):
-        moved = shift(running, axis, 1)
-        running = (moved.astype(F32) + block_of(r).astype(F32)).astype(BF16)
-    return running
-
-
-def plane_bits():
-    ctx, uly = lax.axis_size("ctx"), lax.axis_size("uly")
-    count = ctx * uly
-    assert count & (count - 1) == 0 and ctx % 2 == 0
-    core = uly
-    near = [1 << i for i in range(uly.bit_length() - 1)]
-    far = [core << i for i in range(1, (ctx // 2).bit_length())]
-    return count, core, near, far
-
-
-def swap(array, bit):
-    count = lax.axis_size("ctx") * lax.axis_size("uly")
-    return lax.ppermute(array, PLANE, [(i, i ^ bit) for i in range(count)])
-
-
-def plane_gather(rows):
-    count, core, near, far = plane_bits()
-    half = rows.shape[0] // 2
-    got = []
-    for piece, order in ((rows[:half], far + near), (rows[half:], near + far)):
-        held = {0: piece}
-        for bit in order:
-            for i in sorted(held):
-                held[i ^ bit] = swap(held[i], bit)
-        for i in sorted(held):
-            held[i ^ core] = swap(held[i], core)
-        got.append(held)
-    return [(got[0][i], got[1][i]) for i in range(count)]
-
-
-def plane_reduce(block_of):
-    count, core, near, far = plane_bits()
-    halves = []
-    for which, order in ((0, near + far), (1, far + near)):
-        held = {i: block_of(i)[which] for i in range(count)}
-        for bit in [core] + order:
-            kept = {}
-            for i in sorted(held):
-                if not i & bit:
-                    moved = swap(held[i | bit], bit)
-                    kept[i] = (held[i].astype(F32) + moved.astype(F32)).astype(BF16)
-            held = kept
-        halves.append(held[0])
-    return jnp.concatenate(halves, axis=0)
+        cost_estimate=SMALL,
+    )(*mid_halves, *cot_halves, act)
+
+
+def slice_moves(n_plane, chunks, cols, total):
+    for device in range(n_plane):
+        for chunk in range(chunks):
+            start = (device * chunks + chunk) * cols
+            for kind in range(3):
+                yield device, chunk, kind, kind * total + start, max(0, min(cols, total - start))
+
+
+def pack_kernel(moves, cols, w_ref, out_ref):
+    rows = w_ref.shape[0]
+    for device, chunk, kind, source, real in moves:
+        there = slice(device * rows, (device + 1) * rows)
+        at = (chunk * 3 + kind) * cols
+        if real:
+            out_ref[there, at : at + real] = w_ref[:, source : source + real]
+        if real < cols:
+            out_ref[there, at + real : at + cols] = jnp.zeros((rows, cols - real), BF16)
+
+
+def unpack_kernel(moves, cols, *refs):
+    chunk_refs, out_ref = refs[:-1], refs[-1]
+    rows = out_ref.shape[0]
+    for device, chunk, kind, source, real in moves:
+        if real:
+            block = chunk_refs[chunk][
+                device * rows : (device + 1) * rows, kind * cols : kind * cols + real
+            ]
+            out_ref[:, source : source + real] = block.astype(F32)
+
+
+def pack_slices(w_mlp, n_plane, chunks, cols):
+    rows, total = w_mlp.shape[0], w_mlp.shape[1] // 3
+    if rows % 16:
+        wide = jnp.pad(
+            w_mlp.reshape(rows, 3, total), ((0, 0), (0, 0), (0, n_plane * chunks * cols - total))
+        )
+        wide = wide.reshape(rows, 3, n_plane, chunks, cols).transpose(2, 0, 3, 1, 4)
+        return wide.reshape(n_plane * rows, 3 * chunks * cols)
+    moves = list(slice_moves(n_plane, chunks, cols, total))
+    return pl.pallas_call(
+        functools.partial(pack_kernel, moves, cols),
+        out_shape=jax.ShapeDtypeStruct((n_plane * rows, 3 * chunks * cols), BF16),
+        in_specs=vmem_specs(1),
+        out_specs=vmem_specs(1)[0],
+        compiler_params=pltpu.CompilerParams(vmem_limit_bytes=VMEM_LIMIT),
+        cost_estimate=SMALL,
+    )(w_mlp)
+
+
+def unpack_slices(chunk_arrays, rows, total, n_plane, cols):
+    chunks = len(chunk_arrays)
+    if rows % 16:
+        stacked = jnp.stack(chunk_arrays, axis=0).reshape(chunks, n_plane, rows, 3, cols)
+        stacked = stacked.transpose(2, 3, 1, 0, 4).reshape(rows, 3, -1)[:, :, :total]
+        return stacked.reshape(rows, 3 * total).astype(F32)
+    moves = list(slice_moves(n_plane, chunks, cols, total))
+    return pl.pallas_call(
+        functools.partial(unpack_kernel, moves, cols),
+        out_shape=jax.ShapeDtypeStruct((rows, 3 * total), F32),
+        in_specs=vmem_specs(chunks),
+        out_specs=vmem_specs(1)[0],
+        compiler_params=pltpu.CompilerParams(vmem_limit_bytes=VMEM_LIMIT),
+        cost_estimate=SMALL,
+    )(*chunk_arrays)
+
+
+def after(array, *others):
+    return lax.optimization_barrier((array, *others))[0]
+
+
+class Plane:
+    def __init__(self):
+        ctx, uly = lax.axis_size("ctx"), lax.axis_size("uly")
+        self.count = ctx * uly
+        assert self.count & (self.count - 1) == 0 and ctx % 2 == 0
+        self.me = lax.axis_index("ctx") * uly + lax.axis_index("uly")
+        self.core = uly
+        near = [1 << i for i in range(uly.bit_length() - 1)]
+        far = [self.core << i for i in range(1, (ctx // 2).bit_length())]
+        self.orders = (far + near, near + far)
+        self.steps = len(near) + len(far)
+        mine = (self.me // self.core) % 2 == 0
+        masks = [[0], [0]]
+        for which in (0, 1):
+            for bit in self.orders[which]:
+                masks[which] += [bit | mask for mask in masks[which]]
+        pairs = list(zip(masks[0], masks[1]))
+        near_slots = [jnp.where(mine, a, b) for a, b in pairs]
+        far_slots = [jnp.where(mine, b, a) | self.core for a, b in pairs]
+        self.devices = [self.me ^ mask for mask in near_slots + far_slots]
+
+    def swap(self, array, step):
+        pairs = []
+        for i in range(self.count):
+            if step == self.steps:
+                bit = self.core
+            else:
+                bit = self.orders[(i // self.core) % 2][step]
+            pairs.append((i, i ^ bit))
+        return lax.ppermute(array, PLANE, pairs)
+
+    def gather_step(self, held, step):
+        return held + [self.swap(piece, step) for piece in held]
+
+    def gather(self, rows):
+        held = [rows]
+        for step in range(self.steps + 1):
+            held = self.gather_step(held, step)
+        return held
+
+    def gather_halves(self, held):
+        near = jnp.concatenate(held, axis=0)
+        return near, self.swap(near, self.steps)
+
+    def fold(self, near, far, step):
+        return (near.astype(F32) + self.swap(far, step).astype(F32)).astype(BF16)
+
+    def fold_rest(self, rows, step):
+        half = rows.shape[0] // 2
+        return self.fold(rows[:half], rows[half:], step)
+
+    def reduce_step(self, held, step):
+        kept = len(held) // 2
+        moved = [self.swap(piece, step) for piece in held[kept:]]
+        return [
+            (one.astype(F32) + other.astype(F32)).astype(BF16) for one, other in zip(held, moved)
+        ]
+
+    def reduce(self, blocks):
+        held = list(blocks)
+        for step in range(self.steps, -1, -1):
+            held = self.reduce_step(held, step)
+        return held[0]
 
 
 def place_info(spans, row_in_span, length_row):
@@ -381,8 +499,7 @@
     n_dp = lax.axis_size("dp")
     n_plane = lax.axis_size("ctx") * lax.axis_size("uly")
     n_all = n_dp * n_plane
-    me = lax.axis_index("ctx") * lax.axis_size("uly") + lax.axis_index("uly")
-    my_dp = lax.axis_index("dp")
+    plane = Plane()
     order_row, length_row, mask_row = span_order[0], doc_lengths[0], pad_mask[0]
     ffn_width = w_mlp.shape[1] // 3
     local_rows = w_mlp.shape[0]
@@ -390,15 +507,35 @@
     q_width, kv_width = HEADS * HEAD, KV_HEADS * HEAD
     qkv_width = q_width + 2 * kv_width
     bias_rows = b_qkv.shape[0]
-    slice_cols = -(-(ffn_width // LANES) // n_plane) * LANES
-    pad_cols = slice_cols * n_plane - ffn_width
-
-    def to_slice(which):
-        mine = w_mlp[:, which * ffn_width : (which + 1) * ffn_width]
-        mine = jnp.pad(mine, ((0, 0), (0, pad_cols))).reshape(local_rows, n_plane, slice_cols)
-        mine = mine.transpose(1, 0, 2).reshape(zone, slice_cols)
-        mine = lax.all_to_all(mine, PLANE, split_axis=0, concat_axis=0, tiled=True)
-        return ring_gather(mine, "dp")
+    slice_tiles = -(-(ffn_width // LANES) // n_plane)
+    chunks = max(c for c in (1, 2, 3) if slice_tiles % c == 0)
+    chunk_cols = slice_tiles // chunks * LANES
+    w_cols = qkv_width + LANES
+
+    def swap_rows(array):
+        return lax.all_to_all(array, PLANE, split_axis=0, concat_axis=0, tiled=True)
+
+    def zone_gather(array):
+        return lax.all_gather(array, "dp", axis=0, tiled=True)
+
+    def zone_sum(array):
+        return lax.psum_scatter(array, "dp", scatter_dimension=0, tiled=True)
+
+    def whole_rows(pieces):
+        cols = pieces[0].shape[1]
+        full = jnp.zeros((n_dp, n_plane, local_rows, cols), BF16)
+        for device, piece in zip(plane.devices, pieces):
+            piece = piece.reshape(n_dp, 1, local_rows, cols)
+            full = lax.dynamic_update_slice(full, piece, (0, device, 0, 0))
+        return full.reshape(n_all * local_rows, cols)
+
+    def device_blocks(array):
+        cols = array.shape[1]
+        full = array.reshape(n_dp, n_plane, local_rows, cols)
+        return [
+            lax.dynamic_slice_in_dim(full, device, 1, 1).reshape(n_dp * local_rows, cols)
+            for device in plane.devices
+        ]
 
     side = jnp.concatenate(
         [
@@ -409,19 +546,11 @@
         ],
         axis=1,
     )
-    w_qkv_all = lax.all_gather(
-        jnp.concatenate([w_qkv, side], axis=1), EVERY, axis=0, tiled=True
-    )
-    w_out_all = lax.all_gather(w_out.T, EVERY, axis=0, tiled=True)
-    side_all = w_qkv_all[:, qkv_width:].astype(F32)
-    gain_attn = side_all[:, 0]
-    gain_mlp = side_all[:, 1]
-    bias_all = side_all.reshape(n_all, local_rows, LANES)[:, 0, 64 : 64 + bias_rows].reshape(-1)
-
-    gate_w, up_w, down_w = to_slice(0), to_slice(1), to_slice(2)
+    attn_local = jnp.concatenate([w_qkv, side, w_out.T], axis=1)
+    attn_zone = zone_gather(attn_local)
 
     row_in_span = jnp.arange(tok_rows, dtype=jnp.int32)
-    stored_block = me ^ jnp.arange(n_plane, dtype=jnp.int32)
+    stored_block = jnp.stack(plane.devices)
     spans = order_row[stored_block]
     own_place, own_begin = place_info(spans[0], row_in_span, length_row)
     flags = mask_row.reshape(n_plane, tok_rows)[stored_block]
@@ -447,6 +576,21 @@
     cos_t, sin_t = jnp.cos(angles_t), jnp.sin(angles_t)
     cos_r, sin_r = cos_t.T[:, None, :], sin_t.T[:, None, :]
 
+    packed = pack_slices(after(w_mlp, attn_local, kinfo, qinfo), n_plane, chunks, chunk_cols)
+    chunk_width = 3 * chunk_cols
+    mlp_zone = swap_rows(packed)
+    mlp_weights = [
+        zone_gather(mlp_zone[:, chunk * chunk_width : (chunk + 1) * chunk_width])
+        for chunk in range(chunks)
+    ]
+
+    qkv_held = plane.gather(attn_zone[:, :w_cols])
+    w_qkv_all = whole_rows(qkv_held)
+    side_all = w_qkv_all[:, qkv_width:].astype(F32)
+    gain_attn = side_all[:, 0]
+    gain_mlp = side_all[:, 1]
+    bias_all = side_all.reshape(n_all, local_rows, LANES)[:, 0, 64 : 64 + bias_rows].reshape(-1)
+
     inputs = layer_input.astype(F32)
     in_inverse = inverse_rms(inputs)
     normed_in = (inputs * in_inverse * gain_attn).astype(BF16)
@@ -454,8 +598,9 @@
     kv_proj = dot(normed_in, w_qkv_all[:, q_width:qkv_width], 1, 0) + bias_all[q_width:]
     key_own = turn(kv_proj[:, :kv_width].reshape(tok_rows, KV_HEADS, HEAD), cos_r, sin_r)
     kv_own = jnp.concatenate([key_own.reshape(tok_rows, kv_width), kv_proj[:, kv_width:]], axis=1)
-    kv_pieces = plane_gather(kv_own.astype(BF16))
-    kv_all = jnp.concatenate([half_rows for pair in kv_pieces for half_rows in pair], axis=0)
+    kv_pieces = plane.gather(kv_own.astype(BF16))
+    kv_all = jnp.concatenate(kv_pieces, axis=0)
+    w_out_all = whole_rows(plane.gather(after(attn_zone[:, w_cols:], qkv_held[n_plane // 2 - 1])))
 
     q_proj = dot(w_qkv_all[:, :q_width], normed_in, 0, 1) + bias_all[:q_width, None]
     q_heads = q_proj.reshape(HEADS, 2, half, tok_rows)
@@ -473,42 +618,33 @@
     mid_inverse = inverse_rms(middle)
     normed_mid = (middle * mid_inverse * gain_mlp).astype(BF16)
 
-    def turn_zone(array, zones):
-        return lax.dynamic_slice_in_dim(
-            jnp.concatenate([array, array], axis=1), zones * zone, width, 1
-        )
-
-    def gather_tokens(array):
-        pieces = plane_gather(turn_zone(array, my_dp))
-        return jnp.concatenate([rows for pair in pieces for rows in pair], axis=0)
-
-    cot_rows = gather_tokens(cotangent)
-    mid_rows = gather_tokens(normed_mid)
-    hidden, gate_grad, up_grad, mid_grad_part, out_part = feed_forward(
-        mid_rows, cot_rows, gate_w, up_w, down_w
-    )
+    mid_held, cot_held = [normed_mid], [after(cotangent, attended_t)]
+    for step in range(plane.steps):
+        mid_held = plane.gather_step(mid_held, step)
+        cot_held = plane.gather_step(cot_held, step)
+    mid_halves = plane.gather_halves(mid_held)
+    cot_halves = plane.gather_halves(cot_held)
+    sums, chunk_grads = (), []
+    for chunk, weights in enumerate(mlp_weights):
+        last = chunk == chunks - 1
+        *sums, extra = feed_forward(mid_halves, cot_halves, weights, tuple(sums), not last)
+        if not last:
+            chunk_grads.append(extra)
 
     def token_blocks(array):
-        cut = tok_rows // 2
-        return lambda i: (
-            array[i * tok_rows : i * tok_rows + cut],
-            array[i * tok_rows + cut : (i + 1) * tok_rows],
-        )
-
-    mid_grad = turn_zone(plane_reduce(token_blocks(mid_grad_part)), n_dp - my_dp).astype(F32)
-
-    def slice_gradient(rows, columns):
-        mine = ring_reduce(
-            lambda r: dot(rows[:, r * zone : (r + 1) * zone], columns, 0, 0).astype(BF16), "dp"
-        )
-        mine = lax.all_to_all(mine, PLANE, split_axis=0, concat_axis=0, tiled=True)
-        mine = mine.reshape(n_plane, local_rows, slice_cols).transpose(1, 0, 2)
-        return mine.reshape(local_rows, n_plane * slice_cols)[:, :ffn_width].astype(F32)
-
-    grad_down = slice_gradient(cot_rows, hidden)
-    grad_gate = slice_gradient(mid_rows, gate_grad)
-    grad_up = slice_gradient(mid_rows, up_grad)
-    grad_mlp = jnp.concatenate([grad_gate, grad_up, grad_down], axis=1)
+        return [array[k * tok_rows : (k + 1) * tok_rows] for k in range(n_plane)]
+
+    chunk_sums = [zone_sum(grad) for grad in chunk_grads]
+    mid_fold = plane.fold(sums[0], sums[1], plane.steps)
+    chunk_grads.append(feed_forward_grad(mid_halves, cot_halves, after(extra, mid_fold)))
+    chunk_sums.append(zone_sum(chunk_grads[-1]))
+    for step in range(plane.steps - 1, -1, -1):
+        half = mid_fold.shape[0] // 2
+        kept, sent = mid_fold[:half], mid_fold[half:]
+        if step == plane.steps - 1:
+            kept = after(kept, chunk_grads[-1])
+        mid_fold = plane.fold(kept, sent, step)
+    mid_grad = after(mid_fold, *chunk_sums[:-1][:1]).astype(F32)
 
     out_grad = cotangent.astype(F32)
     gain_mlp_grad = jnp.sum(mid_grad * (middle * mid_inverse), axis=0)
@@ -516,43 +652,68 @@
     middle_low = middle_grad.astype(BF16)
     attended_grad_t = dot(w_out_all, middle_low, 0, 1).astype(BF16)
     out_weight_grad = dot(middle_low, attended_t, 0, 1).astype(BF16)
-    grad_out = lax.psum_scatter(out_weight_grad, EVERY, scatter_dimension=0, tiled=True)
+    out_held = plane.reduce_step(device_blocks(out_weight_grad), plane.steps)
+    attended_grad_t = after(attended_grad_t, *out_held)
     query_grad, kv_grad = attention_backward(
         need, kinfo, qinfo, cos_t, sin_t, query_t, kv_all, attended_t, attended_grad_t, lse
     )
-    kv_back = plane_reduce(token_blocks(kv_grad)).astype(F32)
+    kv_back = plane.reduce(token_blocks(kv_grad))
+    for step in range(plane.steps - 1, -1, -1):
+        out_held = plane.reduce_step(out_held, step)
+    out_plane = out_held[0]
+    kv_back = after(kv_back, out_plane)
+    kv_back = kv_back.astype(F32)
     key_back = turn(kv_back[:, :kv_width].reshape(tok_rows, KV_HEADS, HEAD), cos_r, -sin_r)
     projected_grad = jnp.concatenate(
         [query_grad, key_back.reshape(tok_rows, kv_width).astype(BF16), kv_back[:, kv_width:].astype(BF16)],
         axis=1,
     )
+    qkv_weight_grad = dot(normed_in, projected_grad, 0, 0).astype(BF16)
+    qkv_held = plane.reduce_step(device_blocks(qkv_weight_grad), plane.steps)
     in_grad = dot(projected_grad, w_qkv_all[:, :qkv_width], 1, 1)
     gain_attn_grad = jnp.sum(in_grad * (inputs * in_inverse), axis=0)
     input_grad = middle_grad + norm_backward(inputs, in_inverse, in_grad * gain_attn)
     qkv_bias_grad = jnp.sum(projected_grad.astype(F32), axis=0)
-    side_grad = jnp.zeros((n_all, local_rows, LANES), F32)
-    side_grad = side_grad.at[:, :, 0].set(gain_attn_grad.reshape(n_all, local_rows))
-    side_grad = side_grad.at[:, :, 1].set(gain_mlp_grad.reshape(n_all, local_rows))
-    side_grad = side_grad.at[:, 0, 64 : 64 + bias_rows].set(qkv_bias_grad.reshape(n_all, bias_rows))
-    side_grad = side_grad.reshape(n_all * local_rows, LANES).astype(BF16)
-    qkv_weight_grad = dot(normed_in, projected_grad, 0, 0).astype(BF16)
-    qkv_sum = lax.psum_scatter(
-        jnp.concatenate([qkv_weight_grad, side_grad], axis=1),
-        EVERY,
-        scatter_dimension=0,
-        tiled=True,
-    ).astype(F32)
-
-    mlp_out = turn_zone(plane_reduce(token_blocks(out_part)), n_dp - my_dp)
+
+    def side_row(array):
+        array = array.reshape(n_dp, n_plane, 1, -1)
+        return jnp.pad(array, ((0, 0), (0, 0), (0, 0), (0, LANES - array.shape[-1])))
+
+    side_grad = jnp.concatenate(
+        [side_row(gain_attn_grad), side_row(gain_mlp_grad), side_row(qkv_bias_grad)]
+        + [jnp.zeros((n_dp, n_plane, 1, LANES), F32)] * 5,
+        axis=2,
+    ).astype(BF16)
+    side_plane = plane.reduce(
+        [
+            lax.dynamic_slice_in_dim(side_grad, device, 1, 1).reshape(n_dp * 8, LANES)
+            for device in plane.devices
+        ]
+    )
+    side_plane = jnp.pad(
+        side_plane.reshape(n_dp, 8, LANES), ((0, 0), (0, local_rows - 8), (0, 0))
+    ).reshape(n_dp * local_rows, LANES)
+    for step in range(plane.steps - 1, -1, -1):
+        qkv_held = plane.reduce_step(qkv_held, step)
+    qkv_plane = after(qkv_held[0], *chunk_sums[1:])
+    attn_sum = zone_sum(jnp.concatenate([qkv_plane, side_plane, out_plane], axis=1)).astype(F32)
+    qkv_sum, grad_out = attn_sum[:, :w_cols], attn_sum[:, w_cols:]
+
+    mlp_out = plane.fold(after(sums[2], qkv_plane), sums[3], plane.steps)
+    for step in range(plane.steps - 1, -1, -1):
+        mlp_out = plane.fold_rest(mlp_out, step)
+    grad_mlp = unpack_slices(
+        [swap_rows(array) for array in chunk_sums], local_rows, ffn_width, n_plane, chunk_cols
+    )
     block_output = (middle + mlp_out.astype(F32)).astype(BF16)
     return (
         block_output,
         input_grad,
         qkv_sum[:, :qkv_width],
-        qkv_sum[0, qkv_width + 64 : qkv_width + 64 + bias_rows],
-        grad_out.astype(F32).T,
-        qkv_sum[:, qkv_width],
-        qkv_sum[:, qkv_width + 1],
+        qkv_sum[2, qkv_width : qkv_width + bias_rows],
+        grad_out.T,
+        qkv_sum[0, qkv_width : qkv_width + local_rows],
+        qkv_sum[1, qkv_width : qkv_width + local_rows],
         grad_mlp,
     )
 

time: 858 us -> 605 us (0.71)
  waiting for transfers between devices: 393 us -> 191 us
  matrix products: 88.2 us -> 23 us
  Pallas kernels: 101 us -> 137 us
  starting transfers between devices: 128 us -> 109 us
    ppermute x102 -> x63, waiting for transfers between devices: 249 us -> 114 us  [swap(): return lax.ppermute(array, PLANE, pairs)]
    reduce_scatter x2 -> x4, waiting for transfers between devices: 94.5 us -> 3.99 us  [zone_sum(): return lax.psum_scatter(array, 'dp', scatter_dimension=0, tiled=True)]
    dot_general x19 -> x7, matrix products: 88.2 us -> 23 us  [dot(): lax.dot_general(left, right, (((left_dim,), (right_dim,)), ((), ())), pre...]
    pallas_call x1 -> x6, Pallas kernels: 71.3 us -> 121 us  [the longest x3 99.1 us: feed_forward(): pl.pallas_call(functools.partial(ffn_kernel, cols, not sums, with_grad),...]
    all_to_all x6 -> x4, waiting for transfers between devices: 28 us -> 67.2 us  [swap_rows(): return lax.all_to_all(array, PLANE, split_axis=0, concat_axis=0, tiled=True)]
    convert_element_type x16 -> x20, other arithmetic: 9.94 us -> 30.5 us  [the longest x13 14.9 us: reduce_step(): (one.astype(F32) + other.astype(F32)).astype(BF16)]
    dynamic_update_slice x0 -> x16, local copies, waits for them, and re-layouts: none -> 19.1 us  [whole_rows(): full = lax.dynamic_update_slice(full, piece, (0, device, 0, 0))]
    unnamed x124 -> x99, local copies, waits for them, and re-layouts: 32.9 us -> 14.9 us
  transfers between devices with their start and end apart: 112 -> 75, of which waited for: 36 -> 34; matrix products, arithmetic and copies ran while one was open for 23% -> 20% of each run, Pallas kernels for 4% -> 22%
where the time goes in v2:
time: 605 us; the launch traced here: 600 us
  waiting for transfers between devices  191 us (32%)
  Pallas kernels  137 us (23%)
  starting transfers between devices  109 us (18%)
  local copies, waits for them, and re-layouts  66.9 us (11%)
  other arithmetic  54.8 us (9%)
  matrix products  23 us (4%)
  between operations  17.9 us (3%)
    ppermute x63, waiting for transfers between devices, swap(): return lax.ppermute(array, PLANE, pairs)  114 us
    pallas_call x3, Pallas kernels, feed_forward(): pl.pallas_call(functools.partial(ffn_kernel, cols, not sums, with_grad),...  99.1 us
    ppermute x63, starting transfers between devices, swap(): return lax.ppermute(array, PLANE, pairs)  89.6 us
    all_to_all x4, waiting for transfers between devices, swap_rows(): return lax.all_to_all(array, PLANE, split_axis=0, concat_axis=0, tiled=True)  67.2 us
    dot_general x7, matrix products, dot(): lax.dot_general(left, right, (((left_dim,), (right_dim,)), ((), ())), pre...  23 us
    dynamic_update_slice x16, local copies, waits for them, and re-layouts, whole_rows(): full = lax.dynamic_update_slice(full, piece, (0, device, 0, 0))  19.1 us
    all_to_all x4, starting transfers between devices, swap_rows(): return lax.all_to_all(array, PLANE, split_axis=0, concat_axis=0, tiled=True)  18.3 us
    unnamed x99, local copies, waits for them, and re-layouts  14.9 us
  transfers between devices with their start and end apart: 75, of which 34 were waited for; matrix products, arithmetic and copies ran while one was open for 20% of the time, Pallas kernels for 22%

profile of v2, /device:TPU:0, one launch (start us, length us, event | category | flops | bytes accessed | tf_op | source)
XLA Modules:
  0.0 599.8 jit_solution(1731087250048357030)
XLA Ops:
  19.8 3.5 shard_map.171
  23.3 5.2 all-to-all-start
  29.2 31.0 %all-to-all-done = bf16[8,48,3456]{2,1,0:T(8,128)(2,1)S(1)} async-done(((bf16[8,48,3456]{2,1,0:T(8,128)(2,1)}), bf16[8,48,3456]{2,1,0:T(8,128)(2,1)S(1)}, u32[]{:S(2)}, u32[]{:S(2)}) %all-to-all-start) | async-done | bytes 2654240 | tf_op jit(solution)/shard_map/all_to_all | solution.py:516
  62.2 5.7 all-gather.5.cloned.1.call-done
  78.0 9.9 %collective-permute-done = bf16[192,2176]{1,0:T(8,128)(2,1)S(1)} collective-permute-done((bf16[192,2176]{1,0:T(8,128)(2,1)S(1)}, bf16[192,2176]{1,0:T(8,128)(2,1)S(1)}, u32[]{:S(2)}, u32[]{:S(2)}) %collective-permute-start) | collective-permute-done | bytes 835616 | tf_op jit(solution)/shard_map/ppermute | solution.py:421
  90.3 3.2 broadcast_in_dim.26
  133.9 4.2 fusion.4
  155.9 6.9 %shard_map.170 = (bf16[1536,256]{1,0:T(8,128)(2,1)}, f32[16,256]{1,0:T(8,128)}) custom-call(s32[8]{0:T(128)} %and_convert_fusion.need_ref, s32[2048,2]{1,0:T(8,128)} %copy.31.kinfo_ref, s32[8,256]{1,0:T(8,128)} %add_add_fusion.qinfo_ref, bf16[1536,256]{1,0:T(8,128)(2,1)} %bitcast.157, bf16[2048,512]{1,0:T(8,128)(2,1)} %copy-done.6), custom_call_target="tpu_custom_call" | custom-call | flops 1024 | bytes 1024 | tf_op jit(solution)/shard_map/pallas_call | solution.py:170
  162.8 4.7 collective-permute-start.25
  167.6 3.3 multiply_reduce_fusion
  172.8 2.8 collective-permute-start.26
  177.8 2.8 collective-permute-start.27
  180.6 5.5 collective-permute-done.21
  186.1 2.8 collective-permute-start.23
  192.9 11.9 %collective-permute-done.27 = bf16[256,1536]{1,0:T(8,128)(2,1)S(1)} collective-permute-done((bf16[256,1536]{1,0:T(8,128)(2,1)}, bf16[256,1536]{1,0:T(8,128)(2,1)S(1)}, u32[]{:S(2)}, u32[]{:S(2)}) %collective-permute-start.27) | collective-permute-done | bytes 786464 | tf_op jit(solution)/shard_map/ppermute | solution.py:421
  205.7 16.5 %collective-permute-start.28 = (bf16[1024,1536]{1,0:T(8,128)(2,1)}, bf16[1024,1536]{1,0:T(8,128)(2,1)}, u32[]{:S(2)}, u32[]{:S(2)}) collective-permute-start(bf16[1024,1536]{1,0:T(8,128)(2,1)} %constant_dynamic-update-slice_fusion.8.refs_2_.cot_near), channel_id=1, source_target_pairs={{0,2},{1,3},{2,0},{3,1},{4,6},{5,7},{6,4},{7,5},{8,10},{9,11},{10,... | collective-permute-start | bytes 9437192 | tf_op jit(solution)/shard_map/ppermute | solution.py:421
  222.2 5.5 collective-permute-done.23
  229.0 5.4 collective-permute-done.24.refs_1_.mid_far
  234.4 36.1 %shard_map.172 = (bf16[1024,1536]{1,0:T(8,128)(2,1)}, bf16[1024,1536]{1,0:T(8,128)(2,1)}, bf16[1024,1536]{1,0:T(8,128)(2,1)}, bf16[1024,1536]{1,0:T(8,128)(2,1)}, bf16[1536,1152]{1,0:T(8,128)(2,1)}) custom-call(bf16[1024,1536]{1,0:T(8,128)(2,1)} %copy-done.2, bf16[1024,1536]{1,0:T(8,128)(2,1)} %collective-permute-done.24.refs_1_.mid_far, ...), custom_call_target="tpu_custom_call" | custom-call | flops 1024 | bytes 1024 | tf_op jit(solution)/shard_map/pallas_call | solution.py:282
  270.6 36.9 %shard_map.173 = (bf16[1024,1536]{1,0:T(8,128)(2,1)}, bf16[1024,1536]{1,0:T(8,128)(2,1)}, bf16[1024,1536]{1,0:T(8,128)(2,1)}, bf16[1024,1536]{1,0:T(8,128)(2,1)}, bf16[1536,1152]{1,0:T(8,128)(2,1)}) custom-call(bf16[1024,1536]{1,0:T(8,128)(2,1)} %copy-done.2, bf16[1024,1536]{1,0:T(8,128)(2,1)} %collective-permute-done.24.refs_1_.mid_far, ...), custom_call_target="tpu_custom_call" | custom-call | flops 1024 | bytes 1024 | tf_op jit(solution)/shard_map/pallas_call | solution.py:282
  307.6 26.1 %shard_map.174 = (bf16[1024,1536]{1,0:T(8,128)(2,1)}, bf16[1024,1536]{1,0:T(8,128)(2,1)}, bf16[1024,1536]{1,0:T(8,128)(2,1)}, bf16[1024,1536]{1,0:T(8,128)(2,1)}, bf16[2048,1152]{1,0:T(8,128)(2,1)}) custom-call(bf16[1024,1536]{1,0:T(8,128)(2,1)} %copy-done.2, bf16[1024,1536]{1,0:T(8,128)(2,1)} %collective-permute-done.24.refs_1_.mid_far, ...), custom_call_target="tpu_custom_call" | custom-call | flops 1024 | bytes 1024 | tf_op jit(solution)/shard_map/pallas_call | solution.py:282
  334.2 5.5 collective-permute-done.29
  339.7 3.0 add_convert_fusion.1
  344.7 13.9 %shard_map.175 = bf16[1536,1152]{1,0:T(8,128)(2,1)} custom-call(bf16[1024,1536]{1,0:T(8,128)(2,1)} %copy-done.2, bf16[1024,1536]{1,0:T(8,128)(2,1)} %collective-permute-done.24.refs_1_.mid_far, bf16[1024,1536]{1,0:T(8,128)(2,1)} %constant_dynamic-update-slice_fusion.8.refs_2_.cot_near, bf16[1024,1536]{1,0:T(8,128)(2,1)} %collective-permute-done.28.refs_3_.cot_far, ...), custom_call_target="tpu_custom_call" | custom-call | flops 1024 | bytes 1024 | tf_op jit(solution)/shard_map/pallas_call | solution.py:310
  358.6 4.9 collective-permute-done.30
  367.5 11.1 %collective-permute-done.31 = bf16[256,1536]{1,0:T(8,128)(2,1)S(1)} collective-permute-done((bf16[256,1536]{1,0:T(8,128)(2,1)S(1)}, bf16[256,1536]{1,0:T(8,128)(2,1)S(1)}, u32[]{:S(2)}, u32[]{:S(2)}) %collective-permute-start.31) | collective-permute-done | bytes 786464 | tf_op jit(solution)/shard_map/ppermute | solution.py:421
  389.6 7.3 %collective-permute-done.44 = bf16[192,1536]{1,0:T(8,128)(2,1)S(1)} collective-permute-done((bf16[192,1536]{1,0:T(8,128)(2,1)S(1)}, bf16[192,1536]{1,0:T(8,128)(2,1)S(1)}, u32[]{:S(2)}, u32[]{:S(2)}) %collective-permute-start.44) | collective-permute-done | bytes 589856 | tf_op jit(solution)/shard_map/ppermute | solution.py:421
  400.3 6.9 %collective-permute-done.43 = bf16[192,1536]{1,0:T(8,128)(2,1)S(1)} collective-permute-done((bf16[192,1536]{1,0:T(8,128)(2,1)S(1)}, bf16[192,1536]{1,0:T(8,128)(2,1)S(1)}, u32[]{:S(2)}, u32[]{:S(2)}) %collective-permute-start.43) | collective-permute-done | bytes 589856 | tf_op jit(solution)/shard_map/ppermute | solution.py:421
  409.9 8.9 %shard_map.176 = (bf16[256,1536]{1,0:T(8,128)(2,1)}, bf16[2048,512]{1,0:T(8,128)(2,1)}) custom-call(s32[8]{0:T(128)} %and_convert_fusion.need_ref, s32[2048,2]{1,0:T(8,128)} %copy.31.kinfo_ref, s32[8,256]{1,0:T(8,128)} %add_add_fusion.qinfo_ref, f32[64,256]{1,0:T(8,128)} %copy-done.28, f32[64,256]{1,0:T(8,128)} %get-tuple-element.127.sin_ref, ...), custom_call_target="tpu_custom_call" | custom-call | flops 1024 | bytes 1024 | tf_op jit(solution)/shard_map/pallas_call | solution.py:191
  421.0 8.4 %collective-permute-start.40 = (bf16[256,512]{1,0:T(8,128)(2,1)}, bf16[256,512]{1,0:T(8,128)(2,1)}, u32[]{:S(2)}, u32[]{:S(2)}) collective-permute-start(bf16[256,512]{1,0:T(8,128)(2,1)} %get-tuple-element.100), channel_id=1, source_target_pairs={{0,2},{1,3},{2,0},{3,1},{4,6},{5,7},{6,4},{7,5},{8,10},{9,11},{10,... | collective-permute-start | bytes 786440 | tf_op jit(solution)/shard_map/ppermute | solution.py:421
  432.6 12.8 %collective-permute-start.41 = (bf16[256,512]{1,0:T(8,128)(2,1)S(1)}, bf16[256,512]{1,0:T(8,128)(2,1)S(1)}, u32[]{:S(2)}, u32[]{:S(2)}) collective-permute-start(bf16[256,512]{1,0:T(8,128)(2,1)S(1)} %get-tuple-element.104), channel_id=1, source_target_pairs={{0,1},{1,0},{2,6},{3,7},{4,5},{5,4},{6,2},{7,3},{8,9},{9,8},{10,14... | collective-permute-start | bytes 786440 | tf_op jit(solution)/shard_map/ppermute | solution.py:421
  445.8 3.9 collective-permute-done.41
  452.5 4.8 collective-permute-done.42
  462.1 3.4 convolution_convert_fusion
  468.5 2.9 collective-permute-done.50
  477.9 6.9 %collective-permute-done.51 = bf16[192,2048]{1,0:T(8,128)(2,1)} collective-permute-done((bf16[192,2048]{1,0:T(8,128)(2,1)}, bf16[192,2048]{1,0:T(8,128)(2,1)}, u32[]{:S(2)}, u32[]{:S(2)}) %collective-permute-start.51) | collective-permute-done | bytes 786464 | tf_op jit(solution)/shard_map/ppermute | solution.py:421
  487.5 6.2 %fusion.12 = (bf16[1536]{0:T(1024)(128)(2,1)S(1)}, f32[256]{0:T(256)S(1)}, f32[256,1536]{1,0:T(8,128)}) fusion(bf16[256,1536]{1,0:T(8,128)(2,1)S(1)} %copy-done.17, f32[256]{0:T(256)S(1)} %copy-done.37, f32[1536]{0:T(1024)S(1)} %copy-done.33, bf16[1536,2176]{1,0:T(8,128)(2,1)} %bitcast.27, bf16[256,256]{1,0:T(8,128)(2,1)S(1)} %copy-done.30, ...), kind=kOutput, calls=%fused_computation.27 | convolution fusion | flops 1616509184 | bytes 9710592 | tf_op jit(solution)/shard_map/dot_general | solution.py:32
  502.8 3.3 add_convert_fusion.6
  506.1 4.0 reduce-scatter.9.cloned.1.call-done
  510.1 3.7 add_convert_fusion
  519.7 4.2 all-to-all-start.1
  526.6 19.2 %all-to-all-done.1 = bf16[8,48,1152]{2,1,0:T(8,128)(2,1)} async-done(((bf16[8,48,1152]{2,1,0:T(8,128)(2,1)}), bf16[8,48,1152]{2,1,0:T(8,128)(2,1)}, u32[]{:S(2)}, u32[]{:S(2)}) %all-to-all-start.1) | async-done | bytes 884768 | tf_op jit(solution)/shard_map/all_to_all | solution.py:516
  545.9 4.7 all-to-all-start.2
  556.9 6.5 %all-to-all-done.2 = bf16[8,48,1152]{2,1,0:T(8,128)(2,1)} async-done(((bf16[8,48,1152]{2,1,0:T(8,128)(2,1)}), bf16[8,48,1152]{2,1,0:T(8,128)(2,1)}, u32[]{:S(2)}, u32[]{:S(2)}) %all-to-all-start.2) | async-done | bytes 884768 | tf_op jit(solution)/shard_map/all_to_all | solution.py:516
  563.4 4.2 all-to-all-start.3
  567.7 3.2 fusion.20
  570.9 10.4 %all-to-all-done.3 = bf16[8,48,1152]{2,1,0:T(8,128)(2,1)} async-done(((bf16[8,48,1152]{2,1,0:T(8,128)(2,1)}), bf16[8,48,1152]{2,1,0:T(8,128)(2,1)}, u32[]{:S(2)}, u32[]{:S(2)}) %all-to-all-start.3) | async-done | bytes 884768 | tf_op jit(solution)/shard_map/all_to_all | solution.py:516
  581.4 4.5 shard_map.177
  (348 shorter events, 173.4 us)
Async XLA Ops:
  23.3 36.9 %all-to-all-start = ((bf16[8,48,3456]{2,1,0:T(8,128)(2,1)}), bf16[8,48,3456]{2,1,0:T(8,128)(2,1)S(1)}, u32[]{:S(2)}, u32[]{:S(2)}) async-start(bf16[8,48,3456]{2,1,0:T(8,128)(2,1)} %bitcast.153), calls=%async_computation | async-start | bytes 5308416 | tf_op jit(solution)/shard_map/all_to_all | solution.py:516
  28.5 39.4 %all-gather.5.cloned.1.call-start = ((), (), s32[]{:S(2)}) async-start(), calls=%async_computation.8 | async-start | bytes 1781760 | tf_op jit(solution)/shard_map/all_gather | solution.py:519
  29.2 199.8 %all-gather.11.cloned.1.call-start = ((), (), s32[]{:S(2)}) async-start(), calls=%async_computation.11 | async-start | bytes 4423680 | tf_op jit(solution)/shard_map/all_gather | solution.py:519
  61.9 208.8 %all-gather.9.cloned.1.call-start = ((), (), s32[]{:S(2)}) async-start(), calls=%async_computation.10 | async-start | bytes 4423680 | tf_op jit(solution)/shard_map/all_gather | solution.py:519
  69.1 18.8 %collective-permute-start = (bf16[192,2176]{1,0:T(8,128)(2,1)S(1)}, bf16[192,2176]{1,0:T(8,128)(2,1)S(1)}, u32[]{:S(2)}, u32[]{:S(2)}) collective-permute-start(bf16[192,2176]{1,0:T(8,128)(2,1)S(1)} %slice.222), channel_id=1, source_target_pairs={{0,4},{1,5},{2,3},{3,2},{4,0},{5,1},{6,7},{7,6},{8,12},{9,13},{10,... | collective-permute-start | bytes 2506760 | tf_op jit(solution)/shard_map/ppermute | solution.py:421
  73.9 22.9 %collective-permute-start.1 = (bf16[192,2176]{1,0:T(8,128)(2,1)S(1)}, bf16[192,2176]{1,0:T(8,128)(2,1)S(1)}, u32[]{:S(2)}, u32[]{:S(2)}) collective-permute-start(bf16[192,2176]{1,0:T(8,128)(2,1)S(1)} %slice.222), channel_id=1, source_target_pairs={{0,1},{1,0},{2,6},{3,7},{4,5},{5,4},{6,2},{7,3},{8,9},{9,8},{10,14... | collective-permute-start | bytes 2506760 | tf_op jit(solution)/shard_map/ppermute | solution.py:421
  78.0 27.1 %collective-permute-start.3 = (bf16[192,2176]{1,0:T(8,128)(2,1)S(1)}, bf16[192,2176]{1,0:T(8,128)(2,1)}, u32[]{:S(2)}, u32[]{:S(2)}) collective-permute-start(bf16[192,2176]{1,0:T(8,128)(2,1)S(1)} %slice.222), channel_id=1, source_target_pairs={{0,2},{1,3},{2,0},{3,1},{4,6},{5,7},{6,4},{7,5},{8,10},{9,11},{10,... | collective-permute-start | bytes 2506760 | tf_op jit(solution)/shard_map/ppermute | solution.py:421
  87.9 13.0 %collective-permute-start.2 = (bf16[192,2176]{1,0:T(8,128)(2,1)S(1)}, bf16[192,2176]{1,0:T(8,128)(2,1)}, u32[]{:S(2)}, u32[]{:S(2)}) collective-permute-start(bf16[192,2176]{1,0:T(8,128)(2,1)S(1)} %collective-permute-done), channel_id=1, source_target_pairs={{0,1},{1,0},{2,6},{3,7},{4,5},{5,4},{6,2},{7,3},{8,9},{9,8},{10,14... | collective-permute-start | bytes 2506760 | tf_op jit(solution)/shard_map/ppermute | solution.py:421
  95.6 212.0 %all-gather.7.cloned.1.call-start = ((), (), s32[]{:S(2)}) async-start(), calls=%async_computation.9 | async-start | bytes 4423680 | tf_op jit(solution)/shard_map/all_gather | solution.py:519
  96.8 11.9 %collective-permute-start.4 = (bf16[192,2176]{1,0:T(8,128)(2,1)S(1)}, bf16[192,2176]{1,0:T(8,128)(2,1)S(1)}, u32[]{:S(2)}, u32[]{:S(2)}) collective-permute-start(bf16[192,2176]{1,0:T(8,128)(2,1)S(1)} %collective-permute-done), channel_id=1, source_target_pairs={{0,2},{1,3},{2,0},{3,1},{4,6},{5,7},{6,4},{7,5},{8,10},{9,11},{10,... | collective-permute-start | bytes 2506760 | tf_op jit(solution)/shard_map/ppermute | solution.py:421
  97.8 12.4 %collective-permute-start.5 = (bf16[192,2176]{1,0:T(8,128)(2,1)S(1)}, bf16[192,2176]{1,0:T(8,128)(2,1)S(1)}, u32[]{:S(2)}, u32[]{:S(2)}) collective-permute-start(bf16[192,2176]{1,0:T(8,128)(2,1)S(1)} %collective-permute-done.1), channel_id=1, source_target_pairs={{0,2},{1,3},{2,0},{3,1},{4,6},{5,7},{6,4},{7,5},{8,10},{9,11},{10,... | collective-permute-start | bytes 2506760 | tf_op jit(solution)/shard_map/ppermute | solution.py:421
  100.9 43.3 %collective-permute-start.17 = (bf16[192,1536]{1,0:T(8,128)(2,1)S(1)}, bf16[192,1536]{1,0:T(8,128)(2,1)}, u32[]{:S(2)}, u32[]{:S(2)}) collective-permute-start(bf16[192,1536]{1,0:T(8,128)(2,1)S(1)} %slice.235), channel_id=1, source_target_pairs={{0,2},{1,3},{2,0},{3,1},{4,6},{5,7},{6,4},{7,5},{8,10},{9,11},{10,... | collective-permute-start | bytes 1769480 | tf_op jit(solution)/shard_map/ppermute | solution.py:421
  100.9 13.1 %collective-permute-start.15 = (bf16[192,1536]{1,0:T(8,128)(2,1)S(1)}, bf16[192,1536]{1,0:T(8,128)(2,1)}, u32[]{:S(2)}, u32[]{:S(2)}) collective-permute-start(bf16[192,1536]{1,0:T(8,128)(2,1)S(1)} %slice.235), channel_id=1, source_target_pairs={{0,1},{1,0},{2,6},{3,7},{4,5},{5,4},{6,2},{7,3},{8,9},{9,8},{10,14... | collective-permute-start | bytes 1769480 | tf_op jit(solution)/shard_map/ppermute | solution.py:421
  108.7 12.4 %collective-permute-start.6 = (bf16[192,2176]{1,0:T(8,128)(2,1)}, bf16[192,2176]{1,0:T(8,128)(2,1)S(1)}, u32[]{:S(2)}, u32[]{:S(2)}) collective-permute-start(bf16[192,2176]{1,0:T(8,128)(2,1)} %collective-permute-done.2), channel_id=1, source_target_pairs={{0,2},{1,3},{2,0},{3,1},{4,6},{5,7},{6,4},{7,5},{8,10},{9,11},{10,... | collective-permute-start | bytes 2506760 | tf_op jit(solution)/shard_map/ppermute | solution.py:421
  114.0 35.3 %collective-permute-start.19 = (bf16[192,1536]{1,0:T(8,128)(2,1)}, bf16[192,1536]{1,0:T(8,128)(2,1)}, u32[]{:S(2)}, u32[]{:S(2)}) collective-permute-start(bf16[192,1536]{1,0:T(8,128)(2,1)} %collective-permute-done.15), channel_id=1, source_target_pairs={{0,2},{1,3},{2,0},{3,1},{4,6},{5,7},{6,4},{7,5},{8,10},{9,11},{10,... | collective-permute-start | bytes 1769480 | tf_op jit(solution)/shard_map/ppermute | solution.py:421
  116.7 25.2 %collective-permute-start.16 = (bf16[192,1536]{1,0:T(8,128)(2,1)}, bf16[192,1536]{1,0:T(8,128)(2,1)}, u32[]{:S(2)}, u32[]{:S(2)}) collective-permute-start(bf16[192,1536]{1,0:T(8,128)(2,1)} %collective-permute-done.14), channel_id=1, source_target_pairs={{0,1},{1,0},{2,6},{3,7},{4,5},{5,4},{6,2},{7,3},{8,9},{9,8},{10,14... | collective-permute-start | bytes 1769480 | tf_op jit(solution)/shard_map/ppermute | solution.py:421
  140.6 12.3 %collective-permute-start.10 = (bf16[256,512]{1,0:T(8,128)(2,1)}, bf16[256,512]{1,0:T(8,128)(2,1)S(1)}, u32[]{:S(2)}, u32[]{:S(2)}) collective-permute-start(bf16[256,512]{1,0:T(8,128)(2,1)} %get-tuple-element.115), channel_id=1, source_target_pairs={{0,2},{1,3},{2,0},{3,1},{4,6},{5,7},{6,4},{7,5},{8,10},{9,11},{10,... | collective-permute-start | bytes 786440 | tf_op jit(solution)/shard_map/ppermute | solution.py:421
  151.2 16.3 %collective-permute-start.20 = (bf16[192,1536]{1,0:T(8,128)(2,1)}, bf16[192,1536]{1,0:T(8,128)(2,1)S(1)}, u32[]{:S(2)}, u32[]{:S(2)}) collective-permute-start(bf16[192,1536]{1,0:T(8,128)(2,1)} %collective-permute-done.16), channel_id=1, source_target_pairs={{0,2},{1,3},{2,0},{3,1},{4,6},{5,7},{6,4},{7,5},{8,10},{9,11},{10,... | collective-permute-start | bytes 1769480 | tf_op jit(solution)/shard_map/ppermute | solution.py:421
  162.8 15.0 %collective-permute-start.25 = (bf16[256,1536]{1,0:T(8,128)(2,1)}, bf16[256,1536]{1,0:T(8,128)(2,1)}, u32[]{:S(2)}, u32[]{:S(2)}) collective-permute-start(bf16[256,1536]{1,0:T(8,128)(2,1)} %param.21), channel_id=1, source_target_pairs={{0,4},{1,5},{2,3},{3,2},{4,0},{5,1},{6,7},{7,6},{8,12},{9,13},{10,... | collective-permute-start | bytes 2359304 | tf_op jit(solution)/shard_map/ppermute | solution.py:421
  172.3 13.9 %collective-permute-start.21 = (bf16[256,1536]{1,0:T(8,128)(2,1)S(1)}, bf16[256,1536]{1,0:T(8,128)(2,1)S(1)}, u32[]{:S(2)}, u32[]{:S(2)}) collective-permute-start(bf16[256,1536]{1,0:T(8,128)(2,1)S(1)} %multiply_convert_fusion), channel_id=1, source_target_pairs={{0,4},{1,5},{2,3},{3,2},{4,0},{5,1},{6,7},{7,6},{8,12},{9,13},{10,... | collective-permute-start | bytes 2359304 | tf_op jit(solution)/shard_map/ppermute | solution.py:421
  172.4 207.6 %reduce-scatter.5.cloned.1.call-start = ((), (), s32[]{:S(2)}) async-start(), calls=%async_computation.12 | async-start | bytes 4423680 | tf_op jit(solution)/shard_map/reduce_scatter | solution.py:522
  172.8 19.1 %collective-permute-start.26 = (bf16[256,1536]{1,0:T(8,128)(2,1)S(1)}, bf16[256,1536]{1,0:T(8,128)(2,1)S(1)}, u32[]{:S(2)}, u32[]{:S(2)}) collective-permute-start(bf16[256,1536]{1,0:T(8,128)(2,1)S(1)} %copy-done.21), channel_id=1, source_target_pairs={{0,1},{1,0},{2,6},{3,7},{4,5},{5,4},{6,2},{7,3},{8,9},{9,8},{10,14... | collective-permute-start | bytes 2359304 | tf_op jit(solution)/shard_map/ppermute | solution.py:421
  177.8 27.0 %collective-permute-start.27 = (bf16[256,1536]{1,0:T(8,128)(2,1)}, bf16[256,1536]{1,0:T(8,128)(2,1)S(1)}, u32[]{:S(2)}, u32[]{:S(2)}) collective-permute-start(bf16[256,1536]{1,0:T(8,128)(2,1)} %collective-permute-done.25), channel_id=1, source_target_pairs={{0,1},{1,0},{2,6},{3,7},{4,5},{5,4},{6,2},{7,3},{8,9},{9,8},{10,14... | collective-permute-start | bytes 2359304 | tf_op jit(solution)/shard_map/ppermute | solution.py:421
  180.6 41.6 %collective-permute-start.22 = (bf16[256,1536]{1,0:T(8,128)(2,1)S(1)}, bf16[256,1536]{1,0:T(8,128)(2,1)S(1)}, u32[]{:S(2)}, u32[]{:S(2)}) collective-permute-start(bf16[256,1536]{1,0:T(8,128)(2,1)S(1)} %multiply_convert_fusion), channel_id=1, source_target_pairs={{0,1},{1,0},{2,6},{3,7},{4,5},{5,4},{6,2},{7,3},{8,9},{9,8},{10,14... | collective-permute-start | bytes 2359304 | tf_op jit(solution)/shard_map/ppermute | solution.py:421
  186.1 41.6 %collective-permute-start.23 = (bf16[256,1536]{1,0:T(8,128)(2,1)S(1)}, bf16[256,1536]{1,0:T(8,128)(2,1)S(1)}, u32[]{:S(2)}, u32[]{:S(2)}) collective-permute-start(bf16[256,1536]{1,0:T(8,128)(2,1)S(1)} %collective-permute-done.21), channel_id=1, source_target_pairs={{0,1},{1,0},{2,6},{3,7},{4,5},{5,4},{6,2},{7,3},{8,9},{9,8},{10,14... | collective-permute-start | bytes 2359304 | tf_op jit(solution)/shard_map/ppermute | solution.py:421
  205.7 23.3 %collective-permute-start.28 = (bf16[1024,1536]{1,0:T(8,128)(2,1)}, bf16[1024,1536]{1,0:T(8,128)(2,1)}, u32[]{:S(2)}, u32[]{:S(2)}) collective-permute-start(bf16[1024,1536]{1,0:T(8,128)(2,1)} %constant_dynamic-update-slice_fusion.8.refs_2_.cot_near), channel_id=1, source_target_pairs={{0,2},{1,3},{2,0},{3,1},{4,6},{5,7},{6,4},{7,5},{8,10},{9,11},{10,... | collective-permute-start | bytes 9437192 | tf_op jit(solution)/shard_map/ppermute | solution.py:421
  270.6 235.5 %reduce-scatter.7.cloned.1.call-start = ((), (), s32[]{:S(2)}) async-start(), calls=%async_computation.13 | async-start | bytes 4423680 | tf_op jit(solution)/shard_map/reduce_scatter | solution.py:522
  342.9 20.6 %collective-permute-start.30 = (bf16[512,1536]{1,0:T(8,128)(2,1)S(1)}, bf16[512,1536]{1,0:T(8,128)(2,1)}, u32[]{:S(2)}, u32[]{:S(2)}) collective-permute-start(bf16[512,1536]{1,0:T(8,128)(2,1)S(1)} %get-tuple-element.95), channel_id=1, source_target_pairs={{0,1},{1,0},{2,6},{3,7},{4,5},{5,4},{6,2},{7,3},{8,9},{9,8},{10,14... | collective-permute-start | bytes 4718600 | tf_op jit(solution)/shard_map/ppermute | solution.py:421
  366.6 12.1 %collective-permute-start.31 = (bf16[256,1536]{1,0:T(8,128)(2,1)S(1)}, bf16[256,1536]{1,0:T(8,128)(2,1)S(1)}, u32[]{:S(2)}, u32[]{:S(2)}) collective-permute-start(bf16[256,1536]{1,0:T(8,128)(2,1)S(1)} %slice.243), channel_id=1, source_target_pairs={{0,4},{1,5},{2,3},{3,2},{4,0},{5,1},{6,7},{7,6},{8,12},{9,13},{10,... | collective-permute-start | bytes 2359304 | tf_op jit(solution)/shard_map/ppermute | solution.py:421
  367.3 142.8 %reduce-scatter.9.cloned.1.call-start = ((), (), s32[]{:S(2)}) async-start(), calls=%async_computation.14 | async-start | bytes 4423680 | tf_op jit(solution)/shard_map/reduce_scatter | solution.py:522
  389.0 18.2 %collective-permute-start.43 = (bf16[192,1536]{1,0:T(8,128)(2,1)S(1)}, bf16[192,1536]{1,0:T(8,128)(2,1)S(1)}, u32[]{:S(2)}, u32[]{:S(2)}) collective-permute-start(bf16[192,1536]{1,0:T(8,128)(2,1)S(1)} %fusion.31), channel_id=1, source_target_pairs={{0,1},{1,0},{2,6},{3,7},{4,5},{5,4},{6,2},{7,3},{8,9},{9,8},{10,14... | collective-permute-start | bytes 1769480 | tf_op jit(solution)/shard_map/ppermute | solution.py:421
  429.4 16.4 %collective-permute-start.39 = (bf16[256,512]{1,0:T(8,128)(2,1)}, bf16[256,512]{1,0:T(8,128)(2,1)S(1)}, u32[]{:S(2)}, u32[]{:S(2)}) collective-permute-start(bf16[256,512]{1,0:T(8,128)(2,1)} %get-tuple-element.101), channel_id=1, source_target_pairs={{0,2},{1,3},{2,0},{3,1},{4,6},{5,7},{6,4},{7,5},{8,10},{9,11},{10,... | collective-permute-start | bytes 786440 | tf_op jit(solution)/shard_map/ppermute | solution.py:421
  432.6 17.1 %collective-permute-start.41 = (bf16[256,512]{1,0:T(8,128)(2,1)S(1)}, bf16[256,512]{1,0:T(8,128)(2,1)S(1)}, u32[]{:S(2)}, u32[]{:S(2)}) collective-permute-start(bf16[256,512]{1,0:T(8,128)(2,1)S(1)} %get-tuple-element.104), channel_id=1, source_target_pairs={{0,1},{1,0},{2,6},{3,7},{4,5},{5,4},{6,2},{7,3},{8,9},{9,8},{10,14... | collective-permute-start | bytes 786440 | tf_op jit(solution)/shard_map/ppermute | solution.py:421
  472.5 12.3 %collective-permute-start.51 = (bf16[192,2048]{1,0:T(8,128)(2,1)}, bf16[192,2048]{1,0:T(8,128)(2,1)}, u32[]{:S(2)}, u32[]{:S(2)}) collective-permute-start(bf16[192,2048]{1,0:T(8,128)(2,1)} %fusion.23), channel_id=1, source_target_pairs={{0,1},{1,0},{2,6},{3,7},{4,5},{5,4},{6,2},{7,3},{8,9},{9,8},{10,14... | collective-permute-start | bytes 2359304 | tf_op jit(solution)/shard_map/ppermute | solution.py:421
  474.5 35.6 %collective-permute-start.53 = (bf16[1024,1536]{1,0:T(8,128)(2,1)}, bf16[1024,1536]{1,0:T(8,128)(2,1)}, u32[]{:S(2)}, u32[]{:S(2)}) collective-permute-start(bf16[1024,1536]{1,0:T(8,128)(2,1)} %get-tuple-element.65), channel_id=1, source_target_pairs={{0,2},{1,3},{2,0},{3,1},{4,6},{5,7},{6,4},{7,5},{8,10},{9,11},{10,... | collective-permute-start | bytes 9437192 | tf_op jit(solution)/shard_map/ppermute | solution.py:421
  474.7 24.0 %collective-permute-start.46 = (bf16[192,2048]{1,0:T(8,128)(2,1)}, bf16[192,2048]{1,0:T(8,128)(2,1)}, u32[]{:S(2)}, u32[]{:S(2)}) collective-permute-start(bf16[192,2048]{1,0:T(8,128)(2,1)} %bitcast.175), channel_id=1, source_target_pairs={{0,2},{1,3},{2,0},{3,1},{4,6},{5,7},{6,4},{7,5},{8,10},{9,11},{10,... | collective-permute-start | bytes 2359304 | tf_op jit(solution)/shard_map/ppermute | solution.py:421
  477.8 21.2 %collective-permute-start.48 = (bf16[192,2048]{1,0:T(8,128)(2,1)}, bf16[192,2048]{1,0:T(8,128)(2,1)}, u32[]{:S(2)}, u32[]{:S(2)}) collective-permute-start(bf16[192,2048]{1,0:T(8,128)(2,1)} %fusion.25), channel_id=1, source_target_pairs={{0,1},{1,0},{2,6},{3,7},{4,5},{5,4},{6,2},{7,3},{8,9},{9,8},{10,14... | collective-permute-start | bytes 2359304 | tf_op jit(solution)/shard_map/ppermute | solution.py:421
  487.4 13.4 %collective-permute-start.52 = (bf16[192,2048]{1,0:T(8,128)(2,1)}, bf16[192,2048]{1,0:T(8,128)(2,1)}, u32[]{:S(2)}, u32[]{:S(2)}) collective-permute-start(bf16[192,2048]{1,0:T(8,128)(2,1)} %add_convert_fusion.7), channel_id=1, source_target_pairs={{0,4},{1,5},{2,3},{3,2},{4,0},{5,1},{6,7},{7,6},{8,12},{9,13},{10,... | collective-permute-start | bytes 2359304 | tf_op jit(solution)/shard_map/ppermute | solution.py:421
  498.3 25.7 %collective-permute-start.56 = (bf16[32,128]{1,0:T(8,128)(2,1)S(1)}, bf16[32,128]{1,0:T(8,128)(2,1)S(1)}, u32[]{:S(2)}, u32[]{:S(2)}) collective-permute-start(bf16[32,128]{1,0:T(8,128)(2,1)S(1)} %get-tuple-element.117), channel_id=1, source_target_pairs={{0,2},{1,3},{2,0},{3,1},{4,6},{5,7},{6,4},{7,5},{8,10},{9,11},{10,... | collective-permute-start | bytes 24584 | tf_op jit(solution)/shard_map/ppermute | solution.py:421
  498.7 19.4 %collective-permute-start.59 = (bf16[32,128]{1,0:T(8,128)(2,1)S(1)}, bf16[32,128]{1,0:T(8,128)(2,1)S(1)}, u32[]{:S(2)}, u32[]{:S(2)}) collective-permute-start(bf16[32,128]{1,0:T(8,128)(2,1)S(1)} %get-tuple-element.119), channel_id=1, source_target_pairs={{0,2},{1,3},{2,0},{3,1},{4,6},{5,7},{6,4},{7,5},{8,10},{9,11},{10,... | collective-permute-start | bytes 24584 | tf_op jit(solution)/shard_map/ppermute | solution.py:421
  498.9 25.1 %collective-permute-start.58 = (bf16[32,128]{1,0:T(8,128)(2,1)S(1)}, bf16[32,128]{1,0:T(8,128)(2,1)S(1)}, u32[]{:S(2)}, u32[]{:S(2)}) collective-permute-start(bf16[32,128]{1,0:T(8,128)(2,1)S(1)} %get-tuple-element.121), channel_id=1, source_target_pairs={{0,1},{1,0},{2,6},{3,7},{4,5},{5,4},{6,2},{7,3},{8,9},{9,8},{10,14... | collective-permute-start | bytes 24584 | tf_op jit(solution)/shard_map/ppermute | solution.py:421
  500.8 17.3 %collective-permute-start.61 = (bf16[32,128]{1,0:T(8,128)(2,1)S(1)}, bf16[32,128]{1,0:T(8,128)(2,1)S(1)}, u32[]{:S(2)}, u32[]{:S(2)}) collective-permute-start(bf16[32,128]{1,0:T(8,128)(2,1)S(1)} %get-tuple-element.122), channel_id=1, source_target_pairs={{0,1},{1,0},{2,6},{3,7},{4,5},{5,4},{6,2},{7,3},{8,9},{9,8},{10,14... | collective-permute-start | bytes 24584 | tf_op jit(solution)/shard_map/ppermute | solution.py:421
  516.7 33.9 %collective-permute-start.54 = (bf16[512,1536]{1,0:T(8,128)(2,1)}, bf16[512,1536]{1,0:T(8,128)(2,1)}, u32[]{:S(2)}, u32[]{:S(2)}) collective-permute-start(bf16[512,1536]{1,0:T(8,128)(2,1)} %slice.247), channel_id=1, source_target_pairs={{0,1},{1,0},{2,6},{3,7},{4,5},{5,4},{6,2},{7,3},{8,9},{9,8},{10,14... | collective-permute-start | bytes 4718600 | tf_op jit(solution)/shard_map/ppermute | solution.py:421
  519.7 26.2 %all-to-all-start.1 = ((bf16[8,48,1152]{2,1,0:T(8,128)(2,1)}), bf16[8,48,1152]{2,1,0:T(8,128)(2,1)}, u32[]{:S(2)}, u32[]{:S(2)}) async-start(bf16[8,48,1152]{2,1,0:T(8,128)(2,1)} %bitcast.167), calls=%async_computation.5 | async-start | bytes 1769472 | tf_op jit(solution)/shard_map/all_to_all | solution.py:516
  523.9 64.2 %reduce-scatter.11.cloned.1.call-start = ((), (), s32[]{:S(2)}) async-start(), calls=%async_computation.15 | async-start | bytes 1781760 | tf_op jit(solution)/shard_map/reduce_scatter | solution.py:522
  545.9 17.6 %all-to-all-start.2 = ((bf16[8,48,1152]{2,1,0:T(8,128)(2,1)}), bf16[8,48,1152]{2,1,0:T(8,128)(2,1)}, u32[]{:S(2)}, u32[]{:S(2)}) async-start(bf16[8,48,1152]{2,1,0:T(8,128)(2,1)} %bitcast.168), calls=%async_computation.6 | async-start | bytes 1769472 | tf_op jit(solution)/shard_map/all_to_all | solution.py:516
  554.9 30.9 %collective-permute-start.55 = (bf16[256,1536]{1,0:T(8,128)(2,1)}, bf16[256,1536]{1,0:T(8,128)(2,1)}, u32[]{:S(2)}, u32[]{:S(2)}) collective-permute-start(bf16[256,1536]{1,0:T(8,128)(2,1)} %slice.249), channel_id=1, source_target_pairs={{0,4},{1,5},{2,3},{3,2},{4,0},{5,1},{6,7},{7,6},{8,12},{9,13},{10,... | collective-permute-start | bytes 2359304 | tf_op jit(solution)/shard_map/ppermute | solution.py:421
  563.4 17.9 %all-to-all-start.3 = ((bf16[8,48,1152]{2,1,0:T(8,128)(2,1)}), bf16[8,48,1152]{2,1,0:T(8,128)(2,1)}, u32[]{:S(2)}, u32[]{:S(2)}) async-start(bf16[8,48,1152]{2,1,0:T(8,128)(2,1)} %bitcast.169), calls=%async_computation.7 | async-start | bytes 1769472 | tf_op jit(solution)/shard_map/all_to_all | solution.py:516
  (68 other events, 694.5 us)
Sparse Core Ops, SparseCore 0:
  31.4 36.3 all-gather.4
  69.4 68.8 all-gather.10
  139.9 68.5 all-gather.8
  209.9 68.5 all-gather.6
  280.7 64.9 reduce-scatter.4
  367.4 70.1 reduce-scatter.6
  439.9 70.0 reduce-scatter.8
  527.1 33.8 reduce-scatter.10

commit v3 on v2

--- a/solution.py
+++ b/solution.py
@@ -98,7 +98,8 @@
     do_ref,
     lse_ref,
     dq_ref,
-    dkv_ref,
+    near_ref,
+    far_ref,
     dots_ref,
     acc_ref,
     bias_ref,
@@ -115,12 +116,14 @@
         )
     acc_ref[...] = jnp.zeros(acc_ref.shape, F32)
 
-    def one_block(block, carry):
+    def one_block(dkv_ref, first, at, carry):
+        block = first + at
         rows = pl.ds(pl.multiple_of(block * TOK_DEV, TOK_DEV), TOK_DEV)
+        out_rows = pl.ds(pl.multiple_of(at * TOK_DEV, TOK_DEV), TOK_DEV)
 
         @pl.when(need_ref[block] == 0)
         def _():
-            dkv_ref[rows, :] = jnp.zeros((TOK_DEV, 2 * KV_HEADS * HEAD), BF16)
+            dkv_ref[out_rows, :] = jnp.zeros((TOK_DEV, 2 * KV_HEADS * HEAD), BF16)
 
         @pl.when(need_ref[block] > 0)
         def _():
@@ -143,12 +146,14 @@
                     acc_ref[span, :] += dot(key_t, score_grad, 1, 0)
                     key_grad += dot(score_grad, query, 1, 1)
                     value_grad += dot(probs.astype(BF16), grad, 1, 1)
-                dkv_ref[rows, key_cols] = (key_grad * SCALE).astype(BF16)
-                dkv_ref[rows, value_cols] = value_grad.astype(BF16)
+                dkv_ref[out_rows, key_cols] = (key_grad * SCALE).astype(BF16)
+                dkv_ref[out_rows, value_cols] = value_grad.astype(BF16)
 
         return carry
 
-    lax.fori_loop(0, blocks, one_block, 0)
+    half_blocks = blocks // 2
+    lax.fori_loop(0, half_blocks, functools.partial(one_block, near_ref, 0), 0)
+    lax.fori_loop(0, half_blocks, functools.partial(one_block, far_ref, half_blocks), 0)
     cosine, sine = cos_ref[...], sin_ref[...]
     half = HEAD // 2
     for head in range(HEADS):
@@ -192,10 +197,11 @@
         attn_bwd_kernel,
         out_shape=(
             jax.ShapeDtypeStruct((rows, HEADS * HEAD), BF16),
-            jax.ShapeDtypeStruct(kv_all.shape, BF16),
+            jax.ShapeDtypeStruct((kv_all.shape[0] // 2, kv_all.shape[1]), BF16),
+            jax.ShapeDtypeStruct((kv_all.shape[0] // 2, kv_all.shape[1]), BF16),
         ),
         in_specs=[pl.BlockSpec(memory_space=pltpu.SMEM)] + vmem_specs(9),
-        out_specs=tuple(vmem_specs(2)),
+        out_specs=tuple(vmem_specs(3)),
         scratch_shapes=[
             pltpu.VMEM((16, rows), F32),
             pltpu.VMEM((HEADS * HEAD, rows), F32),
@@ -207,21 +213,7 @@
     )(need, kinfo, qinfo, cos_t, sin_t, query_t, kv_all, out_t, grad_t, lse)
 
 
-def ffn_kernel(cols, first, with_grad, *refs):
-    mid_near, mid_far, cot_near, cot_far, w_ref = refs[:5]
-    refs = refs[5:]
-    if not first:
-        mid_sums, out_sums = refs[:2], refs[2:4]
-        refs = refs[4:]
-    mid_outs, out_outs = refs[:2], refs[2:4]
-    if with_grad:
-        grad_ref, act_ref, acc_ref, mid_ref, cot_ref = refs[4:]
-    else:
-        act_ref, mid_ref, cot_ref = refs[4:]
-    step, last = pl.program_id(0), pl.num_programs(0) - 1
-    near = step < pl.num_programs(0) // 2
-    mid_ref[...] = jnp.where(near, mid_near[...], mid_far[...])
-    cot_ref[...] = jnp.where(near, cot_near[...], cot_far[...])
+def ffn_tile(cols, mid_ref, cot_ref, w_ref, sums, outs, act_ref, acc_ref):
     both = dot(mid_ref[...], w_ref[:, : 2 * cols], 1, 0)
     hidden_grad = dot(cot_ref[...], w_ref[:, 2 * cols :], 1, 0)
     gate, up = both[:, :cols], both[:, cols:]
@@ -232,31 +224,44 @@
     act_ref[:, 2 * cols :] = (acted * up).astype(BF16)
     mid_grad = dot(act_ref[:, : 2 * cols], w_ref[:, : 2 * cols], 1, 1)
     out = dot(act_ref[:, 2 * cols :], w_ref[:, 2 * cols :], 1, 1)
+    if sums:
+        mid_grad = mid_grad + sums[0][...].astype(F32)
+        out = out + sums[1][...].astype(F32)
+    outs[0][...] = mid_grad.astype(BF16)
+    outs[1][...] = out.astype(BF16)
+    if acc_ref is not None:
+        acc_ref[:, : 2 * cols] += dot(mid_ref[...], act_ref[:, : 2 * cols], 0, 0)
+        acc_ref[:, 2 * cols :] += dot(cot_ref[...], act_ref[:, 2 * cols :], 0, 0)
+
+
+def ffn_kernel(cols, first, with_grad, *refs):
+    mids, cots, w_ref, refs = refs[:2], refs[2:4], refs[4], refs[5:]
+    mid_sums = out_sums = None
     if not first:
-        mid_grad = mid_grad + jnp.where(near, mid_sums[0][...], mid_sums[1][...]).astype(F32)
-        out = out + jnp.where(near, out_sums[0][...], out_sums[1][...]).astype(F32)
-
-    @pl.when(near)
-    def _():
-        mid_outs[0][...] = mid_grad.astype(BF16)
-        out_outs[0][...] = out.astype(BF16)
-
-    @pl.when(jnp.logical_not(near))
-    def _():
-        mid_outs[1][...] = mid_grad.astype(BF16)
-        out_outs[1][...] = out.astype(BF16)
+        mid_sums, out_sums, refs = refs[:2], refs[2:4], refs[4:]
+    mid_outs, out_outs, refs = refs[:2], refs[2:4], refs[4:]
+    if with_grad:
+        grad_ref, act_ref, acc_ref = refs
+    else:
+        (act_ref,), acc_ref = refs, None
+    step, last = pl.program_id(0), pl.num_programs(0) - 1
+    near = step < pl.num_programs(0) // 2
 
     if with_grad:
 
         @pl.when(step == 0)
         def _():
-            acc_ref[:, : 2 * cols] = dot(mid_ref[...], act_ref[:, : 2 * cols], 0, 0)
-            acc_ref[:, 2 * cols :] = dot(cot_ref[...], act_ref[:, 2 * cols :], 0, 0)
-
-        @pl.when(step > 0)
-        def _():
-            acc_ref[:, : 2 * cols] += dot(mid_ref[...], act_ref[:, : 2 * cols], 0, 0)
-            acc_ref[:, 2 * cols :] += dot(cot_ref[...], act_ref[:, 2 * cols :], 0, 0)
+            acc_ref[...] = jnp.zeros(acc_ref.shape, F32)
+
+    def tile(which):
+        sums = () if first else (mid_sums[which], out_sums[which])
+        outs = (mid_outs[which], out_outs[which])
+        ffn_tile(cols, mids[which], cots[which], w_ref, sums, outs, act_ref, acc_ref)
+
+    pl.when(near)(lambda: tile(0))
+    pl.when(jnp.logical_not(near))(lambda: tile(1))
+
+    if with_grad:
 
         @pl.when(step == last)
         def _():
@@ -272,7 +277,6 @@
     act_spec = pl.BlockSpec((TOK_DEV, 3 * cols), lambda i: (i, 0))
     once = pl.BlockSpec(weights.shape, lambda i: (0, 0), pipeline_mode=pl.Buffered(1))
     row_shape = jax.ShapeDtypeStruct((half_tokens, width), BF16)
-    row_scratch = [pltpu.VMEM((TOK_DEV, width), BF16)] * 2
     if with_grad:
         last_shape, last_spec = jax.ShapeDtypeStruct(weights.shape, BF16), once
         scratch = [pltpu.VMEM((TOK_DEV, 3 * cols), BF16), pltpu.VMEM(weights.shape, F32)]
@@ -285,7 +289,7 @@
         out_shape=(row_shape,) * 4 + (last_shape,),
         in_specs=[near_spec, far_spec] * 2 + [once] + [near_spec, far_spec] * (len(sums) // 2),
         out_specs=(near_spec, far_spec) * 2 + (last_spec,),
-        scratch_shapes=scratch + row_scratch,
+        scratch_shapes=scratch,
         compiler_params=pltpu.CompilerParams(vmem_limit_bytes=VMEM_LIMIT),
         cost_estimate=SMALL,
     )(*mid_halves, *cot_halves, weights, *sums)
@@ -338,14 +342,12 @@
             out_ref[there, at + real : at + cols] = jnp.zeros((rows, cols - real), BF16)
 
 
-def unpack_kernel(moves, cols, *refs):
-    chunk_refs, out_ref = refs[:-1], refs[-1]
+def unpack_kernel(moves, cols, in_ref, out_ref):
     rows = out_ref.shape[0]
     for device, chunk, kind, source, real in moves:
         if real:
-            block = chunk_refs[chunk][
-                device * rows : (device + 1) * rows, kind * cols : kind * cols + real
-            ]
+            at = (chunk * 3 + kind) * cols
+            block = in_ref[device * rows : (device + 1) * rows, at : at + real]
             out_ref[:, source : source + real] = block.astype(F32)
 
 
@@ -368,21 +370,86 @@
     )(w_mlp)
 
 
-def unpack_slices(chunk_arrays, rows, total, n_plane, cols):
-    chunks = len(chunk_arrays)
+def unpack_slices(array, rows, total, n_plane, chunks, cols):
     if rows % 16:
-        stacked = jnp.stack(chunk_arrays, axis=0).reshape(chunks, n_plane, rows, 3, cols)
-        stacked = stacked.transpose(2, 3, 1, 0, 4).reshape(rows, 3, -1)[:, :, :total]
-        return stacked.reshape(rows, 3 * total).astype(F32)
+        stacked = array.reshape(n_plane, rows, chunks, 3, cols).transpose(1, 3, 0, 2, 4)
+        return stacked.reshape(rows, 3, -1)[:, :, :total].reshape(rows, 3 * total).astype(F32)
     moves = list(slice_moves(n_plane, chunks, cols, total))
     return pl.pallas_call(
         functools.partial(unpack_kernel, moves, cols),
         out_shape=jax.ShapeDtypeStruct((rows, 3 * total), F32),
-        in_specs=vmem_specs(chunks),
+        in_specs=vmem_specs(1),
         out_specs=vmem_specs(1)[0],
         compiler_params=pltpu.CompilerParams(vmem_limit_bytes=VMEM_LIMIT),
         cost_estimate=SMALL,
-    )(*chunk_arrays)
+    )(array)
+
+
+def weight_grad_kernel(n_dp, local_rows, across, dev_ref, *refs):
+    count = len(across)
+    lefts, rights = refs[: 2 * count : 2], refs[1 : 2 * count : 2]
+    sides, (near_ref, far_ref, turned_ref, block_ref) = refs[2 * count : -4], refs[-4:]
+    half = near_ref.shape[0] // (n_dp * local_rows)
+    tile = block_ref.shape[1]
+
+    def move(from_ref, at):
+        cols = slice(at, at + from_ref.shape[1])
+        for slot in range(2 * half):
+            out_ref = near_ref if slot < half else far_ref
+            for zone in range(n_dp):
+                source = (zone * 2 * half + dev_ref[slot]) * local_rows
+                source = pl.ds(pl.multiple_of(source, local_rows), local_rows)
+                there = ((slot % half) * n_dp + zone) * local_rows
+                out_ref[there : there + local_rows, cols] = from_ref[source, :]
+
+    at = 0
+    for left, right, is_across in zip(lefts, rights, across):
+        turned_ref[...] = left[...].T
+        cols = right.shape[0] if is_across else right.shape[1]
+        for start in range(0, cols, tile):
+            span = slice(start, start + tile)
+            if is_across:
+                block = dot(turned_ref[...], right[span, :], 1, 1)
+            else:
+                block = dot(turned_ref[...], right[:, span], 1, 0)
+            block_ref[...] = block.astype(BF16)
+            move(block_ref, at)
+            at += tile
+    for side_ref in sides:
+        move(side_ref, at)
+
+
+def weight_grads(plane, local_rows, terms, side=None):
+    n_dp = lax.axis_size("dp")
+    tokens, width = terms[0][0].shape
+    widths = [right.shape[0 if across else 1] for _, right, across in terms]
+    if local_rows % 16:
+        full = jnp.concatenate(
+            [dot(left, right, 0, 1 if across else 0) for left, right, across in terms], axis=1
+        ).astype(BF16)
+        if side is not None:
+            full = jnp.concatenate([full, side], axis=1)
+        full = full.reshape(n_dp, plane.count, local_rows, full.shape[1])
+        blocks = [
+            lax.dynamic_slice_in_dim(full, device, 1, 1).reshape(n_dp * local_rows, -1)
+            for device in plane.devices
+        ]
+        half = plane.count // 2
+        return jnp.concatenate(blocks[:half]), jnp.concatenate(blocks[half:])
+    tile = 512
+    extra = [] if side is None else [side]
+    total = sum(widths) + sum(array.shape[1] for array in extra)
+    shape = jax.ShapeDtypeStruct((width // 2, total), BF16)
+    return pl.pallas_call(
+        functools.partial(weight_grad_kernel, n_dp, local_rows, [term[2] for term in terms]),
+        out_shape=(shape, shape),
+        in_specs=[pl.BlockSpec(memory_space=pltpu.SMEM)]
+        + vmem_specs(2 * len(terms) + len(extra)),
+        out_specs=tuple(vmem_specs(2)),
+        scratch_shapes=[pltpu.VMEM((width, tokens), BF16), pltpu.VMEM((width, tile), BF16)],
+        compiler_params=pltpu.CompilerParams(vmem_limit_bytes=VMEM_LIMIT),
+        cost_estimate=SMALL,
+    )(jnp.stack(plane.devices), *[array for term in terms for array in term[:2]], *extra)
 
 
 def after(array, *others):
@@ -420,18 +487,16 @@
             pairs.append((i, i ^ bit))
         return lax.ppermute(array, PLANE, pairs)
 
-    def gather_step(self, held, step):
-        return held + [self.swap(piece, step) for piece in held]
-
-    def gather(self, rows):
-        held = [rows]
-        for step in range(self.steps + 1):
-            held = self.gather_step(held, step)
-        return held
-
-    def gather_halves(self, held):
-        near = jnp.concatenate(held, axis=0)
-        return near, self.swap(near, self.steps)
+    def widen(self, rows, step):
+        return jnp.concatenate([rows, self.swap(rows, step)], axis=0)
+
+    def gather(self, rows, late_step=None, *others):
+        stages = [rows]
+        for step in range(self.steps):
+            if step == late_step:
+                stages[-1] = after(stages[-1], *others)
+            stages.append(self.widen(stages[-1], step))
+        return stages + [self.swap(stages[-1], self.steps)]
 
     def fold(self, near, far, step):
         return (near.astype(F32) + self.swap(far, step).astype(F32)).astype(BF16)
@@ -439,19 +504,6 @@
     def fold_rest(self, rows, step):
         half = rows.shape[0] // 2
         return self.fold(rows[:half], rows[half:], step)
-
-    def reduce_step(self, held, step):
-        kept = len(held) // 2
-        moved = [self.swap(piece, step) for piece in held[kept:]]
-        return [
-            (one.astype(F32) + other.astype(F32)).astype(BF16) for one, other in zip(held, moved)
-        ]
-
-    def reduce(self, blocks):
-        held = list(blocks)
-        for step in range(self.steps, -1, -1):
-            held = self.reduce_step(held, step)
-        return held[0]
 
 
 def place_info(spans, row_in_span, length_row):
@@ -500,7 +552,6 @@
     n_plane = lax.axis_size("ctx") * lax.axis_size("uly")
     n_all = n_dp * n_plane
     plane = Plane()
-    order_row, length_row, mask_row = span_order[0], doc_lengths[0], pad_mask[0]
     ffn_width = w_mlp.shape[1] // 3
     local_rows = w_mlp.shape[0]
     zone = local_rows * n_plane
@@ -510,7 +561,7 @@
     slice_tiles = -(-(ffn_width // LANES) // n_plane)
     chunks = max(c for c in (1, 2, 3) if slice_tiles % c == 0)
     chunk_cols = slice_tiles // chunks * LANES
-    w_cols = qkv_width + LANES
+    kv_cols = 2 * kv_width + LANES
 
     def swap_rows(array):
         return lax.all_to_all(array, PLANE, split_axis=0, concat_axis=0, tiled=True)
@@ -524,8 +575,9 @@
     def whole_rows(pieces):
         cols = pieces[0].shape[1]
         full = jnp.zeros((n_dp, n_plane, local_rows, cols), BF16)
-        for device, piece in zip(plane.devices, pieces):
-            piece = piece.reshape(n_dp, 1, local_rows, cols)
+        slots = [block for piece in pieces for block in jnp.split(piece, n_plane // 2)]
+        for device, block in zip(plane.devices, slots):
+            piece = block.reshape(n_dp, 1, local_rows, cols)
             full = lax.dynamic_update_slice(full, piece, (0, device, 0, 0))
         return full.reshape(n_all * local_rows, cols)
 
@@ -546,9 +598,40 @@
         ],
         axis=1,
     )
-    attn_local = jnp.concatenate([w_qkv, side, w_out.T], axis=1)
-    attn_zone = zone_gather(attn_local)
-
+    my_dp = lax.axis_index("dp")
+
+    def zone_rows(array):
+        full = jnp.zeros((n_dp, *array.shape), BF16)
+        for step in range(n_dp):
+            moved = array
+            if step:
+                moved = lax.ppermute(array, "dp", [(i, (i + step) % n_dp) for i in range(n_dp)])
+            full = lax.dynamic_update_slice(
+                full, moved[None], ((my_dp + n_dp - step) % n_dp, 0, 0)
+            )
+        return full.reshape(n_dp * array.shape[0], array.shape[1])
+
+    kv_local = jnp.concatenate([w_qkv[:, q_width:], side], axis=1)
+    attn_local = jnp.concatenate([kv_local, w_qkv[:, :q_width], w_out.T], axis=1)
+    attn_zone = zone_rows(attn_local)
+    kv_zone = attn_zone[:, : kv_local.shape[1]]
+    big_zone = attn_zone[:, kv_local.shape[1] :]
+
+    packed = pack_slices(after(w_mlp, attn_local), n_plane, chunks, chunk_cols)
+    chunk_width = 3 * chunk_cols
+    mlp_zone = swap_rows(packed)
+    mlp_weights = [
+        zone_gather(mlp_zone[:, chunk * chunk_width : (chunk + 1) * chunk_width])
+        for chunk in range(chunks)
+    ]
+
+    w_kv_stages = plane.gather(kv_zone, 1, mlp_zone)
+    w_q_stages = plane.gather(after(big_zone[:, :q_width], w_kv_stages[1]))
+    w_out_stages = plane.gather(after(big_zone[:, q_width:], w_q_stages[-2]))
+
+    order_row, length_row, mask_row = after(
+        (span_order[0], doc_lengths[0], pad_mask[0]), w_kv_stages[1]
+    )
     row_in_span = jnp.arange(tok_rows, dtype=jnp.int32)
     stored_block = jnp.stack(plane.devices)
     spans = order_row[stored_block]
@@ -576,17 +659,8 @@
     cos_t, sin_t = jnp.cos(angles_t), jnp.sin(angles_t)
     cos_r, sin_r = cos_t.T[:, None, :], sin_t.T[:, None, :]
 
-    packed = pack_slices(after(w_mlp, attn_local, kinfo, qinfo), n_plane, chunks, chunk_cols)
-    chunk_width = 3 * chunk_cols
-    mlp_zone = swap_rows(packed)
-    mlp_weights = [
-        zone_gather(mlp_zone[:, chunk * chunk_width : (chunk + 1) * chunk_width])
-        for chunk in range(chunks)
-    ]
-
-    qkv_held = plane.gather(attn_zone[:, :w_cols])
-    w_qkv_all = whole_rows(qkv_held)
-    side_all = w_qkv_all[:, qkv_width:].astype(F32)
+    w_kv_all = whole_rows(w_kv_stages[-2:])
+    side_all = w_kv_all[:, 2 * kv_width :].astype(F32)
     gain_attn = side_all[:, 0]
     gain_mlp = side_all[:, 1]
     bias_all = side_all.reshape(n_all, local_rows, LANES)[:, 0, 64 : 64 + bias_rows].reshape(-1)
@@ -595,14 +669,16 @@
     in_inverse = inverse_rms(inputs)
     normed_in = (inputs * in_inverse * gain_attn).astype(BF16)
 
-    kv_proj = dot(normed_in, w_qkv_all[:, q_width:qkv_width], 1, 0) + bias_all[q_width:]
+    kv_proj = dot(normed_in, w_kv_all[:, : 2 * kv_width], 1, 0) + bias_all[q_width:]
     key_own = turn(kv_proj[:, :kv_width].reshape(tok_rows, KV_HEADS, HEAD), cos_r, sin_r)
     kv_own = jnp.concatenate([key_own.reshape(tok_rows, kv_width), kv_proj[:, kv_width:]], axis=1)
-    kv_pieces = plane.gather(kv_own.astype(BF16))
-    kv_all = jnp.concatenate(kv_pieces, axis=0)
-    w_out_all = whole_rows(plane.gather(after(attn_zone[:, w_cols:], qkv_held[n_plane // 2 - 1])))
-
-    q_proj = dot(w_qkv_all[:, :q_width], normed_in, 0, 1) + bias_all[:q_width, None]
+    kv_own = after(kv_own.astype(BF16), w_q_stages[1])
+    kv_stages = plane.gather(kv_own, 1, w_out_stages[1])
+    kv_all = jnp.concatenate(kv_stages[-2:], axis=0)
+    w_q_all = whole_rows(w_q_stages[-2:])
+    w_out_all = whole_rows(w_out_stages[-2:])
+
+    q_proj = dot(w_q_all, normed_in, 0, 1) + bias_all[:q_width, None]
     q_heads = q_proj.reshape(HEADS, 2, half, tok_rows)
     q_first, q_second = q_heads[:, 0], q_heads[:, 1]
     query_t = (
@@ -612,18 +688,20 @@
         .reshape(q_width, tok_rows)
         .astype(BF16)
     )
+    need = after(need, w_out_stages[-2])
     attended_t, lse = attention_forward(need, kinfo, qinfo, query_t, kv_all)
 
     middle = inputs + dot(attended_t, w_out_all, 0, 1)
     mid_inverse = inverse_rms(middle)
     normed_mid = (middle * mid_inverse * gain_mlp).astype(BF16)
 
-    mid_held, cot_held = [normed_mid], [after(cotangent, attended_t)]
+    cot_stages = plane.gather(after(cotangent, w_out_stages[-2]))
+    cot_halves = cot_stages[-2:]
+    mid_near = after(normed_mid, cot_stages[1])
     for step in range(plane.steps):
-        mid_held = plane.gather_step(mid_held, step)
-        cot_held = plane.gather_step(cot_held, step)
-    mid_halves = plane.gather_halves(mid_held)
-    cot_halves = plane.gather_halves(cot_held)
+        mid_near = plane.widen(mid_near, step)
+    mid_near = after(mid_near, mlp_weights[0])
+    mid_halves = mid_near, plane.swap(mid_near, plane.steps)
     sums, chunk_grads = (), []
     for chunk, weights in enumerate(mlp_weights):
         last = chunk == chunks - 1
@@ -644,6 +722,8 @@
         if step == plane.steps - 1:
             kept = after(kept, chunk_grads[-1])
         mid_fold = plane.fold(kept, sent, step)
+        if step == 0:
+            out_fold = plane.fold(after(sums[2], kept), sums[3], plane.steps)
     mid_grad = after(mid_fold, *chunk_sums[:-1][:1]).astype(F32)
 
     out_grad = cotangent.astype(F32)
@@ -651,69 +731,86 @@
     middle_grad = out_grad + norm_backward(middle, mid_inverse, mid_grad * gain_mlp)
     middle_low = middle_grad.astype(BF16)
     attended_grad_t = dot(w_out_all, middle_low, 0, 1).astype(BF16)
-    out_weight_grad = dot(middle_low, attended_t, 0, 1).astype(BF16)
-    out_held = plane.reduce_step(device_blocks(out_weight_grad), plane.steps)
-    attended_grad_t = after(attended_grad_t, *out_held)
-    query_grad, kv_grad = attention_backward(
+    attended_grad_t = after(attended_grad_t, out_fold)
+    query_grad, *kv_grads = attention_backward(
         need, kinfo, qinfo, cos_t, sin_t, query_t, kv_all, attended_t, attended_grad_t, lse
     )
-    kv_back = plane.reduce(token_blocks(kv_grad))
+    kv_fold = plane.fold(*kv_grads, plane.steps)
+    mlp_out = after(out_fold, mid_fold)
+    for step in range(plane.steps - 1, 0, -1):
+        mlp_out = plane.fold_rest(mlp_out, step)
+    big_grads = weight_grads(
+        plane,
+        local_rows,
+        [
+            (after(normed_in, mlp_out, kv_fold, *chunk_sums[1:-1]), query_grad, False),
+            (middle_low, attended_t, True),
+        ],
+    )
+    big_fold = plane.fold(*big_grads, plane.steps)
+    mlp_out = plane.fold_rest(after(mlp_out, kv_fold), 0)
     for step in range(plane.steps - 1, -1, -1):
-        out_held = plane.reduce_step(out_held, step)
-    out_plane = out_held[0]
-    kv_back = after(kv_back, out_plane)
+        kv_fold = plane.fold_rest(kv_fold, step)
+    kv_back = after(kv_fold, big_fold, mlp_out)
     kv_back = kv_back.astype(F32)
     key_back = turn(kv_back[:, :kv_width].reshape(tok_rows, KV_HEADS, HEAD), cos_r, -sin_r)
     projected_grad = jnp.concatenate(
         [query_grad, key_back.reshape(tok_rows, kv_width).astype(BF16), kv_back[:, kv_width:].astype(BF16)],
         axis=1,
     )
-    qkv_weight_grad = dot(normed_in, projected_grad, 0, 0).astype(BF16)
-    qkv_held = plane.reduce_step(device_blocks(qkv_weight_grad), plane.steps)
-    in_grad = dot(projected_grad, w_qkv_all[:, :qkv_width], 1, 1)
+    in_grad = dot(projected_grad[:, :q_width], w_q_all, 1, 1) + dot(
+        projected_grad[:, q_width:], w_kv_all[:, : 2 * kv_width], 1, 1
+    )
     gain_attn_grad = jnp.sum(in_grad * (inputs * in_inverse), axis=0)
     input_grad = middle_grad + norm_backward(inputs, in_inverse, in_grad * gain_attn)
     qkv_bias_grad = jnp.sum(projected_grad.astype(F32), axis=0)
 
-    def side_row(array):
+    def side_rows(array):
         array = array.reshape(n_dp, n_plane, 1, -1)
         return jnp.pad(array, ((0, 0), (0, 0), (0, 0), (0, LANES - array.shape[-1])))
 
     side_grad = jnp.concatenate(
-        [side_row(gain_attn_grad), side_row(gain_mlp_grad), side_row(qkv_bias_grad)]
+        [side_rows(gain_attn_grad), side_rows(gain_mlp_grad), side_rows(qkv_bias_grad)]
         + [jnp.zeros((n_dp, n_plane, 1, LANES), F32)] * 5,
         axis=2,
-    ).astype(BF16)
-    side_plane = plane.reduce(
-        [
-            lax.dynamic_slice_in_dim(side_grad, device, 1, 1).reshape(n_dp * 8, LANES)
-            for device in plane.devices
-        ]
-    )
-    side_plane = jnp.pad(
-        side_plane.reshape(n_dp, 8, LANES), ((0, 0), (0, local_rows - 8), (0, 0))
-    ).reshape(n_dp * local_rows, LANES)
+    )
+    side_grad = jnp.pad(side_grad, ((0, 0), (0, 0), (0, local_rows - 8), (0, 0)))
+    side_grad = side_grad.reshape(n_all * local_rows, LANES).astype(BF16)
+    for step in range(plane.steps - 1, 0, -1):
+        big_fold = plane.fold_rest(big_fold, step)
+    small_grads = weight_grads(
+        plane,
+        local_rows,
+        [(after(normed_in, big_fold), projected_grad[:, q_width:], False)],
+        side_grad,
+    )
+    big_fold = plane.fold_rest(big_fold, 0)
+    small_fold = plane.fold(*small_grads, plane.steps)
     for step in range(plane.steps - 1, -1, -1):
-        qkv_held = plane.reduce_step(qkv_held, step)
-    qkv_plane = after(qkv_held[0], *chunk_sums[1:])
-    attn_sum = zone_sum(jnp.concatenate([qkv_plane, side_plane, out_plane], axis=1)).astype(F32)
-    qkv_sum, grad_out = attn_sum[:, :w_cols], attn_sum[:, w_cols:]
-
-    mlp_out = plane.fold(after(sums[2], qkv_plane), sums[3], plane.steps)
-    for step in range(plane.steps - 1, -1, -1):
-        mlp_out = plane.fold_rest(mlp_out, step)
+        rows = small_fold.shape[0] // 2
+        kept, sent = small_fold[:rows], small_fold[rows:]
+        if step == 0:
+            kept = after(kept, chunk_sums[-1])
+        small_fold = plane.fold(kept, sent, step)
+    attn_plane = jnp.concatenate([big_fold, small_fold], axis=1)
+    attn_sum = zone_sum(attn_plane).astype(F32)
+    kv_at, side_at = q_width + width, qkv_width + width
+    grad_qkv = jnp.concatenate([attn_sum[:, :q_width], attn_sum[:, kv_at:side_at]], axis=1)
+    side_sum = attn_sum[:, side_at:]
+
+    all_swapped = swap_rows(after(jnp.concatenate(chunk_sums, axis=1), attn_plane))
     grad_mlp = unpack_slices(
-        [swap_rows(array) for array in chunk_sums], local_rows, ffn_width, n_plane, chunk_cols
+        all_swapped, local_rows, ffn_width, n_plane, chunks, chunk_cols
     )
     block_output = (middle + mlp_out.astype(F32)).astype(BF16)
     return (
         block_output,
         input_grad,
-        qkv_sum[:, :qkv_width],
-        qkv_sum[2, qkv_width : qkv_width + bias_rows],
-        grad_out.T,
-        qkv_sum[0, qkv_width : qkv_width + local_rows],
-        qkv_sum[1, qkv_width : qkv_width + local_rows],
+        grad_qkv,
+        side_sum[2, :bias_rows],
+        attn_sum[:, q_width:kv_at].T,
+        side_sum[0, :local_rows],
+        side_sum[1, :local_rows],
         grad_mlp,
     )
 

time: 605 us -> 583 us (0.964)
  starting transfers between devices: 109 us -> 48.2 us
  Pallas kernels: 137 us -> 164 us
  waiting for transfers between devices: 191 us -> 202 us
  matrix products: 23 us -> 16.4 us
    ppermute x63 -> x33, starting transfers between devices: 89.6 us -> 32.9 us  [swap(): return lax.ppermute(array, PLANE, pairs)]
    ppermute x63 -> x33, waiting for transfers between devices: 114 us -> 143 us  [swap(): return lax.ppermute(array, PLANE, pairs)]
    convert_element_type x15 -> x4, other arithmetic: 17 us -> 2.46 us  [the longest x1 1.03 us: shards(): attn_sum = zone_sum(attn_plane).astype(F32)]
    all_to_all x4 -> x2, waiting for transfers between devices: 67.2 us -> 52.8 us  [swap_rows(): return lax.all_to_all(array, PLANE, split_axis=0, concat_axis=0, tiled=True)]
    dynamic_update_slice x16 -> x23, local copies, waits for them, and re-layouts: 19.1 us -> 6 us  [whole_rows(): full = lax.dynamic_update_slice(full, piece, (0, device, 0, 0))]
    convert_element_type x5 -> x14, other arithmetic: 12.2 us -> 25.2 us  [fold(): return (near.astype(F32) + self.swap(far, step).astype(F32)).astype(BF16)]
    pallas_call x0 -> x2, Pallas kernels: none -> 12.2 us  [weight_grads(): pl.pallas_call(functools.partial(weight_grad_kernel, n_dp, local_rows, [t...]
    pallas_call x1, Pallas kernels: 8.93 us -> 19.9 us  [attention_backward(): pl.pallas_call(attn_bwd_kernel, out_shape=(jax.ShapeDtypeStruct((rows, HE...]
  transfers between devices with their start and end apart: 75 -> 45, of which waited for: 34 -> 22; matrix products, arithmetic and copies ran while one was open for 20% -> 20% of each run, Pallas kernels for 22% -> 27%
where the time goes in v3:
time: 583 us; the launch traced here: 572 us
  waiting for transfers between devices  202 us (35%)
  Pallas kernels  164 us (28%)
  local copies, waits for them, and re-layouts  66.9 us (11%)
  other arithmetic  55.2 us (9%)
  starting transfers between devices  48.2 us (8%)
  between operations  18.2 us (3%)
  matrix products  16.4 us (3%)
    ppermute x33, waiting for transfers between devices, swap(): return lax.ppermute(array, PLANE, pairs)  143 us
    pallas_call x3, Pallas kernels, feed_forward(): pl.pallas_call(functools.partial(ffn_kernel, cols, not sums, with_grad),...  92.7 us
    all_to_all x2, waiting for transfers between devices, swap_rows(): return lax.all_to_all(array, PLANE, split_axis=0, concat_axis=0, tiled=True)  52.8 us
    ppermute x33, starting transfers between devices, swap(): return lax.ppermute(array, PLANE, pairs)  32.9 us
    convert_element_type x14, other arithmetic, fold(): return (near.astype(F32) + self.swap(far, step).astype(F32)).astype(BF16)  25.2 us
    pallas_call x1, Pallas kernels, attention_backward(): pl.pallas_call(attn_bwd_kernel, out_shape=(jax.ShapeDtypeStruct((rows, HE...  19.9 us
    pallas_call x1, Pallas kernels, attention_forward(): pl.pallas_call(attn_fwd_kernel, out_shape=(jax.ShapeDtypeStruct((HEADS *...  17.7 us
    dot_general x6, matrix products, dot(): lax.dot_general(left, right, (((left_dim,), (right_dim,)), ((), ())), pre...  16.4 us
  transfers between devices with their start and end apart: 45, of which 22 were waited for; matrix products, arithmetic and copies ran while one was open for 20% of the time, Pallas kernels for 27%

profile of v3, /device:TPU:0, one launch (start us, length us, event | category | flops | bytes accessed | tf_op | source)
XLA Modules:
  0.0 571.8 jit_solution(15553862822118923452)
XLA Ops:
  12.8 3.5 shard_map.170
  16.3 5.3 all-to-all-start
  21.6 3.7 collective-permute-start.2
  28.8 24.6 %all-to-all-done = bf16[8,48,3456]{2,1,0:T(8,128)(2,1)S(1)} async-done(((bf16[8,48,3456]{2,1,0:T(8,128)(2,1)}), bf16[8,48,3456]{2,1,0:T(8,128)(2,1)S(1)}, u32[]{:S(2)}, u32[]{:S(2)}) %all-to-all-start) | async-done | bytes 2654240 | tf_op jit(solution)/shard_map/all_to_all | solution.py:567
  62.8 2.2 fusion.38
  65.0 2.5 collective-permute-done.3
  89.6 2.2 constant_dynamic-update-slice_fusion
  103.1 6.6 %collective-permute-done.11 = bf16[256,512]{1,0:T(8,128)(2,1)S(1)} collective-permute-done((bf16[256,512]{1,0:T(8,128)(2,1)S(1)}, bf16[256,512]{1,0:T(8,128)(2,1)S(1)}, u32[]{:S(2)}, u32[]{:S(2)}) %collective-permute-start.11) | collective-permute-done | bytes 262176 | tf_op jit(solution)/shard_map/ppermute | solution.py:488
  111.1 2.5 constant_dynamic-update-slice_fusion.2
  115.5 7.9 %collective-permute-done.6 = bf16[192,1536]{1,0:T(8,128)(2,1)S(1)} collective-permute-done((bf16[192,1536]{1,0:T(8,128)(2,1)S(1)}, bf16[192,1536]{1,0:T(8,128)(2,1)S(1)}, u32[]{:S(2)}, u32[]{:S(2)}) %collective-permute-start.6) | collective-permute-done | bytes 589856 | tf_op jit(solution)/shard_map/ppermute | solution.py:488
  126.5 18.9 %collective-permute-done.12 = bf16[512,512]{1,0:T(8,128)(2,1)S(1)} collective-permute-done((bf16[512,512]{1,0:T(8,128)(2,1)S(1)}, bf16[512,512]{1,0:T(8,128)(2,1)S(1)}, u32[]{:S(2)}, u32[]{:S(2)}) %collective-permute-start.12) | collective-permute-done | bytes 524320 | tf_op jit(solution)/shard_map/ppermute | solution.py:488
  150.0 8.6 %collective-permute-done.15 = bf16[256,1536]{1,0:T(8,128)(2,1)S(1)} collective-permute-done((bf16[256,1536]{1,0:T(8,128)(2,1)S(1)}, bf16[256,1536]{1,0:T(8,128)(2,1)S(1)}, u32[]{:S(2)}, u32[]{:S(2)}) %collective-permute-start.15) | collective-permute-done | bytes 786464 | tf_op jit(solution)/shard_map/ppermute | solution.py:488
  165.0 17.7 %shard_map.171 = (bf16[1536,256]{1,0:T(8,128)(2,1)}, f32[16,256]{1,0:T(8,128)}) custom-call(s32[8]{0:T(128)} %and_convert_fusion.need_ref, s32[2048,2]{1,0:T(8,128)} %copy.31.kinfo_ref, s32[8,256]{1,0:T(8,128)} %add_add_fusion.qinfo_ref, bf16[1536,256]{1,0:T(8,128)(2,1)} %bitcast.119, bf16[2048,512]{1,0:T(8,128)(2,1)} %copy-done.8), custom_call_target="tpu_custom_call" | custom-call | flops 1024 | bytes 1024 | tf_op jit(solution)/shard_map/pallas_call | solution.py:175
  187.7 4.1 collective-permute-start.19
  191.8 16.3 %collective-permute-done.16 = bf16[256,1536]{1,0:T(8,128)(2,1)S(1)} collective-permute-done((bf16[256,1536]{1,0:T(8,128)(2,1)S(1)}, bf16[256,1536]{1,0:T(8,128)(2,1)S(1)}, u32[]{:S(2)}, u32[]{:S(2)}) %collective-permute-start.16) | collective-permute-done | bytes 786464 | tf_op jit(solution)/shard_map/ppermute | solution.py:488
  208.2 4.1 collective-permute-start.17
  213.7 17.1 %collective-permute-done.17 = bf16[512,1536]{1,0:T(8,128)(2,1)S(1)} collective-permute-done((bf16[512,1536]{1,0:T(8,128)(2,1)S(1)}, bf16[512,1536]{1,0:T(8,128)(2,1)S(1)}, u32[]{:S(2)}, u32[]{:S(2)}) %collective-permute-start.17) | collective-permute-done | bytes 1572896 | tf_op jit(solution)/shard_map/ppermute | solution.py:488
  232.4 5.6 collective-permute-done.18.refs_1_.mid_far
  239.7 33.3 %shard_map.172 = (bf16[1024,1536]{1,0:T(8,128)(2,1)}, bf16[1024,1536]{1,0:T(8,128)(2,1)}, bf16[1024,1536]{1,0:T(8,128)(2,1)}, bf16[1024,1536]{1,0:T(8,128)(2,1)}, bf16[1536,1152]{1,0:T(8,128)(2,1)}) custom-call(bf16[1024,1536]{1,0:T(8,128)(2,1)} %copy-done.2, bf16[1024,1536]{1,0:T(8,128)(2,1)} %copy-done.3, ...), custom_call_target="tpu_custom_call" | custom-call | flops 1024 | bytes 1024 | tf_op jit(solution)/shard_map/pallas_call | solution.py:286
  273.1 34.5 %shard_map.173 = (bf16[1024,1536]{1,0:T(8,128)(2,1)}, bf16[1024,1536]{1,0:T(8,128)(2,1)}, bf16[1024,1536]{1,0:T(8,128)(2,1)}, bf16[1024,1536]{1,0:T(8,128)(2,1)}, bf16[1536,1152]{1,0:T(8,128)(2,1)}) custom-call(bf16[1024,1536]{1,0:T(8,128)(2,1)} %copy-done.2, bf16[1024,1536]{1,0:T(8,128)(2,1)} %copy-done.3, ...), custom_call_target="tpu_custom_call" | custom-call | flops 1024 | bytes 1024 | tf_op jit(solution)/shard_map/pallas_call | solution.py:286
  307.6 24.9 %shard_map.174 = (bf16[1024,1536]{1,0:T(8,128)(2,1)}, bf16[1024,1536]{1,0:T(8,128)(2,1)}, bf16[1024,1536]{1,0:T(8,128)(2,1)}, bf16[1024,1536]{1,0:T(8,128)(2,1)}, bf16[2048,1152]{1,0:T(8,128)(2,1)}) custom-call(bf16[1024,1536]{1,0:T(8,128)(2,1)} %copy-done.2, bf16[1024,1536]{1,0:T(8,128)(2,1)} %copy-done.3, ...), custom_call_target="tpu_custom_call" | custom-call | flops 1024 | bytes 1024 | tf_op jit(solution)/shard_map/pallas_call | solution.py:286
  333.2 5.4 collective-permute-done.21
  338.6 2.9 add_convert_fusion.2
  341.8 2.1 collective-permute-start.22
  343.9 14.1 %shard_map.175 = bf16[1536,1152]{1,0:T(8,128)(2,1)} custom-call(bf16[1024,1536]{1,0:T(8,128)(2,1)} %copy-done.2, bf16[1024,1536]{1,0:T(8,128)(2,1)} %copy-done.3, bf16[1024,1536]{1,0:T(8,128)(2,1)} %constant_dynamic-update-slice_fusion.15.refs_2_.cot_near, bf16[1024,1536]{1,0:T(8,128)(2,1)} %collective-permute-done.20.refs_3_.cot_far, ...), custom_call_target="tpu_custom_call" | custom-call | flops 1024 | bytes 1024 | tf_op jit(solution)/shard_map/pallas_call | solution.py:314
  357.9 4.4 collective-permute-done.22
  364.7 2.9 add_convert_fusion.1
  367.6 8.8 %collective-permute-done.24 = bf16[256,1536]{1,0:T(8,128)(2,1)S(1)} collective-permute-done((bf16[256,1536]{1,0:T(8,128)(2,1)S(1)}, bf16[256,1536]{1,0:T(8,128)(2,1)S(1)}, u32[]{:S(2)}, u32[]{:S(2)}) %collective-permute-start.24) | collective-permute-done | bytes 786464 | tf_op jit(solution)/shard_map/ppermute | solution.py:488
  380.9 4.9 convolution_convert_fusion.do_ref
  385.9 19.9 %shard_map.176 = (bf16[256,1536]{1,0:T(8,128)(2,1)}, bf16[1024,512]{1,0:T(8,128)(2,1)}, bf16[1024,512]{1,0:T(8,128)(2,1)}) custom-call(s32[8]{0:T(128)} %and_convert_fusion.need_ref, s32[2048,2]{1,0:T(8,128)} %copy.31.kinfo_ref, s32[8,256]{1,0:T(8,128)} %add_add_fusion.qinfo_ref, f32[64,256]{1,0:T(8,128)} %get-tuple-element.170.cos_ref, ...), custom_call_target="tpu_custom_call" | custom-call | flops 1024 | bytes 1024 | tf_op jit(solution)/shard_map/pallas_call | solution.py:196
  406.5 3.5 add_convert_fusion.4
  412.5 3.4 reduce-scatter.7.cloned.1.call-done
  416.0 8.9 %shard_map.177 = (bf16[768,3072]{1,0:T(8,128)(2,1)}, bf16[768,3072]{1,0:T(8,128)(2,1)}) custom-call(s32[8]{0:T(128)} %stack.91.dev_ref, bf16[256,1536]{1,0:T(8,128)(2,1)} %copy-done.15, bf16[256,1536]{1,0:T(8,128)(2,1)} %get-tuple-element.95.refs_1_, bf16[256,1536]{1,0:T(8,128)(2,1)} %copy-done.25, bf16[1536,256]{1,0:T(8,128)(2,1)} %get-tuple-element.67.o_ref.refs_3_), custom_call_target="tpu_custom_call" | custom-call | flops 1024 | bytes 1024 | tf_op jit(solution)/shard_map/pallas_call | solution.py:443
  426.6 7.6 %collective-permute-done.28 = bf16[512,512]{1,0:T(8,128)(2,1)S(1)} collective-permute-done((bf16[512,512]{1,0:T(8,128)(2,1)S(1)}, bf16[512,512]{1,0:T(8,128)(2,1)S(1)}, u32[]{:S(2)}, u32[]{:S(2)}) %collective-permute-start.28) | collective-permute-done | bytes 524320 | tf_op jit(solution)/shard_map/ppermute | solution.py:488
  441.7 5.7 %add_convert_fusion = bf16[768,3072]{1,0:T(8,128)(2,1)S(1)} fusion(bf16[768,3072]{1,0:T(8,128)(2,1)} %collective-permute-done.30, bf16[768,3072]{1,0:T(8,128)(2,1)} %get-tuple-element.98), kind=kLoop, calls=%fused_computation.2 | loop fusion | flops 9437184 | bytes 14155776 | tf_op jit(solution)/shard_map/convert_element_type | solution.py:502
  454.3 2.1 fusion.14
  456.4 5.0 fusion.5
  464.6 14.9 %collective-permute-done.31 = bf16[384,3072]{1,0:T(8,128)(2,1)} collective-permute-done((bf16[384,3072]{1,0:T(8,128)(2,1)}, bf16[384,3072]{1,0:T(8,128)(2,1)}, u32[]{:S(2)}, u32[]{:S(2)}) %collective-permute-start.31) | collective-permute-done | bytes 2359328 | tf_op jit(solution)/shard_map/ppermute | solution.py:488
  479.5 3.3 add_convert_fusion.3
  482.8 3.3 shard_map.178
  490.8 12.6 %collective-permute-done.34 = bf16[384,640]{1,0:T(8,128)(2,1)S(1)} collective-permute-done((bf16[384,640]{1,0:T(8,128)(2,1)S(1)}, bf16[384,640]{1,0:T(8,128)(2,1)S(1)}, u32[]{:S(2)}, u32[]{:S(2)}) %collective-permute-start.34) | collective-permute-done | bytes 491552 | tf_op jit(solution)/shard_map/ppermute | solution.py:488
  509.1 2.7 reduce-scatter.9.cloned.1.call-done
  512.8 2.5 pad_maximum_fusion.3
  515.4 3.4 pad_maximum_fusion.1
  518.8 4.5 all-to-all-start.1
  523.3 3.5 fusion.13
  526.8 28.2 %all-to-all-done.1 = bf16[8,48,3456]{2,1,0:T(8,128)(2,1)} async-done(((bf16[8,48,3456]{2,1,0:T(8,128)(2,1)}), bf16[8,48,3456]{2,1,0:T(8,128)(2,1)}, u32[]{:S(2)}, u32[]{:S(2)}) %all-to-all-start.1) | async-done | bytes 2654240 | tf_op jit(solution)/shard_map/all_to_all | solution.py:567
  555.0 4.4 shard_map.179
  (338 shorter events, 122.5 us)
Async XLA Ops:
  7.2 61.9 %copy-start = (s32[1,8]{1,0:T(1,128)S(1)}, s32[1,8]{1,0:T(1,128)}, u32[]{:S(2)}) copy-start(s32[1,8]{1,0:T(1,128)} %param.12) | copy-start | bytes 100
  16.3 37.1 %all-to-all-start = ((bf16[8,48,3456]{2,1,0:T(8,128)(2,1)}), bf16[8,48,3456]{2,1,0:T(8,128)(2,1)S(1)}, u32[]{:S(2)}, u32[]{:S(2)}) async-start(bf16[8,48,3456]{2,1,0:T(8,128)(2,1)} %bitcast.111), calls=%async_computation | async-start | bytes 5308416 | tf_op jit(solution)/shard_map/all_to_all | solution.py:567
  21.6 210.7 %all-gather.4.cloned.1.call-start = ((), (), s32[]{:S(2)}) async-start(), calls=%async_computation.6 | async-start | bytes 4423680 | tf_op jit(solution)/shard_map/all_gather | solution.py:570
  21.6 36.9 %collective-permute-start.2 = (bf16[48,3712]{1,0:T(8,128)(2,1)}, bf16[48,3712]{1,0:T(8,128)(2,1)}, u32[]{:S(2)}, u32[]{:S(2)}) collective-permute-start(bf16[48,3712]{1,0:T(8,128)(2,1)} %concatenate.103), channel_id=1, source_target_pairs={{0,24},{8,0},{16,8},{24,16},{1,25},{9,1},{17,9},{25,17},{2,26},{10... | collective-permute-start | bytes 1069064 | tf_op jit(solution)/shard_map/ppermute | solution.py:608
  25.3 31.5 %collective-permute-start.1 = (bf16[48,3712]{1,0:T(8,128)(2,1)}, bf16[48,3712]{1,0:T(8,128)(2,1)}, u32[]{:S(2)}, u32[]{:S(2)}) collective-permute-start(bf16[48,3712]{1,0:T(8,128)(2,1)} %concatenate.103), channel_id=1, source_target_pairs={{0,16},{8,24},{16,0},{24,8},{1,17},{9,25},{17,1},{25,9},{2,18},{10... | collective-permute-start | bytes 1069064 | tf_op jit(solution)/shard_map/ppermute | solution.py:608
  25.3 29.7 %collective-permute-start = (bf16[48,3712]{1,0:T(8,128)(2,1)}, bf16[48,3712]{1,0:T(8,128)(2,1)}, u32[]{:S(2)}, u32[]{:S(2)}) collective-permute-start(bf16[48,3712]{1,0:T(8,128)(2,1)} %concatenate.103), channel_id=1, source_target_pairs={{0,8},{8,16},{16,24},{24,0},{1,9},{9,17},{17,25},{25,1},{2,10},{10... | collective-permute-start | bytes 1069064 | tf_op jit(solution)/shard_map/ppermute | solution.py:608
  26.8 28.2 %copy-start.42 = (f32[256]{0:T(256)}, f32[256]{0:T(256)S(1)}, u32[]{:S(2)}) copy-start(f32[256]{0:T(256)S(1)} %fusion.10) | copy-start | bytes 3076
  26.8 69.2 %copy-start.44 = (f32[256]{0:T(256)}, f32[256]{0:T(256)S(1)}, u32[]{:S(2)}) copy-start(f32[256]{0:T(256)S(1)} %add_rsqrt_fusion.1) | copy-start | bytes 3076
  55.0 218.1 %all-gather.8.cloned.1.call-start = ((), (), s32[]{:S(2)}) async-start(), calls=%async_computation.8 | async-start | bytes 4423680 | tf_op jit(solution)/shard_map/all_gather | solution.py:570
  61.3 6.3 %collective-permute-start.3 = (bf16[192,640]{1,0:T(8,128)(2,1)S(1)}, bf16[192,640]{1,0:T(8,128)(2,1)S(1)}, u32[]{:S(2)}, u32[]{:S(2)}) collective-permute-start(bf16[192,640]{1,0:T(8,128)(2,1)S(1)} %slice.248), channel_id=1, source_target_pairs={{0,4},{1,5},{2,3},{3,2},{4,0},{5,1},{6,7},{7,6},{8,12},{9,13},{10,... | collective-permute-start | bytes 737288 | tf_op jit(solution)/shard_map/ppermute | solution.py:488
  67.6 16.0 %collective-permute-start.9 = (bf16[384,640]{1,0:T(8,128)(2,1)S(1)}, bf16[384,640]{1,0:T(8,128)(2,1)S(1)}, u32[]{:S(2)}, u32[]{:S(2)}) collective-permute-start(bf16[384,640]{1,0:T(8,128)(2,1)S(1)} %pad_maximum_fusion.8), channel_id=1, source_target_pairs={{0,1},{1,0},{2,6},{3,7},{4,5},{5,4},{6,2},{7,3},{8,9},{9,8},{10,14... | collective-permute-start | bytes 1474568 | tf_op jit(solution)/shard_map/ppermute | solution.py:488
  74.9 14.6 %collective-permute-start.4 = (bf16[192,1536]{1,0:T(8,128)(2,1)S(1)}, bf16[192,1536]{1,0:T(8,128)(2,1)}, u32[]{:S(2)}, u32[]{:S(2)}) collective-permute-start(bf16[192,1536]{1,0:T(8,128)(2,1)S(1)} %get-tuple-element.61), channel_id=1, source_target_pairs={{0,4},{1,5},{2,3},{3,2},{4,0},{5,1},{6,7},{7,6},{8,12},{9,13},{10,... | collective-permute-start | bytes 1769480 | tf_op jit(solution)/shard_map/ppermute | solution.py:488
  79.3 228.3 %all-gather.6.cloned.1.call-start = ((), (), s32[]{:S(2)}) async-start(), calls=%async_computation.7 | async-start | bytes 4423680 | tf_op jit(solution)/shard_map/all_gather | solution.py:570
  84.7 7.6 %collective-permute-start.10 = (bf16[768,640]{1,0:T(8,128)(2,1)}, bf16[768,640]{1,0:T(8,128)(2,1)}, u32[]{:S(2)}, u32[]{:S(2)}) collective-permute-start(bf16[768,640]{1,0:T(8,128)(2,1)} %pad_maximum_fusion.5), channel_id=1, source_target_pairs={{0,2},{1,3},{2,0},{3,1},{4,6},{5,7},{6,4},{7,5},{8,10},{9,11},{10,... | collective-permute-start | bytes 2949128 | tf_op jit(solution)/shard_map/ppermute | solution.py:488
  91.7 19.3 %collective-permute-start.5 = (bf16[384,1536]{1,0:T(8,128)(2,1)}, bf16[384,1536]{1,0:T(8,128)(2,1)}, u32[]{:S(2)}, u32[]{:S(2)}) collective-permute-start(bf16[384,1536]{1,0:T(8,128)(2,1)} %get-tuple-element.151), channel_id=1, source_target_pairs={{0,1},{1,0},{2,6},{3,7},{4,5},{5,4},{6,2},{7,3},{8,9},{9,8},{10,14... | collective-permute-start | bytes 3538952 | tf_op jit(solution)/shard_map/ppermute | solution.py:488
  100.4 9.3 %collective-permute-start.11 = (bf16[256,512]{1,0:T(8,128)(2,1)S(1)}, bf16[256,512]{1,0:T(8,128)(2,1)S(1)}, u32[]{:S(2)}, u32[]{:S(2)}) collective-permute-start(bf16[256,512]{1,0:T(8,128)(2,1)S(1)} %pad_maximum_fusion.10), channel_id=1, source_target_pairs={{0,4},{1,5},{2,3},{3,2},{4,0},{5,1},{6,7},{7,6},{8,12},{9,13},{10,... | collective-permute-start | bytes 786440 | tf_op jit(solution)/shard_map/ppermute | solution.py:488
  113.6 35.2 %collective-permute-start.8 = (bf16[768,1536]{1,0:T(8,128)(2,1)}, bf16[768,1536]{1,0:T(8,128)(2,1)S(1)}, u32[]{:S(2)}, u32[]{:S(2)}) collective-permute-start(bf16[768,1536]{1,0:T(8,128)(2,1)} %constant_dynamic-update-slice_fusion.2), channel_id=1, source_target_pairs={{0,2},{1,3},{2,0},{3,1},{4,6},{5,7},{6,4},{7,5},{8,10},{9,11},{10,... | collective-permute-start | bytes 7077896 | tf_op jit(solution)/shard_map/ppermute | solution.py:488
  113.6 9.9 %collective-permute-start.6 = (bf16[192,1536]{1,0:T(8,128)(2,1)S(1)}, bf16[192,1536]{1,0:T(8,128)(2,1)S(1)}, u32[]{:S(2)}, u32[]{:S(2)}) collective-permute-start(bf16[192,1536]{1,0:T(8,128)(2,1)S(1)} %copy-done.18), channel_id=1, source_target_pairs={{0,4},{1,5},{2,3},{3,2},{4,0},{5,1},{6,7},{7,6},{8,12},{9,13},{10,... | collective-permute-start | bytes 1769480 | tf_op jit(solution)/shard_map/ppermute | solution.py:488
  123.6 22.1 %collective-permute-start.7 = (bf16[384,1536]{1,0:T(8,128)(2,1)S(1)}, bf16[384,1536]{1,0:T(8,128)(2,1)S(1)}, u32[]{:S(2)}, u32[]{:S(2)}) collective-permute-start(bf16[384,1536]{1,0:T(8,128)(2,1)S(1)} %get-tuple-element.147), channel_id=1, source_target_pairs={{0,1},{1,0},{2,6},{3,7},{4,5},{5,4},{6,2},{7,3},{8,9},{9,8},{10,14... | collective-permute-start | bytes 3538952 | tf_op jit(solution)/shard_map/ppermute | solution.py:488
  124.8 20.6 %collective-permute-start.12 = (bf16[512,512]{1,0:T(8,128)(2,1)S(1)}, bf16[512,512]{1,0:T(8,128)(2,1)S(1)}, u32[]{:S(2)}, u32[]{:S(2)}) collective-permute-start(bf16[512,512]{1,0:T(8,128)(2,1)S(1)} %pad_maximum_fusion.7), channel_id=1, source_target_pairs={{0,1},{1,0},{2,6},{3,7},{4,5},{5,4},{6,2},{7,3},{8,9},{9,8},{10,14... | collective-permute-start | bytes 1572872 | tf_op jit(solution)/shard_map/ppermute | solution.py:488
  145.5 3.1 collective-permute-start.13
  145.7 14.2 %collective-permute-start.14 = (bf16[768,1536]{1,0:T(8,128)(2,1)S(1)}, bf16[768,1536]{1,0:T(8,128)(2,1)S(1)}, u32[]{:S(2)}, u32[]{:S(2)}) collective-permute-start(bf16[768,1536]{1,0:T(8,128)(2,1)S(1)} %constant_dynamic-update-slice_fusion.7), channel_id=1, source_target_pairs={{0,2},{1,3},{2,0},{3,1},{4,6},{5,7},{6,4},{7,5},{8,10},{9,11},{10,... | collective-permute-start | bytes 7077896 | tf_op jit(solution)/shard_map/ppermute | solution.py:488
  146.7 12.0 %collective-permute-start.15 = (bf16[256,1536]{1,0:T(8,128)(2,1)S(1)}, bf16[256,1536]{1,0:T(8,128)(2,1)S(1)}, u32[]{:S(2)}, u32[]{:S(2)}) collective-permute-start(bf16[256,1536]{1,0:T(8,128)(2,1)S(1)} %copy-done.12), channel_id=1, source_target_pairs={{0,4},{1,5},{2,3},{3,2},{4,0},{5,1},{6,7},{7,6},{8,12},{9,13},{10,... | collective-permute-start | bytes 2359304 | tf_op jit(solution)/shard_map/ppermute | solution.py:488
  187.6 20.5 %collective-permute-start.16 = (bf16[256,1536]{1,0:T(8,128)(2,1)S(1)}, bf16[256,1536]{1,0:T(8,128)(2,1)S(1)}, u32[]{:S(2)}, u32[]{:S(2)}) collective-permute-start(bf16[256,1536]{1,0:T(8,128)(2,1)S(1)} %multiply_convert_fusion), channel_id=1, source_target_pairs={{0,4},{1,5},{2,3},{3,2},{4,0},{5,1},{6,7},{7,6},{8,12},{9,13},{10,... | collective-permute-start | bytes 2359304 | tf_op jit(solution)/shard_map/ppermute | solution.py:488
  187.7 24.7 %collective-permute-start.19 = (bf16[512,1536]{1,0:T(8,128)(2,1)}, bf16[512,1536]{1,0:T(8,128)(2,1)S(1)}, u32[]{:S(2)}, u32[]{:S(2)}) collective-permute-start(bf16[512,1536]{1,0:T(8,128)(2,1)} %get-tuple-element.142), channel_id=1, source_target_pairs={{0,1},{1,0},{2,6},{3,7},{4,5},{5,4},{6,2},{7,3},{8,9},{9,8},{10,14... | collective-permute-start | bytes 4718600 | tf_op jit(solution)/shard_map/ppermute | solution.py:488
  191.8 188.1 %reduce-scatter.5.cloned.1.call-start = ((), (), s32[]{:S(2)}) async-start(), calls=%async_computation.9 | async-start | bytes 4423680 | tf_op jit(solution)/shard_map/reduce_scatter | solution.py:573
  208.2 22.5 %collective-permute-start.17 = (bf16[512,1536]{1,0:T(8,128)(2,1)S(1)}, bf16[512,1536]{1,0:T(8,128)(2,1)S(1)}, u32[]{:S(2)}, u32[]{:S(2)}) collective-permute-start(bf16[512,1536]{1,0:T(8,128)(2,1)S(1)} %pad_maximum_fusion.2), channel_id=1, source_target_pairs={{0,1},{1,0},{2,6},{3,7},{4,5},{5,4},{6,2},{7,3},{8,9},{9,8},{10,14... | collective-permute-start | bytes 4718600 | tf_op jit(solution)/shard_map/ppermute | solution.py:488
  213.6 18.8 %collective-permute-start.20 = (bf16[1024,1536]{1,0:T(8,128)(2,1)}, bf16[1024,1536]{1,0:T(8,128)(2,1)}, u32[]{:S(2)}, u32[]{:S(2)}) collective-permute-start(bf16[1024,1536]{1,0:T(8,128)(2,1)} %constant_dynamic-update-slice_fusion.15.refs_2_.cot_near), channel_id=1, source_target_pairs={{0,2},{1,3},{2,0},{3,1},{4,6},{5,7},{6,4},{7,5},{8,10},{9,11},{10,... | collective-permute-start | bytes 9437192 | tf_op jit(solution)/shard_map/ppermute | solution.py:488
  232.3 5.7 %collective-permute-start.18 = (bf16[1024,1536]{1,0:T(8,128)(2,1)S(1)}, bf16[1024,1536]{1,0:T(8,128)(2,1)S(1)}, u32[]{:S(2)}, u32[]{:S(2)}) collective-permute-start(bf16[1024,1536]{1,0:T(8,128)(2,1)S(1)} %pad_maximum_fusion.refs_0_.mid_near), channel_id=1, source_target_pairs={{0,2},{1,3},{2,0},{3,1},{4,6},{5,7},{6,4},{7,5},{8,10},{9,11},{10,... | collective-permute-start | bytes 9437192 | tf_op jit(solution)/shard_map/ppermute | solution.py:488
  273.0 142.9 %reduce-scatter.7.cloned.1.call-start = ((), (), s32[]{:S(2)}) async-start(), calls=%async_computation.10 | async-start | bytes 4423680 | tf_op jit(solution)/shard_map/reduce_scatter | solution.py:573
  332.5 6.1 %collective-permute-start.21 = (bf16[1024,1536]{1,0:T(8,128)(2,1)}, bf16[1024,1536]{1,0:T(8,128)(2,1)}, u32[]{:S(2)}, u32[]{:S(2)}) collective-permute-start(bf16[1024,1536]{1,0:T(8,128)(2,1)} %get-tuple-element.81), channel_id=1, source_target_pairs={{0,2},{1,3},{2,0},{3,1},{4,6},{5,7},{6,4},{7,5},{8,10},{9,11},{10,... | collective-permute-start | bytes 9437192 | tf_op jit(solution)/shard_map/ppermute | solution.py:488
  332.7 31.9 %collective-permute-start.23 = (bf16[1024,1536]{1,0:T(8,128)(2,1)}, bf16[1024,1536]{1,0:T(8,128)(2,1)}, u32[]{:S(2)}, u32[]{:S(2)}) collective-permute-start(bf16[1024,1536]{1,0:T(8,128)(2,1)} %get-tuple-element.86), channel_id=1, source_target_pairs={{0,2},{1,3},{2,0},{3,1},{4,6},{5,7},{6,4},{7,5},{8,10},{9,11},{10,... | collective-permute-start | bytes 9437192 | tf_op jit(solution)/shard_map/ppermute | solution.py:488
  333.1 178.7 %reduce-scatter.9.cloned.1.call-start = ((), (), s32[]{:S(2)}) async-start(), calls=%async_computation.11 | async-start | bytes 4423680 | tf_op jit(solution)/shard_map/reduce_scatter | solution.py:573
  341.8 20.6 %collective-permute-start.22 = (bf16[512,1536]{1,0:T(8,128)(2,1)S(1)}, bf16[512,1536]{1,0:T(8,128)(2,1)}, u32[]{:S(2)}, u32[]{:S(2)}) collective-permute-start(bf16[512,1536]{1,0:T(8,128)(2,1)S(1)} %get-tuple-element.117), channel_id=1, source_target_pairs={{0,1},{1,0},{2,6},{3,7},{4,5},{5,4},{6,2},{7,3},{8,9},{9,8},{10,14... | collective-permute-start | bytes 4718600 | tf_op jit(solution)/shard_map/ppermute | solution.py:488
  364.3 12.1 %collective-permute-start.24 = (bf16[256,1536]{1,0:T(8,128)(2,1)S(1)}, bf16[256,1536]{1,0:T(8,128)(2,1)S(1)}, u32[]{:S(2)}, u32[]{:S(2)}) collective-permute-start(bf16[256,1536]{1,0:T(8,128)(2,1)S(1)} %slice.270), channel_id=1, source_target_pairs={{0,4},{1,5},{2,3},{3,2},{4,0},{5,1},{6,7},{7,6},{8,12},{9,13},{10,... | collective-permute-start | bytes 2359304 | tf_op jit(solution)/shard_map/ppermute | solution.py:488
  377.9 28.6 %collective-permute-start.25 = (bf16[512,1536]{1,0:T(8,128)(2,1)}, bf16[512,1536]{1,0:T(8,128)(2,1)}, u32[]{:S(2)}, u32[]{:S(2)}) collective-permute-start(bf16[512,1536]{1,0:T(8,128)(2,1)} %slice.219), channel_id=1, source_target_pairs={{0,1},{1,0},{2,6},{3,7},{4,5},{5,4},{6,2},{7,3},{8,9},{9,8},{10,14... | collective-permute-start | bytes 4718600 | tf_op jit(solution)/shard_map/ppermute | solution.py:488
  405.8 4.2 collective-permute-start.26
  424.9 16.8 %collective-permute-start.30 = (bf16[768,3072]{1,0:T(8,128)(2,1)}, bf16[768,3072]{1,0:T(8,128)(2,1)}, u32[]{:S(2)}, u32[]{:S(2)}) collective-permute-start(bf16[768,3072]{1,0:T(8,128)(2,1)} %get-tuple-element.99), channel_id=1, source_target_pairs={{0,2},{1,3},{2,0},{3,1},{4,6},{5,7},{6,4},{7,5},{8,10},{9,11},{10,... | collective-permute-start | bytes 14155784 | tf_op jit(solution)/shard_map/ppermute | solution.py:488
  424.9 9.2 %collective-permute-start.28 = (bf16[512,512]{1,0:T(8,128)(2,1)S(1)}, bf16[512,512]{1,0:T(8,128)(2,1)S(1)}, u32[]{:S(2)}, u32[]{:S(2)}) collective-permute-start(bf16[512,512]{1,0:T(8,128)(2,1)S(1)} %slice.272), channel_id=1, source_target_pairs={{0,1},{1,0},{2,6},{3,7},{4,5},{5,4},{6,2},{7,3},{8,9},{9,8},{10,14... | collective-permute-start | bytes 1572872 | tf_op jit(solution)/shard_map/ppermute | solution.py:488
  435.2 6.4 %collective-permute-start.29 = (bf16[256,512]{1,0:T(8,128)(2,1)S(1)}, bf16[256,512]{1,0:T(8,128)(2,1)S(1)}, u32[]{:S(2)}, u32[]{:S(2)}) collective-permute-start(bf16[256,512]{1,0:T(8,128)(2,1)S(1)} %slice.274), channel_id=1, source_target_pairs={{0,4},{1,5},{2,3},{3,2},{4,0},{5,1},{6,7},{7,6},{8,12},{9,13},{10,... | collective-permute-start | bytes 786440 | tf_op jit(solution)/shard_map/ppermute | solution.py:488
  437.3 122.2 %reduce-scatter.11.cloned.1.call-start = ((), (), s32[]{:S(2)}) async-start(), calls=%async_computation.12 | async-start | bytes 1781760 | tf_op jit(solution)/shard_map/reduce_scatter | solution.py:573
  439.4 12.5 %collective-permute-start.27 = (bf16[256,1536]{1,0:T(8,128)(2,1)S(1)}, bf16[256,1536]{1,0:T(8,128)(2,1)S(1)}, u32[]{:S(2)}, u32[]{:S(2)}) collective-permute-start(bf16[256,1536]{1,0:T(8,128)(2,1)S(1)} %slice.221), channel_id=1, source_target_pairs={{0,4},{1,5},{2,3},{3,2},{4,0},{5,1},{6,7},{7,6},{8,12},{9,13},{10,... | collective-permute-start | bytes 2359304 | tf_op jit(solution)/shard_map/ppermute | solution.py:488
  450.3 29.2 %collective-permute-start.31 = (bf16[384,3072]{1,0:T(8,128)(2,1)}, bf16[384,3072]{1,0:T(8,128)(2,1)}, u32[]{:S(2)}, u32[]{:S(2)}) collective-permute-start(bf16[384,3072]{1,0:T(8,128)(2,1)} %slice.278), channel_id=1, source_target_pairs={{0,1},{1,0},{2,6},{3,7},{4,5},{5,4},{6,2},{7,3},{8,9},{9,8},{10,14... | collective-permute-start | bytes 7077896 | tf_op jit(solution)/shard_map/ppermute | solution.py:488
  486.1 2.8 collective-permute-start.33
  486.2 21.5 %collective-permute-start.32 = (bf16[192,3072]{1,0:T(8,128)(2,1)S(1)}, bf16[192,3072]{1,0:T(8,128)(2,1)S(1)}, u32[]{:S(2)}, u32[]{:S(2)}) collective-permute-start(bf16[192,3072]{1,0:T(8,128)(2,1)S(1)} %slice.280), channel_id=1, source_target_pairs={{0,4},{1,5},{2,3},{3,2},{4,0},{5,1},{6,7},{7,6},{8,12},{9,13},{10,... | collective-permute-start | bytes 3538952 | tf_op jit(solution)/shard_map/ppermute | solution.py:488
  489.2 14.2 %collective-permute-start.34 = (bf16[384,640]{1,0:T(8,128)(2,1)S(1)}, bf16[384,640]{1,0:T(8,128)(2,1)S(1)}, u32[]{:S(2)}, u32[]{:S(2)}) collective-permute-start(bf16[384,640]{1,0:T(8,128)(2,1)S(1)} %slice.282), channel_id=1, source_target_pairs={{0,1},{1,0},{2,6},{3,7},{4,5},{5,4},{6,2},{7,3},{8,9},{9,8},{10,14... | collective-permute-start | bytes 1474568 | tf_op jit(solution)/shard_map/ppermute | solution.py:488
  504.3 7.6 %collective-permute-start.35 = (bf16[192,640]{1,0:T(8,128)(2,1)}, bf16[192,640]{1,0:T(8,128)(2,1)}, u32[]{:S(2)}, u32[]{:S(2)}) collective-permute-start(bf16[192,640]{1,0:T(8,128)(2,1)} %get-tuple-element.160), channel_id=1, source_target_pairs={{0,4},{1,5},{2,3},{3,2},{4,0},{5,1},{6,7},{7,6},{8,12},{9,13},{10,... | collective-permute-start | bytes 737288 | tf_op jit(solution)/shard_map/ppermute | solution.py:488
  518.8 36.3 %all-to-all-start.1 = ((bf16[8,48,3456]{2,1,0:T(8,128)(2,1)}), bf16[8,48,3456]{2,1,0:T(8,128)(2,1)}, u32[]{:S(2)}, u32[]{:S(2)}) async-start(bf16[8,48,3456]{2,1,0:T(8,128)(2,1)} %bitcast.113), calls=%async_computation.5 | async-start | bytes 5308416 | tf_op jit(solution)/shard_map/all_to_all | solution.py:567
  (50 other events, 233.0 us)
Sparse Core Ops, SparseCore 0:
  55.1 70.2 all-gather.3
  127.0 68.6 all-gather.7
  197.2 68.5 all-gather.5
  273.1 73.9 reduce-scatter.4
  349.3 66.6 reduce-scatter.6
  437.4 74.3 reduce-scatter.8
  515.5 41.6 reduce-scatter.10
